TPU v7x, 512 devices: a whole 4x4x16 slice. The times are simulated.
512 devices in a mesh: wide: 128 (over y, z, x_hi), narrow: 4 (over x_lo, core).
Axes of the slice: x: 4 (x_hi: 2, x_lo: 2; x = x_hi * 2 + x_lo), y: 4, z: 16, core: 2. Of those that a mesh axis runs over, the one named last changes fastest.
Arguments:
- queries: bfloat16 [131072, 768], P(('wide', 'narrow')), may hold values from -8 to 8
- key_rows: bfloat16 [131072, 768], P(('wide', 'narrow')), may hold values from -8 to 8
- value_rows: bfloat16 [131072, 768], P(('wide', 'narrow')), may hold values from -6 to 6
- upstream: bfloat16 [131072, 768], P(('wide', 'narrow')), may hold values from -12 to 12
- pattern: int32 [1024, 11], P(('wide', 'narrow')), may hold values from 0 to 1, as said below
- expander_pick: int32 [512, 3], P(('wide', 'narrow')), may hold values from 0 to 1
Outputs:
- attention: bfloat16 [131072, 768], P(('wide', 'narrow'))
- query_grad: bfloat16 [131072, 768], P(('wide', 'narrow'))
- key_grad: bfloat16 [131072, 768], P(('wide', 'narrow'))
- value_grad: bfloat16 [131072, 768], P(('wide', 'narrow'))
Inputs may be any that keep to these rules, and one draw needn't show every extreme that they name: `pattern`: row 2 * p + b belongs to block b of partition p and has a 1 in column b. Columns 2 and 3 hold a 1 in some row of every partition. Over the 2 rows of one partition at most 7 columns hold a 1, and in every draw some partition has exactly 7; partitions differ widely in how many.
All inputs are finite; a program needn't handle non-finite values.
Results may differ from a plain program's by a relative error of at most 0.033.
Values may be sent and summed in bfloat16 or wider, within the bound.
No kernel may reach another device: no remote copies, remote signals or barrier semaphores. Data moves between devices by JAX's collectives and lax.ppermute only.
A program may use at most 128 MiB of HBM per device.

v0:
```python
import jax
import jax.numpy as jnp
from jax import lax
from jax.sharding import PartitionSpec as P

D = 768
H = 12
HD = 64
BLK = 128
EXP = 3


def padded(block, sides, width):
    for axis, dim in sides:
        count = lax.axis_size(axis)
        forward = [(i, i + 1) for i in range(count - 1)]
        backward = [(target, source) for source, target in forward]
        low = lax.ppermute(
            lax.slice_in_dim(block, block.shape[dim] - width, None, axis=dim), axis, forward
        )
        high = lax.ppermute(lax.slice_in_dim(block, 0, width, axis=dim), axis, backward)
        block = jnp.concatenate([low, block, high], axis=dim)
    return block


def from_partner(value, axis, distance):
    mask = 2**distance
    pairs = [(source, source ^ mask) for source in range(lax.axis_size(axis))]
    return lax.ppermute(value, axis, pairs)


def attend_group(pieces, allowed):
    query_part, upward_part, key_part, value_part = pieces
    row_count = query_part.shape[0]
    key_count = key_part.shape[0]
    head_count = query_part.shape[1] // HD
    score_scale = HD ** (-0.5)
    query_heads = query_part.reshape(row_count, head_count, HD)
    upward_heads = upward_part.reshape(row_count, head_count, HD)
    key_heads = key_part.reshape(key_count, head_count, HD)
    value_heads = value_part.reshape(key_count, head_count, HD)
    scores = (
        jnp.einsum("qhd,khd->hqk", query_heads, key_heads, preferred_element_type=jnp.float32)
        * score_scale
    )
    scores = jnp.where(allowed[None], scores, -jnp.inf)
    largest = jnp.max(scores, axis=2, keepdims=True)
    summed = jnp.sum(jnp.exp(scores - largest), axis=2, keepdims=True)
    log_norm = largest + jnp.log(summed)
    weights = jnp.exp(scores - log_norm)
    weights_low = weights.astype(jnp.bfloat16)
    attended = jnp.einsum(
        "hqk,khd->qhd", weights_low, value_heads, preferred_element_type=jnp.float32
    ).astype(jnp.bfloat16)
    shifted = jnp.einsum("qhd,qhd->hq", upward_heads, attended, preferred_element_type=jnp.float32)
    weight_grads = jnp.einsum(
        "qhd,khd->hqk", upward_heads, value_heads, preferred_element_type=jnp.float32
    )
    score_grads = (weights * (weight_grads - shifted[:, :, None])).astype(jnp.bfloat16)
    query_grad = (
        jnp.einsum("hqk,khd->qhd", score_grads, key_heads, preferred_element_type=jnp.float32)
        * score_scale
    ).astype(jnp.bfloat16)
    key_term = (
        jnp.einsum("hqk,qhd->khd", score_grads, query_heads, preferred_element_type=jnp.float32)
        * score_scale
    )
    value_term = jnp.einsum(
        "hqk,qhd->khd", weights_low, upward_heads, preferred_element_type=jnp.float32
    )
    return (
        attended.reshape(row_count, -1),
        query_grad.reshape(row_count, -1),
        key_term.reshape(key_count, -1),
        value_term.reshape(key_count, -1),
    )


def attend_all(queries, upstream, pair_rows, allowed):
    group_width = min(H, 2) * HD
    group_total = D // group_width

    def split_heads(tensor):
        return tensor.reshape(tensor.shape[0], group_total, group_width).transpose(1, 0, 2)

    def merge_back(tensor):
        return tensor.transpose(1, 0, 2).reshape(tensor.shape[1], D)

    def group_step(pieces):
        return attend_group(pieces, allowed)

    pieces = (
        split_heads(queries),
        split_heads(upstream),
        split_heads(pair_rows[:, :D]),
        split_heads(pair_rows[:, D:]),
    )
    results = lax.map(group_step, pieces)
    attended, query_grad, key_term, value_term = [merge_back(result) for result in results]
    return (attended, query_grad, jnp.concatenate([key_term, value_term], axis=1))


def on_device(queries, key_rows, value_rows, upstream, pattern, expander_pick):
    block_count = queries.shape[0] // BLK
    wide_total = lax.axis_size("wide")
    narrow_total = lax.axis_size("narrow")
    wide_pos = lax.axis_index("wide")
    narrow_pos = lax.axis_index("narrow")
    top_bit = wide_total.bit_length() - 1
    own_pairs = jnp.concatenate([key_rows, value_rows], axis=1).reshape(block_count, 1, BLK, 2 * D)
    bordered = padded(own_pairs, (("wide", 0), ("narrow", 1)), 1)
    picked = expander_pick[0]
    remote = []
    for expander_slot in range(EXP):
        offered = lax.dynamic_index_in_dim(
            own_pairs[:, 0], picked[expander_slot], 0, keepdims=False
        )
        remote.append(from_partner(offered, "wide", top_bit - 1 - expander_slot))
    candidates = jnp.concatenate(
        [
            bordered[1 : block_count + 1, 1],
            bordered[0:1, 1],
            bordered[block_count + 1 : block_count + 2, 1],
            bordered[1 : block_count + 1, 0],
            bordered[1 : block_count + 1, 2],
            jnp.stack(remote),
        ],
        axis=0,
    )
    ones_own = jnp.ones((block_count,), jnp.int32)
    inside = jnp.concatenate(
        [
            ones_own,
            (wide_pos > 0).astype(jnp.int32)[None],
            (wide_pos < wide_total - 1).astype(jnp.int32)[None],
            ones_own * (narrow_pos > 0).astype(jnp.int32),
            ones_own * (narrow_pos < narrow_total - 1).astype(jnp.int32),
            jnp.ones((EXP,), jnp.int32),
        ]
    )
    permitted = pattern * inside[None, :] > 0
    slot_total = candidates.shape[0]
    allowed = jnp.broadcast_to(
        permitted[:, None, :, None], (block_count, BLK, slot_total, BLK)
    ).reshape(block_count * BLK, slot_total * BLK)
    attended, query_grad, pair_terms = attend_all(
        queries, upstream, candidates.reshape(slot_total * BLK, 2 * D), allowed
    )
    pair_terms = pair_terms.reshape(slot_total, BLK, 2 * D)
    own_grads = pair_terms[:block_count]
    outgoing = pair_terms[block_count:].astype(jnp.bfloat16)
    left_rim = outgoing[0]
    right_rim = outgoing[1]
    lower_rims = outgoing[2 : 2 + block_count]
    upper_rims = outgoing[2 + block_count : 2 + 2 * block_count]
    expander_rims = outgoing[2 + 2 * block_count :]
    block_range = jnp.arange(block_count)
    first_mask = (block_range == 0).astype(jnp.float32)[:, None, None]
    last_mask = (block_range == block_count - 1).astype(jnp.float32)[:, None, None]
    empty_cell = jnp.zeros((1, BLK, 2 * D), jnp.bfloat16)
    wide_column = jnp.concatenate(
        [left_rim[None], jnp.zeros((block_count, BLK, 2 * D), jnp.bfloat16), right_rim[None]],
        axis=0,
    )
    lower_column = jnp.concatenate([empty_cell, lower_rims, empty_cell], axis=0)
    upper_column = jnp.concatenate([empty_cell, upper_rims, empty_cell], axis=0)
    rim_grid = jnp.stack([lower_column, wide_column, upper_column], axis=1)
    returned = padded(rim_grid, (("wide", 0), ("narrow", 1)), 1)
    own_grads = (
        own_grads
        + first_mask * returned[0, 2].astype(jnp.float32)[None]
        + last_mask * returned[block_count + 3, 2].astype(jnp.float32)[None]
    )
    own_grads = (
        own_grads
        + returned[2 : block_count + 2, 0].astype(jnp.float32)
        + returned[2 : block_count + 2, 4].astype(jnp.float32)
    )
    for expander_slot in range(EXP):
        arrived = from_partner(expander_rims[expander_slot], "wide", top_bit - 1 - expander_slot)
        placed = (block_range == picked[expander_slot]).astype(jnp.float32)[:, None, None]
        own_grads = own_grads + placed * arrived.astype(jnp.float32)[None]
    key_grad = own_grads[:, :, :D].reshape(block_count * BLK, D).astype(jnp.bfloat16)
    value_grad = own_grads[:, :, D:].reshape(block_count * BLK, D).astype(jnp.bfloat16)
    return (attended, query_grad, key_grad, value_grad)


def solution(mesh):
    placed = (
        P(("wide", "narrow"), None),
        P(("wide", "narrow"), None),
        P(("wide", "narrow"), None),
        P(("wide", "narrow"), None),
        P(("wide", "narrow"), None),
        P(("wide", "narrow"), None),
    )
    return jax.shard_map(
        on_device,
        mesh=mesh,
        in_specs=placed,
        out_specs=(
            P(("wide", "narrow"), None),
            P(("wide", "narrow"), None),
            P(("wide", "narrow"), None),
            P(("wide", "narrow"), None),
        ),
        check_vma=False,
    )
```

profile of v0, /device:TPU:25, one launch (start us, length us, event | category | flops | bytes accessed | tf_op | source)
XLA Modules:
  0.0 287.5 jit_solution(8147134529734477446)
XLA Ops:
  2.8 4.7 %collective-permute-start = (bf16[1,1,128,1536]{3,2,1,0:T(8,128)(2,1)S(1)}, bf16[1,1,128,1536]{3,2,1,0:T(8,128)(2,1)S(1)}, u32[]{:S(2)}, u32[]{:S(2)}) collective-permute-start(bf16[1,1,128,1536]{3,2,1,0:T(8,128)(2,1)S(1)} %get-tuple-element.141), channel_id=1, source_target_pairs={{0,4},{4,8},{8,12},{12,16},{16,20},{20,24},{24,28},{28,32},{32,36}... | collective-permute-start | bytes 1179656 | tf_op jit(solution)/shard_map/ppermute | solution.py:18
  7.4 11.0 %collective-permute-start.1 = (bf16[1,1,128,1536]{3,2,0,1:T(8,128)(2,1)S(1)}, bf16[1,1,128,1536]{3,2,0,1:T(8,128)(2,1)S(1)}, u32[]{:S(2)}, u32[]{:S(2)}) collective-permute-start(bf16[1,1,128,1536]{3,2,0,1:T(8,128)(2,1)S(1)} %get-tuple-element.140), channel_id=1, source_target_pairs={{4,0},{8,4},{12,8},{16,12},{20,16},{24,20},{28,24},{32,28},{36,32}... | collective-permute-start | bytes 1179656 | tf_op jit(solution)/shard_map/ppermute | solution.py:21
  26.4 3.7 %collective-permute-start.2 = (bf16[4,1,128,1536]{3,2,0,1:T(8,128)(2,1)S(1)}, bf16[4,1,128,1536]{3,2,0,1:T(8,128)(2,1)}, u32[]{:S(2)}, u32[]{:S(2)}) collective-permute-start(bf16[4,1,128,1536]{3,2,0,1:T(8,128)(2,1)S(1)} %pad_maximum_fusion.10), channel_id=1, source_target_pairs={{0,1},{1,2},{2,3},{4,5},{5,6},{6,7},{8,9},{9,10},{10,11},{12,13},{... | collective-permute-start | bytes 4718600 | tf_op jit(solution)/shard_map/ppermute | solution.py:18
  31.2 5.8 %collective-permute-start.4 = (bf16[128,1536]{1,0:T(8,128)(2,1)}, bf16[128,1536]{1,0:T(8,128)(2,1)}, u32[]{:S(2)}, u32[]{:S(2)}) collective-permute-start(bf16[128,1536]{1,0:T(8,128)(2,1)} %get-tuple-element.139), channel_id=1, source_target_pairs={{0,256},{4,260},{8,264},{12,268},{16,272},{20,276},{24,280},{28,28... | collective-permute-start | bytes 1179656 | tf_op jit(solution)/shard_map/ppermute | solution.py:29
  38.9 13.8 %collective-permute-start.6 = (bf16[128,1536]{1,0:T(8,128)(2,1)}, bf16[128,1536]{1,0:T(8,128)(2,1)}, u32[]{:S(2)}, u32[]{:S(2)}) collective-permute-start(bf16[128,1536]{1,0:T(8,128)(2,1)} %get-tuple-element.137), channel_id=1, source_target_pairs={{0,64},{4,68},{8,72},{12,76},{16,80},{20,84},{24,88},{28,92},{32,9... | collective-permute-start | bytes 1179656 | tf_op jit(solution)/shard_map/ppermute | solution.py:29
  58.4 2.5 collective-permute-start.3
  62.3 17.9 %collective-permute-done.3 = bf16[4,1,128,1536]{3,2,0,1:T(8,128)(2,1)S(1)} collective-permute-done((bf16[4,1,128,1536]{3,2,0,1:T(8,128)(2,1)S(1)}, bf16[4,1,128,1536]{3,2,0,1:T(8,128)(2,1)S(1)}, u32[]{:S(2)}, u32[]{:S(2)}) %collective-permute-start.3) | collective-permute-done | bytes 1572896 | tf_op jit(solution)/shard_map/ppermute | solution.py:21
  85.0 4.2 %copy.29 = bf16[1408,768]{0,1:T(8,128)(2,1)} copy(bf16[1408,768]{1,0:T(8,128)(2,1)} %get-tuple-element.134) | data formatting | bytes 4325376 | tf_op jit(solution)/shard_map/slice | solution.py:96
  89.2 2.4 copy.31
  91.6 57.4 %while.17 = (s32[]{:T(128)}, bf16[6,256,128]{1,2,0:T(8,128)(2,1)S(1)}, bf16[6,256,128]{1,2,0:T(8,128)(2,1)}, f32[6,1408,128]{1,2,0:T(8,128)}, f32[6,1408,128]{1,...) while((s32[]{:T(128)}, ...), condition=%wide.region_3.4_spmd.clone, body=%wide.region_0.3_spmd.clone.sunk | while | flops 563428352 | bytes 28399780 | solution.py:98
  149.1 5.9 %copy.33 = f32[1408,768]{1,0:T(8,128)} copy(f32[1408,768]{0,1:T(8,128)} %bitcast.198) | data formatting | bytes 8650752 | tf_op jit(solution)/shard_map/reshape | solution.py:87
  155.0 5.8 %copy.34 = f32[1408,768]{1,0:T(8,128)} copy(f32[1408,768]{0,1:T(8,128)} %bitcast.199) | data formatting | bytes 8650752 | tf_op jit(solution)/shard_map/reshape | solution.py:87
  160.8 4.0 %fusion.11 = bf16[1408,1536]{1,0:T(8,128)(2,1)S(1)} fusion(f32[1408,768]{1,0:T(8,128)} %copy.34, f32[1408,768]{1,0:T(8,128)} %copy.33), kind=kLoop, calls=%fused_computation.29 | loop fusion | flops 8650752 | bytes 12976128 | tf_op jit(solution)/shard_map/convert.8
  166.8 7.8 %collective-permute-start.8 = (bf16[1,3,128,1536]{3,2,0,1:T(8,128)(2,1)S(1)}, bf16[1,3,128,1536]{3,2,0,1:T(8,128)(2,1)S(1)}, u32[]{:S(2)}, u32[]{:S(2)}) collective-permute-start(bf16[1,3,128,1536]{3,2,0,1:T(8,128)(2,1)S(1)} %get-tuple-element.125), channel_id=1, source_target_pairs={{4,0},{8,4},{12,8},{16,12},{20,16},{24,20},{28,24},{32,28},{36,32}... | collective-permute-start | bytes 3538952 | tf_op jit(solution)/shard_map/ppermute | solution.py:21
  176.6 22.6 %collective-permute-done.8 = bf16[1,3,128,1536]{3,2,0,1:T(8,128)(2,1)S(1)} collective-permute-done((bf16[1,3,128,1536]{3,2,0,1:T(8,128)(2,1)S(1)}, bf16[1,3,128,1536]{3,2,0,1:T(8,128)(2,1)S(1)}, u32[]{:S(2)}, u32[]{:S(2)}) %collective-permute-start.8) | collective-permute-done | bytes 1179680 | tf_op jit(solution)/shard_map/ppermute | solution.py:21
  199.2 25.1 %collective-permute-done.7 = bf16[1,3,128,1536]{3,2,0,1:T(8,128)(2,1)S(1)} collective-permute-done((bf16[1,3,128,1536]{3,2,0,1:T(8,128)(2,1)S(1)}, bf16[1,3,128,1536]{3,2,0,1:T(8,128)(2,1)S(1)}, u32[]{:S(2)}, u32[]{:S(2)}) %collective-permute-start.7) | collective-permute-done | bytes 1179680 | tf_op jit(solution)/shard_map/ppermute | solution.py:18
  224.3 2.5 pad_maximum_fusion.5
  226.8 2.4 collective-permute-start.10
  229.2 3.2 %collective-permute-start.9 = (bf16[6,1,128,1536]{3,2,0,1:T(8,128)(2,1)S(1)}, bf16[6,1,128,1536]{3,2,0,1:T(8,128)(2,1)}, u32[]{:S(2)}, u32[]{:S(2)}) collective-permute-start(bf16[6,1,128,1536]{3,2,0,1:T(8,128)(2,1)S(1)} %get-tuple-element.122), channel_id=1, source_target_pairs={{0,1},{1,2},{2,3},{4,5},{5,6},{6,7},{8,9},{9,10},{10,11},{12,13},{... | collective-permute-start | bytes 7077896 | tf_op jit(solution)/shard_map/ppermute | solution.py:18
  233.5 5.4 %collective-permute-start.13 = (bf16[128,1536]{1,0:T(8,128)(2,1)}, bf16[128,1536]{1,0:T(8,128)(2,1)}, u32[]{:S(2)}, u32[]{:S(2)}) collective-permute-start(bf16[128,1536]{1,0:T(8,128)(2,1)} %get-tuple-element.127), channel_id=1, source_target_pairs={{0,64},{4,68},{8,72},{12,76},{16,80},{20,84},{24,88},{28,92},{32,9... | collective-permute-start | bytes 1179656 | tf_op jit(solution)/shard_map/ppermute | solution.py:29
  238.9 3.4 %collective-permute-start.12 = (bf16[128,1536]{1,0:T(8,128)(2,1)}, bf16[128,1536]{1,0:T(8,128)(2,1)}, u32[]{:S(2)}, u32[]{:S(2)}) collective-permute-start(bf16[128,1536]{1,0:T(8,128)(2,1)} %get-tuple-element.128), channel_id=1, source_target_pairs={{0,128},{4,132},{8,136},{12,140},{16,144},{20,148},{24,152},{28,15... | collective-permute-start | bytes 1179656 | tf_op jit(solution)/shard_map/ppermute | solution.py:29
  242.3 3.9 %collective-permute-start.11 = (bf16[128,1536]{1,0:T(8,128)(2,1)}, bf16[128,1536]{1,0:T(8,128)(2,1)}, u32[]{:S(2)}, u32[]{:S(2)}) collective-permute-start(bf16[128,1536]{1,0:T(8,128)(2,1)} %get-tuple-element.126), channel_id=1, source_target_pairs={{0,256},{4,260},{8,264},{12,268},{16,272},{20,276},{24,280},{28,28... | collective-permute-start | bytes 1179656 | tf_op jit(solution)/shard_map/ppermute | solution.py:29
  252.7 27.1 %collective-permute-done.13 = bf16[128,1536]{1,0:T(8,128)(2,1)} collective-permute-done((bf16[128,1536]{1,0:T(8,128)(2,1)}, bf16[128,1536]{1,0:T(8,128)(2,1)}, u32[]{:S(2)}, u32[]{:S(2)}) %collective-permute-start.13) | collective-permute-done | bytes 393248 | tf_op jit(solution)/shard_map/ppermute | solution.py:29
  284.2 2.3 fusion.18
  (167 shorter events, 93.4 us)
Async XLA Ops:
  0.6 17.8 %copy-start.3 = (s32[1,3]{1,0:T(1,128)S(1)}, s32[1,3]{1,0:T(1,128)}, u32[]{:S(2)}) copy-start(s32[1,3]{1,0:T(1,128)} %param.13) | copy-start | bytes 40
  2.8 22.6 %collective-permute-start = (bf16[1,1,128,1536]{3,2,1,0:T(8,128)(2,1)S(1)}, bf16[1,1,128,1536]{3,2,1,0:T(8,128)(2,1)S(1)}, u32[]{:S(2)}, u32[]{:S(2)}) collective-permute-start(bf16[1,1,128,1536]{3,2,1,0:T(8,128)(2,1)S(1)} %get-tuple-element.141), channel_id=1, source_target_pairs={{0,4},{4,8},{8,12},{12,16},{16,20},{20,24},{24,28},{28,32},{32,36}... | collective-permute-start | bytes 1179656 | tf_op jit(solution)/shard_map/ppermute | solution.py:18
  7.4 18.8 %collective-permute-start.1 = (bf16[1,1,128,1536]{3,2,0,1:T(8,128)(2,1)S(1)}, bf16[1,1,128,1536]{3,2,0,1:T(8,128)(2,1)S(1)}, u32[]{:S(2)}, u32[]{:S(2)}) collective-permute-start(bf16[1,1,128,1536]{3,2,0,1:T(8,128)(2,1)S(1)} %get-tuple-element.140), channel_id=1, source_target_pairs={{4,0},{8,4},{12,8},{16,12},{20,16},{24,20},{28,24},{32,28},{36,32}... | collective-permute-start | bytes 1179656 | tf_op jit(solution)/shard_map/ppermute | solution.py:21
  26.4 34.6 %collective-permute-start.2 = (bf16[4,1,128,1536]{3,2,0,1:T(8,128)(2,1)S(1)}, bf16[4,1,128,1536]{3,2,0,1:T(8,128)(2,1)}, u32[]{:S(2)}, u32[]{:S(2)}) collective-permute-start(bf16[4,1,128,1536]{3,2,0,1:T(8,128)(2,1)S(1)} %pad_maximum_fusion.10), channel_id=1, source_target_pairs={{0,1},{1,2},{2,3},{4,5},{5,6},{6,7},{8,9},{9,10},{10,11},{12,13},{... | collective-permute-start | bytes 4718600 | tf_op jit(solution)/shard_map/ppermute | solution.py:18
  30.1 30.9 %copy-start.4 = (s32[2,11]{1,0:T(2,128)S(1)}, s32[2,11]{1,0:T(2,128)}, u32[]{:S(2)}) copy-start(s32[2,11]{1,0:T(2,128)} %param.12) | copy-start | bytes 268
  31.2 49.0 %collective-permute-start.4 = (bf16[128,1536]{1,0:T(8,128)(2,1)}, bf16[128,1536]{1,0:T(8,128)(2,1)}, u32[]{:S(2)}, u32[]{:S(2)}) collective-permute-start(bf16[128,1536]{1,0:T(8,128)(2,1)} %get-tuple-element.139), channel_id=1, source_target_pairs={{0,256},{4,260},{8,264},{12,268},{16,272},{20,276},{24,280},{28,28... | collective-permute-start | bytes 1179656 | tf_op jit(solution)/shard_map/ppermute | solution.py:29
  37.0 44.3 %collective-permute-start.5 = (bf16[128,1536]{1,0:T(8,128)(2,1)}, bf16[128,1536]{1,0:T(8,128)(2,1)}, u32[]{:S(2)}, u32[]{:S(2)}) collective-permute-start(bf16[128,1536]{1,0:T(8,128)(2,1)} %get-tuple-element.138), channel_id=1, source_target_pairs={{0,128},{4,132},{8,136},{12,140},{16,144},{20,148},{24,152},{28,15... | collective-permute-start | bytes 1179656 | tf_op jit(solution)/shard_map/ppermute | solution.py:29
  38.9 43.4 %collective-permute-start.6 = (bf16[128,1536]{1,0:T(8,128)(2,1)}, bf16[128,1536]{1,0:T(8,128)(2,1)}, u32[]{:S(2)}, u32[]{:S(2)}) collective-permute-start(bf16[128,1536]{1,0:T(8,128)(2,1)} %get-tuple-element.137), channel_id=1, source_target_pairs={{0,64},{4,68},{8,72},{12,76},{16,80},{20,84},{24,88},{28,92},{32,9... | collective-permute-start | bytes 1179656 | tf_op jit(solution)/shard_map/ppermute | solution.py:29
  58.4 21.7 %collective-permute-start.3 = (bf16[4,1,128,1536]{3,2,0,1:T(8,128)(2,1)S(1)}, bf16[4,1,128,1536]{3,2,0,1:T(8,128)(2,1)S(1)}, u32[]{:S(2)}, u32[]{:S(2)}) collective-permute-start(bf16[4,1,128,1536]{3,2,0,1:T(8,128)(2,1)S(1)} %pad_maximum_fusion.10), channel_id=1, source_target_pairs={{1,0},{2,1},{3,2},{5,4},{6,5},{7,6},{9,8},{10,9},{11,10},{13,12},{... | collective-permute-start | bytes 4718600 | tf_op jit(solution)/shard_map/ppermute | solution.py:21
  89.2 2.4 copy-start.1
  149.1 5.9 %copy-start.2 = (bf16[6,256,128]{1,2,0:T(8,128)(2,1)}, bf16[6,256,128]{1,2,0:T(8,128)(2,1)S(1)}, u32[]{:S(2)}) copy-start(bf16[6,256,128]{1,2,0:T(8,128)(2,1)S(1)} %get-tuple-element.59) | copy-start | bytes 1179652
  166.8 32.4 %collective-permute-start.8 = (bf16[1,3,128,1536]{3,2,0,1:T(8,128)(2,1)S(1)}, bf16[1,3,128,1536]{3,2,0,1:T(8,128)(2,1)S(1)}, u32[]{:S(2)}, u32[]{:S(2)}) collective-permute-start(bf16[1,3,128,1536]{3,2,0,1:T(8,128)(2,1)S(1)} %get-tuple-element.125), channel_id=1, source_target_pairs={{4,0},{8,4},{12,8},{16,12},{20,16},{24,20},{28,24},{32,28},{36,32}... | collective-permute-start | bytes 3538952 | tf_op jit(solution)/shard_map/ppermute | solution.py:21
  174.6 49.6 %collective-permute-start.7 = (bf16[1,3,128,1536]{3,2,0,1:T(8,128)(2,1)S(1)}, bf16[1,3,128,1536]{3,2,0,1:T(8,128)(2,1)S(1)}, u32[]{:S(2)}, u32[]{:S(2)}) collective-permute-start(bf16[1,3,128,1536]{3,2,0,1:T(8,128)(2,1)S(1)} %get-tuple-element.124), channel_id=1, source_target_pairs={{0,4},{4,8},{8,12},{12,16},{16,20},{20,24},{24,28},{28,32},{32,36}... | collective-permute-start | bytes 3538952 | tf_op jit(solution)/shard_map/ppermute | solution.py:18
  224.3 2.5 copy-start
  226.8 57.4 %collective-permute-start.10 = (bf16[6,1,128,1536]{3,2,0,1:T(8,128)(2,1)}, bf16[6,1,128,1536]{3,2,0,1:T(8,128)(2,1)}, u32[]{:S(2)}, u32[]{:S(2)}) collective-permute-start(bf16[6,1,128,1536]{3,2,0,1:T(8,128)(2,1)} %get-tuple-element.123), channel_id=1, source_target_pairs={{1,0},{2,1},{3,2},{5,4},{6,5},{7,6},{9,8},{10,9},{11,10},{13,12},{... | collective-permute-start | bytes 7077896 | tf_op jit(solution)/shard_map/ppermute | solution.py:21
  229.2 55.0 %collective-permute-start.9 = (bf16[6,1,128,1536]{3,2,0,1:T(8,128)(2,1)S(1)}, bf16[6,1,128,1536]{3,2,0,1:T(8,128)(2,1)}, u32[]{:S(2)}, u32[]{:S(2)}) collective-permute-start(bf16[6,1,128,1536]{3,2,0,1:T(8,128)(2,1)S(1)} %get-tuple-element.122), channel_id=1, source_target_pairs={{0,1},{1,2},{2,3},{4,5},{5,6},{6,7},{8,9},{9,10},{10,11},{12,13},{... | collective-permute-start | bytes 7077896 | tf_op jit(solution)/shard_map/ppermute | solution.py:18
  233.5 46.2 %collective-permute-start.13 = (bf16[128,1536]{1,0:T(8,128)(2,1)}, bf16[128,1536]{1,0:T(8,128)(2,1)}, u32[]{:S(2)}, u32[]{:S(2)}) collective-permute-start(bf16[128,1536]{1,0:T(8,128)(2,1)} %get-tuple-element.127), channel_id=1, source_target_pairs={{0,64},{4,68},{8,72},{12,76},{16,80},{20,84},{24,88},{28,92},{32,9... | collective-permute-start | bytes 1179656 | tf_op jit(solution)/shard_map/ppermute | solution.py:29
  238.9 42.0 %collective-permute-start.12 = (bf16[128,1536]{1,0:T(8,128)(2,1)}, bf16[128,1536]{1,0:T(8,128)(2,1)}, u32[]{:S(2)}, u32[]{:S(2)}) collective-permute-start(bf16[128,1536]{1,0:T(8,128)(2,1)} %get-tuple-element.128), channel_id=1, source_target_pairs={{0,128},{4,132},{8,136},{12,140},{16,144},{20,148},{24,152},{28,15... | collective-permute-start | bytes 1179656 | tf_op jit(solution)/shard_map/ppermute | solution.py:29
  242.3 39.7 %collective-permute-start.11 = (bf16[128,1536]{1,0:T(8,128)(2,1)}, bf16[128,1536]{1,0:T(8,128)(2,1)}, u32[]{:S(2)}, u32[]{:S(2)}) collective-permute-start(bf16[128,1536]{1,0:T(8,128)(2,1)} %get-tuple-element.126), channel_id=1, source_target_pairs={{0,256},{4,260},{8,264},{12,268},{16,272},{20,276},{24,280},{28,28... | collective-permute-start | bytes 1179656 | tf_op jit(solution)/shard_map/ppermute | solution.py:29
  280.9 3.4 %copy-start.5 = (f32[2]{0:T(128)S(1)}, f32[2]{0:T(128)}, u32[]{:S(2)}) copy-start(f32[2]{0:T(128)} %get-tuple-element.150) | copy-start | bytes 28
where the time goes:
time: 293 us; the launch traced here: 287 us
  waiting for transfers between devices  94.7 us (32%)
  starting transfers between devices  71.3 us (24%)
  local copies, waits for them, and re-layouts  70.6 us (24%)
  matrix products  22.9 us (8%)
  other arithmetic  21.2 us (7%)
  between operations  6.34 us (2%)
    ppermute x4, waiting for transfers between devices, padded(): lax.ppermute(lax.slice_in_dim(block, 0, width, axis=dim), axis, backward)  41.4 us
    ppermute x6, starting transfers between devices, from_partner(): return lax.ppermute(value, axis, pairs)  34.2 us
    ppermute x6, waiting for transfers between devices, from_partner(): return lax.ppermute(value, axis, pairs)  27.1 us
    ppermute x4, waiting for transfers between devices, padded(): lax.ppermute(lax.slice_in_dim(block, block.shape[dim] - width, None, axis...  26.1 us
    ppermute x4, starting transfers between devices, padded(): lax.ppermute(lax.slice_in_dim(block, 0, width, axis=dim), axis, backward)  23.7 us
    dynamic_slice x24, local copies, waits for them, and re-layouts, attend_all(): results = lax.map(group_step, pieces)  17.3 us
    ppermute x4, starting transfers between devices, padded(): lax.ppermute(lax.slice_in_dim(block, block.shape[dim] - width, None, axis...  13.4 us
    reshape x2, local copies, waits for them, and re-layouts, merge_back(): return tensor.transpose(1, 0, 2).reshape(tensor.shape[1], D)  11.7 us
  transfers between devices with their start and end apart: 14, of which 6 were waited for; matrix products, arithmetic and copies ran while one was open for 8% of the time, Pallas kernels for 0%

commit v1 on v0

v1 whole, which is shorter than its diff:
```python
import jax
import jax.numpy as jnp
from jax import lax
from jax.experimental import pallas as pl
from jax.experimental.pallas import tpu as pltpu
from jax.sharding import PartitionSpec as P

D = 768
HD = 64
BLK = 128
BW = 2
EXP = 3
ROWS = BW * BLK
NEAR = 2 * BW + 2 + BW + 2
PAIRS = D // BLK
GROUP = 6
SCALE = HD ** (-0.5)
LOG2 = SCALE * 1.4426950408889634
HIDDEN = -1e30

VMEM_LIMIT = 40 * 1024 * 1024
NT = (((1,), (1,)), ((), ()))
NN = (((1,), (0,)), ((), ()))
f32 = jnp.float32
bf16 = jnp.bfloat16


def vmem():
    return pl.BlockSpec(memory_space=pltpu.VMEM)


def smem():
    return pl.BlockSpec(memory_space=pltpu.SMEM)


def dot(a, b, dims):
    return lax.dot_general(a, b, dims, preferred_element_type=f32)


def lanes(pair):
    return pl.ds(pl.multiple_of(pair * BLK, BLK), BLK)


def low_lane(shape):
    return lax.broadcasted_iota(jnp.int32, shape, 1) < HD


def low_row(shape):
    return lax.broadcasted_iota(jnp.int32, shape, 0) < HD


def stacked(tile):
    low = low_lane(tile.shape)
    zero = jnp.zeros_like(tile)
    return jnp.concatenate([jnp.where(low, tile, zero), jnp.where(low, zero, tile)], axis=0)


def stacked_t(tile):
    turned = tile.astype(f32).T
    low = low_row(turned.shape)
    zero = jnp.zeros_like(turned)
    return jnp.concatenate(
        [jnp.where(low, turned, zero), jnp.where(low, zero, turned)], axis=1
    ).astype(bf16)


def by_head(stat):
    return jnp.concatenate(
        [jnp.broadcast_to(stat[0:1], (BLK, ROWS)), jnp.broadcast_to(stat[1:2], (BLK, ROWS))], axis=0
    )


def by_feature(stat):
    return jnp.concatenate(
        [jnp.broadcast_to(stat[0:1], (HD, ROWS)), jnp.broadcast_to(stat[1:2], (HD, ROWS))], axis=0
    )


def seen_row(seen0, seen1):
    first = lax.broadcasted_iota(jnp.int32, (1, ROWS), 1) < BLK
    return jnp.where(first, seen0, seen1) > 0


def head_reduce(fn, tile):
    half = tile.shape[0] // 2
    return jnp.concatenate(
        [fn(tile[:half], axis=0, keepdims=True), fn(tile[half:], axis=0, keepdims=True)], axis=0
    )


def scores_t(key_tile, query_tile):
    return dot(stacked(key_tile), query_tile, NT)


def online(keys, values, queries, row, stat_ref, acc_ref, pairs):
    scores = [scores_t(k, q) for k, q in zip(keys, queries)]
    turned = [stacked_t(v) for v in values]
    probs, decays = [], []
    for pair, tile in zip(pairs, scores):
        old = stat_ref[pair, 0:2, :]
        new = jnp.where(row, jnp.maximum(old, head_reduce(jnp.max, tile) * LOG2), old)
        decay = jnp.exp2(old - new)
        weight = jnp.exp2(tile * LOG2 - by_head(jnp.where(row, new, -HIDDEN)))
        stat_ref[pair, 0:2, :] = new
        stat_ref[pair, 2:4, :] = stat_ref[pair, 2:4, :] * decay + head_reduce(jnp.sum, weight)
        probs.append(weight.astype(bf16))
        decays.append(decay)
    for i, pair in enumerate(pairs):
        acc_ref[pair] = acc_ref[pair] * by_feature(decays[i]) + dot(turned[i], probs[i], NN)


def own_head(product):
    return jnp.where(low_lane((BLK, BLK)), product[:BLK], product[BLK:])


def backward(keys, values, queries, upwards, row, stats):
    scores = [scores_t(k, q) for k, q in zip(keys, queries)]
    products = [dot(stacked(v), u, NT) for v, u in zip(values, upwards)]
    weights, grads = [], []
    for tile, product, stat in zip(scores, products, stats):
        weight = jnp.exp2(tile * LOG2 - by_head(jnp.where(row, stat[0:2], -HIDDEN)))
        weights.append(weight.astype(bf16))
        grads.append((weight * (product - by_head(stat[2:4]))).astype(bf16))
    value_terms = [own_head(dot(w, u, NN)).astype(bf16) for w, u in zip(weights, upwards)]
    key_terms = [(own_head(dot(g, q, NN)) * SCALE).astype(bf16) for g, q in zip(grads, queries)]
    query_ts = [dot(stacked_t(k), g, NN) for k, g in zip(keys, grads)]
    return key_terms, value_terms, query_ts


def groups():
    return [range(first, first + GROUP) for first in range(0, PAIRS, GROUP)]


def near_slots(key, value, left, right, lower, upper, far0, far1):
    own = [(key, b * BLK, value, b * BLK) for b in range(BW)]
    rims = [(r, 0, r, BLK) for r in (left, right)]
    sides = [(r, b * BLK, r, ROWS + b * BLK) for r in (lower, upper) for b in range(BW)]
    fars = [(r, 0, r, BLK) for r in (far0, far1)]
    return own + rims + sides + fars


def feature(pair):
    return slice(pair * BLK, (pair + 1) * BLK)


def load_seen(seen, slots, held, place, sems):
    count = jnp.int32(0)
    for j, (k_ref, k_row, v_ref, v_row) in enumerate(slots):
        used = seen[0, j] + seen[1, j] > 0
        at = count

        @pl.when(used)
        def _():
            place[at] = j
            pltpu.make_async_copy(
                k_ref.at[pl.ds(k_row, BLK)], held.at[at, pl.ds(0, BLK)], sems.at[at]
            ).start()
            pltpu.make_async_copy(
                v_ref.at[pl.ds(v_row, BLK)], held.at[at, pl.ds(BLK, BLK)], sems.at[at]
            ).start()

        count = count + used.astype(jnp.int32)
    return count


def await_slot(held, at, sems):
    pltpu.make_async_copy(held.at[at], held.at[at], sems.at[at]).wait()


def forward_kernel(
    seen, query, upward, key, value, left, right, lower, upper, far0, far1, stat, acc, upward_t, held, place, sems
):
    slots = near_slots(key, value, left, right, lower, upper, far0, far1)
    count = load_seen(seen, slots, held, place, sems)
    for pair in range(PAIRS):
        stat[pair, 0:2, :] = jnp.full((2, ROWS), HIDDEN, f32)
        stat[pair, 2:4, :] = jnp.zeros((2, ROWS), f32)
        acc[pair] = jnp.zeros((BLK, ROWS), f32)
        upward_t[pair] = upward[:, feature(pair)].astype(f32).T

    def step(at, carry):
        await_slot(held, at, sems)
        j = place[at]
        row = seen_row(seen[0, j], seen[1, j])
        for pairs in groups():
            online(
                [held[at, 0:BLK, feature(p)] for p in pairs],
                [held[at, BLK : 2 * BLK, feature(p)] for p in pairs],
                [query[:, feature(p)] for p in pairs],
                row,
                stat,
                acc,
                pairs,
            )
        return carry

    lax.fori_loop(0, count, step, 0)


def middle_kernel(
    seen, query, upward, far2, stat_in, acc_in, upward_t, stat, out_t, query_t, term, acc
):
    last = NEAR
    used = seen[0, last] + seen[1, last] > 0
    row = seen_row(seen[0, last], seen[1, last])
    stat[...] = stat_in[...]
    acc[...] = acc_in[...]

    @pl.when(used)
    def _():
        for pairs in groups():
            online(
                [far2[0:BLK, feature(p)] for p in pairs],
                [far2[BLK : 2 * BLK, feature(p)] for p in pairs],
                [query[:, feature(p)] for p in pairs],
                row,
                stat,
                acc,
                pairs,
            )

    for pair in range(PAIRS):
        total = stat[pair, 2:4, :]
        attended = (acc[pair] * by_feature(1.0 / total)).astype(bf16)
        out_t[pair] = attended
        stat[pair, 0:2, :] = stat[pair, 0:2, :] + jnp.log2(total)
        stat[pair, 2:4, :] = head_reduce(jnp.sum, upward_t[pair] * attended.astype(f32))

    @pl.when(used)
    def _():
        for pairs in groups():
            key_terms, value_terms, grads = backward(
                [far2[0:BLK, feature(p)] for p in pairs],
                [far2[BLK : 2 * BLK, feature(p)] for p in pairs],
                [query[:, feature(p)] for p in pairs],
                [upward[:, feature(p)] for p in pairs],
                row,
                [stat[p] for p in pairs],
            )
            for i, pair in enumerate(pairs):
                term[0:BLK, feature(pair)] = key_terms[i]
                term[BLK : 2 * BLK, feature(pair)] = value_terms[i]
                query_t[pair] = grads[i]

    @pl.when(jnp.logical_not(used))
    def _():
        term[...] = jnp.zeros_like(term)
        query_t[...] = jnp.zeros_like(query_t)


def backward_kernel(
    seen,
    query,
    upward,
    key,
    value,
    left,
    right,
    lower,
    upper,
    far0,
    far1,
    stat,
    out_t,
    query_t_in,
    attention,
    query_grad,
    own_key,
    own_value,
    left_term,
    right_term,
    lower_term,
    upper_term,
    far0_term,
    far1_term,
    query_t,
    held,
    terms,
    place,
    sems,
    out_sems,
):
    sources = near_slots(key, value, left, right, lower, upper, far0, far1)
    targets = near_slots(
        own_key, own_value, left_term, right_term, lower_term, upper_term, far0_term, far1_term
    )
    count = load_seen(seen, sources, held, place, sems)
    for pair in range(PAIRS):
        query_t[pair] = query_t_in[pair]
        attention[:, feature(pair)] = out_t[pair].astype(f32).T.astype(bf16)
    terms[len(sources)] = jnp.zeros((2 * BLK, D), bf16)

    def send(j, at):
        k_ref, k_row, v_ref, v_row = targets[j]
        pltpu.make_async_copy(
            terms.at[at, pl.ds(0, BLK)], k_ref.at[pl.ds(k_row, BLK)], out_sems.at[j]
        ).start()
        pltpu.make_async_copy(
            terms.at[at, pl.ds(BLK, BLK)], v_ref.at[pl.ds(v_row, BLK)], out_sems.at[j]
        ).start()

    for j in range(BW, len(targets)):

        @pl.when(seen[0, j] + seen[1, j] == 0)
        def _():
            send(j, len(targets))

    def step(at, carry):
        await_slot(held, at, sems)
        j = place[at]
        row = seen_row(seen[0, j], seen[1, j])
        for pairs in groups():
            key_terms, value_terms, grads = backward(
                [held[at, 0:BLK, feature(p)] for p in pairs],
                [held[at, BLK : 2 * BLK, feature(p)] for p in pairs],
                [query[:, feature(p)] for p in pairs],
                [upward[:, feature(p)] for p in pairs],
                row,
                [stat[p] for p in pairs],
            )
            for i, pair in enumerate(pairs):
                terms[at, 0:BLK, feature(pair)] = key_terms[i]
                terms[at, BLK : 2 * BLK, feature(pair)] = value_terms[i]
                query_t[pair] = query_t[pair] + grads[i]
        for slot in range(len(targets)):

            @pl.when(j == slot)
            def _():
                send(slot, at)

        return carry

    lax.fori_loop(0, count, step, 0)
    for pair in range(PAIRS):
        query_grad[:, feature(pair)] = (query_t[pair] * SCALE).T.astype(bf16)
    for j in range(len(targets)):
        pltpu.make_async_copy(terms.at[0], terms.at[0], out_sems.at[j]).wait()


def sum_kernel(
    pick, own_key, own_value, low_block, high_block, lower, upper, far0, far1, far2, key_grad, value_grad
):
    for half, (own, out) in enumerate(((own_key, key_grad), (own_value, value_grad))):
        for b in range(BW):
            rows = slice(b * BLK, (b + 1) * BLK)
            side = slice(half * ROWS + b * BLK, half * ROWS + (b + 1) * BLK)
            part = slice(half * BLK, (half + 1) * BLK)
            total = own[rows].astype(f32) + lower[side].astype(f32) + upper[side].astype(f32)
            if b == 0:
                total = total + low_block[part].astype(f32)
            if b == BW - 1:
                total = total + high_block[part].astype(f32)
            for slot, far in enumerate((far0, far1, far2)):
                total = total + jnp.where(pick[0, slot] == b, far[part].astype(f32), 0.0)
            out[rows] = total.astype(bf16)


def call(kernel, shapes, specs, args, scratch=(), outs=None, cost=None):
    return pl.pallas_call(
        kernel,
        out_shape=shapes,
        in_specs=specs,
        out_specs=outs if outs is not None else jax.tree.map(lambda _: vmem(), shapes),
        scratch_shapes=list(scratch),
        compiler_params=pltpu.CompilerParams(vmem_limit_bytes=VMEM_LIMIT),
        cost_estimate=cost,
    )(*args)


def shape(dims, dtype):
    return jax.ShapeDtypeStruct(dims, dtype)


def hbm():
    return pl.BlockSpec(memory_space=pl.ANY)


def block_of(key, value, start, out):
    rows = pl.ds(pl.multiple_of(start, BLK), BLK)
    out[0:BLK] = key[rows]
    out[BLK : 2 * BLK] = value[rows]


def pack_far2_kernel(pick, key, value, out):
    block_of(key, value, pick[0, 2] * BLK, out)


def pack_near_kernel(pick, after, key, value, right, left, far0, far1, whole):
    block_of(key, value, 0, right)
    block_of(key, value, ROWS - BLK, left)
    block_of(key, value, pick[0, 0] * BLK, far0)
    block_of(key, value, pick[0, 1] * BLK, far1)
    whole[0:ROWS] = key[...]
    whole[ROWS : 2 * ROWS] = value[...]


def pack_far2(pick, key, value):
    return call(
        pack_far2_kernel, shape((2 * BLK, D), bf16), [smem(), vmem(), vmem()], (pick, key, value)
    )


def pack_near(pick, after, key, value):
    rim = shape((2 * BLK, D), bf16)
    return call(
        pack_near_kernel,
        [rim] * 4 + [shape((2 * ROWS, D), bf16)],
        [smem(), hbm(), vmem(), vmem()],
        (pick, after, key, value),
    )


def run_forward(seen, near):
    return call(
        forward_kernel,
        [shape((PAIRS, 8, ROWS), f32), shape((PAIRS, BLK, ROWS), f32), shape((PAIRS, BLK, ROWS), f32)],
        [smem()] + [vmem()] * 2 + [hbm()] * (len(near) - 2),
        (seen, *near),
        scratch=[
            pltpu.VMEM((NEAR, 2 * BLK, D), bf16),
            pltpu.SMEM((16,), jnp.int32),
            pltpu.SemaphoreType.DMA((NEAR,)),
        ],
    )


def run_middle(seen, queries, upstream, far2, stat, acc, upward_t):
    return call(
        middle_kernel,
        [
            shape((PAIRS, 8, ROWS), f32),
            shape((PAIRS, BLK, ROWS), bf16),
            shape((PAIRS, BLK, ROWS), f32),
            shape((2 * BLK, D), bf16),
        ],
        [smem()] + [vmem()] * 6,
        (seen, queries, upstream, far2, stat, acc, upward_t),
        scratch=[pltpu.VMEM((PAIRS, BLK, ROWS), f32)],
    )


def run_backward(seen, near, stat, out_t, query_t):
    whole = shape((ROWS, D), bf16)
    rim = shape((2 * BLK, D), bf16)
    side = shape((2 * ROWS, D), bf16)
    return call(
        backward_kernel,
        [whole, whole, whole, whole, rim, rim, side, side, rim, rim],
        [smem()] + [vmem()] * 2 + [hbm()] * (len(near) - 2) + [vmem()] * 3,
        (seen, *near, stat, out_t, query_t),
        outs=[vmem()] * 2 + [hbm()] * 8,
        scratch=[
            pltpu.VMEM((PAIRS, BLK, ROWS), f32),
            pltpu.VMEM((NEAR, 2 * BLK, D), bf16),
            pltpu.VMEM((NEAR + 1, 2 * BLK, D), bf16),
            pltpu.SMEM((16,), jnp.int32),
            pltpu.SemaphoreType.DMA((NEAR,)),
            pltpu.SemaphoreType.DMA((NEAR,)),
        ],
    )


def run_sum(pick, args):
    whole = shape((ROWS, D), bf16)
    return call(sum_kernel, [whole, whole], [smem()] + [vmem()] * len(args), (pick, *args))


def partner(value, distance):
    mask = 2**distance
    return lax.ppermute(value, "wide", [(s, s ^ mask) for s in range(lax.axis_size("wide"))])


def shift(value, axis, step):
    count = lax.axis_size(axis)
    pairs = [(s, s + step) for s in range(count) if 0 <= s + step < count]
    return lax.ppermute(value, axis, pairs)


def on_device(queries, key_rows, value_rows, upstream, pattern, expander_pick):
    wide_total = lax.axis_size("wide")
    narrow_total = lax.axis_size("narrow")
    wide_pos = lax.axis_index("wide")
    narrow_pos = lax.axis_index("narrow")
    top_bit = wide_total.bit_length() - 1

    far2_pair = pack_far2(expander_pick, key_rows, value_rows)
    right_pair, left_pair, far0_pair, far1_pair, whole = pack_near(
        expander_pick, far2_pair, key_rows, value_rows
    )
    far2 = partner(far2_pair, top_bit - EXP)
    far0 = partner(far0_pair, top_bit - 1)
    far1 = partner(far1_pair, top_bit - 2)
    right = shift(right_pair, "wide", -1)
    left = shift(left_pair, "wide", 1)
    lower = shift(whole, "narrow", 1)
    upper = shift(whole, "narrow", -1)

    column = jnp.arange(pattern.shape[1])
    away = (
        ((column == 2) & (wide_pos == 0))
        | ((column == 3) & (wide_pos == wide_total - 1))
        | ((column >= 4) & (column < 6) & (narrow_pos == 0))
        | ((column >= 6) & (column < 8) & (narrow_pos == narrow_total - 1))
    )
    seen = jnp.where(away[None, :], 0, pattern)

    near = (queries, upstream, key_rows, value_rows, left, right, lower, upper, far0, far1)
    stat, acc, upward_t = run_forward(seen, near)
    stat, out_t, query_t, far2_term = run_middle(seen, queries, upstream, far2, stat, acc, upward_t)
    far2_back = partner(far2_term, top_bit - EXP)
    (
        attention,
        query_grad,
        own_key,
        own_value,
        left_term,
        right_term,
        lower_term,
        upper_term,
        far0_term,
        far1_term,
    ) = run_backward(seen, near, stat, out_t, query_t)
    key_grad, value_grad = run_sum(
        expander_pick,
        (
            own_key,
            own_value,
            shift(right_term, "wide", 1),
            shift(left_term, "wide", -1),
            shift(upper_term, "narrow", 1),
            shift(lower_term, "narrow", -1),
            partner(far0_term, top_bit - 1),
            partner(far1_term, top_bit - 2),
            far2_back,
        ),
    )
    return (attention, query_grad, key_grad, value_grad)


def solution(mesh):
    placed = P(("wide", "narrow"), None)
    return jax.shard_map(
        on_device,
        mesh=mesh,
        in_specs=(placed,) * 6,
        out_specs=(placed,) * 4,
        check_vma=False,
    )
```

time: 293 us -> 178 us (0.61); the launches traced: 287 us -> 176 us
  local copies, waits for them, and re-layouts: 70.6 us -> 5.71 us
  waiting for transfers between devices: 94.7 us -> 42.4 us
  starting transfers between devices: 71.3 us -> 99.1 us
  Pallas kernels: 0 us -> 27.4 us
  matrix products: 22.9 us -> 0 us
  other arithmetic: 21.2 us -> 0.01 us
  between operations: 6.34 us -> 0.91 us
    ppermute x14, waiting for transfers between devices: 94.7 us -> 42.4 us  [the longest x6 37.1 us: partner(): lax.ppermute(value, 'wide', [(s, s ^ mask) for s in range(lax.axis_size('...]
    ppermute x14, starting transfers between devices: 71.3 us -> 99.1 us  [the longest x8 55.6 us: shift(): return lax.ppermute(value, axis, pairs)]
    pallas_call x0 -> x6, Pallas kernels: none -> 27.4 us  [call(): pl.pallas_call(kernel, out_shape=shapes, in_specs=specs, out_specs=outs i...]
    dot_general x36 -> x0, matrix products: 22.9 us -> none  [the longest x6 4.93 us: attend_group(): jnp.einsum('qhd,khd->hqk', upward_heads, value_heads, preferred_element_t...]
    dynamic_slice x24 -> x0, local copies, waits for them, and re-layouts: 17.3 us -> none  [attend_all(): results = lax.map(group_step, pieces)]
    reshape x2 -> x0, local copies, waits for them, and re-layouts: 11.7 us -> none  [merge_back(): return tensor.transpose(1, 0, 2).reshape(tensor.shape[1], D)]
    dynamic_update_slice x12 -> x0, local copies, waits for them, and re-layouts: 11.1 us -> none  [attend_all(): results = lax.map(group_step, pieces)]
    slice x8 -> x0, local copies, waits for them, and re-layouts: 11.1 us -> none  [the longest x1 4.16 us: attend_all(): pair_rows[:, D:]]
  transfers between devices with their start and end apart: 14 -> 14, of which waited for: 6 -> 4; matrix products, arithmetic and copies ran while one was open for 8% -> 0% of each run, Pallas kernels for 0% -> 4%
where the time goes in v1:
time: 178 us; the launch traced here: 176 us
  starting transfers between devices  99.1 us (56%)
  waiting for transfers between devices  42.4 us (24%)
  Pallas kernels  27.4 us (15%)
  local copies, waits for them, and re-layouts  5.71 us (3%)
    ppermute x8, starting transfers between devices, shift(): return lax.ppermute(value, axis, pairs)  55.6 us
    ppermute x6, starting transfers between devices, partner(): lax.ppermute(value, 'wide', [(s, s ^ mask) for s in range(lax.axis_size('...  43.5 us
    ppermute x6, waiting for transfers between devices, partner(): lax.ppermute(value, 'wide', [(s, s ^ mask) for s in range(lax.axis_size('...  37.1 us
    pallas_call x6, Pallas kernels, call(): pl.pallas_call(kernel, out_shape=shapes, in_specs=specs, out_specs=outs i...  27.4 us
    unnamed x24, local copies, waits for them, and re-layouts  5.71 us
    ppermute x8, waiting for transfers between devices, shift(): return lax.ppermute(value, axis, pairs)  5.35 us
  transfers between devices with their start and end apart: 14, of which 4 were waited for; matrix products, arithmetic and copies ran while one was open for 0% of the time, Pallas kernels for 4%

profile of v1, /device:TPU:25, one launch (start us, length us, event | category | flops | bytes accessed | tf_op | source)
XLA Modules:
  0.0 175.6 jit_solution(917757232912876741)
XLA Ops:
  1.6 1.0 copy-done.2
  3.3 1.3 shard_map.93.after
  4.6 1.8 %shard_map.94 = (bf16[256,768]{1,0:T(8,128)(2,1)S(1)}, bf16[256,768]{1,0:T(8,128)(2,1)S(1)}, bf16[256,768]{1,0:T(8,128)(2,1)}, bf16[256,768]{1,0:T(8,128)(2,1)}, bf16[512,768]{1,0:T(8,128)(2,1)}) custom-call(s32[1,3]{1,0:T(1,128)S(1)} %copy-done.9, bf16[256,768]{1,0:T(8,128)(2,1)} %shard_map.93.after, bf16[256,768]{1,0:T(8,128)(2,1)S(1)} %copy-done, ...), custom_call_target="tpu_custom_call" | custom-call | tf_op jit(solution)/shard_map/pallas_call | solution.py:359
  6.4 4.6 %collective-permute-start = (bf16[256,768]{1,0:T(8,128)(2,1)S(1)}, bf16[256,768]{1,0:T(8,128)(2,1)S(1)}, u32[]{:S(2)}, u32[]{:S(2)}) collective-permute-start(bf16[256,768]{1,0:T(8,128)(2,1)S(1)} %get-tuple-element.28), channel_id=1, source_target_pairs={{0,4},{4,8},{8,12},{12,16},{16,20},{20,24},{24,28},{28,32},{32,36}... | collective-permute-start | bytes 1179656 | tf_op jit(solution)/shard_map/ppermute | solution.py:476
  11.1 2.9 %collective-permute-start.3 = (bf16[512,768]{1,0:T(8,128)(2,1)}, bf16[512,768]{1,0:T(8,128)(2,1)S(1)}, u32[]{:S(2)}, u32[]{:S(2)}) collective-permute-start(bf16[512,768]{1,0:T(8,128)(2,1)} %get-tuple-element.30), channel_id=1, source_target_pairs={{1,0},{2,1},{3,2},{5,4},{6,5},{7,6},{9,8},{10,9},{11,10},{13,12},{... | collective-permute-start | bytes 2359304 | tf_op jit(solution)/shard_map/ppermute | solution.py:476
  14.0 2.7 %collective-permute-start.2 = (bf16[512,768]{1,0:T(8,128)(2,1)}, bf16[512,768]{1,0:T(8,128)(2,1)S(1)}, u32[]{:S(2)}, u32[]{:S(2)}) collective-permute-start(bf16[512,768]{1,0:T(8,128)(2,1)} %get-tuple-element.30), channel_id=1, source_target_pairs={{0,1},{1,2},{2,3},{4,5},{5,6},{6,7},{8,9},{9,10},{10,11},{12,13},{... | collective-permute-start | bytes 2359304 | tf_op jit(solution)/shard_map/ppermute | solution.py:476
  16.7 11.0 %collective-permute-start.1 = (bf16[256,768]{1,0:T(8,128)(2,1)S(1)}, bf16[256,768]{1,0:T(8,128)(2,1)S(1)}, u32[]{:S(2)}, u32[]{:S(2)}) collective-permute-start(bf16[256,768]{1,0:T(8,128)(2,1)S(1)} %get-tuple-element.29), channel_id=1, source_target_pairs={{4,0},{8,4},{12,8},{16,12},{20,16},{24,20},{28,24},{32,28},{36,32}... | collective-permute-start | bytes 1179656 | tf_op jit(solution)/shard_map/ppermute | solution.py:476
  27.7 2.6 %collective-permute-start.4 = (bf16[256,768]{1,0:T(8,128)(2,1)}, bf16[256,768]{1,0:T(8,128)(2,1)}, u32[]{:S(2)}, u32[]{:S(2)}) collective-permute-start(bf16[256,768]{1,0:T(8,128)(2,1)} %get-tuple-element.31), channel_id=1, source_target_pairs={{0,256},{4,260},{8,264},{12,268},{16,272},{20,276},{24,280},{28,28... | collective-permute-start | bytes 1179656 | tf_op jit(solution)/shard_map/ppermute | solution.py:470
  30.3 1.9 %collective-permute-start.5 = (bf16[256,768]{1,0:T(8,128)(2,1)}, bf16[256,768]{1,0:T(8,128)(2,1)}, u32[]{:S(2)}, u32[]{:S(2)}) collective-permute-start(bf16[256,768]{1,0:T(8,128)(2,1)} %get-tuple-element.32), channel_id=1, source_target_pairs={{0,128},{4,132},{8,136},{12,140},{16,144},{20,148},{24,152},{28,15... | collective-permute-start | bytes 1179656 | tf_op jit(solution)/shard_map/ppermute | solution.py:470
  32.2 5.3 %collective-permute-done.1.right = bf16[256,768]{1,0:T(8,128)(2,1)S(1)} collective-permute-done((bf16[256,768]{1,0:T(8,128)(2,1)S(1)}, bf16[256,768]{1,0:T(8,128)(2,1)S(1)}, u32[]{:S(2)}, u32[]{:S(2)}) %collective-permute-start.1) | collective-permute-done | bytes 393248 | tf_op jit(solution)/shard_map/ppermute | solution.py:476
  38.3 17.5 %collective-permute-start.6 = (bf16[256,768]{1,0:T(8,128)(2,1)}, bf16[256,768]{1,0:T(8,128)(2,1)}, u32[]{:S(2)}, u32[]{:S(2)}) collective-permute-start(bf16[256,768]{1,0:T(8,128)(2,1)} %shard_map.93.after), channel_id=1, source_target_pairs={{0,64},{4,68},{8,72},{12,76},{16,80},{20,84},{24,88},{28,92},{32,9... | collective-permute-start | bytes 1179656 | tf_op jit(solution)/shard_map/ppermute | solution.py:470
  57.6 6.2 %shard_map.95 = (f32[6,8,256]{2,1,0:T(8,128)S(1)}, f32[6,128,256]{2,1,0:T(8,128)S(1)}, f32[6,128,256]{2,1,0:T(8,128)S(1)}) custom-call(s32[2,11]{1,0:T(2,128)S(1)} %broadcast_select_fusion.seen, bf16[256,768]{1,0:T(8,128)(2,1)S(1)} %copy-done.4, bf16[256,768]{1,0:T(8,128)(2,1)S(1)} %copy-done.5, bf16[256,768]{1,0:T(8,128)(2,1)S(1)} %copy-done.1, ...), custom_call_target="tpu_custom_call" | custom-call | tf_op jit(solution)/shard_map/pallas_call | solution.py:359
  63.8 2.2 %collective-permute-done.6.far2 = bf16[256,768]{1,0:T(8,128)(2,1)} collective-permute-done((bf16[256,768]{1,0:T(8,128)(2,1)}, bf16[256,768]{1,0:T(8,128)(2,1)}, u32[]{:S(2)}, u32[]{:S(2)}) %collective-permute-start.6) | collective-permute-done | bytes 393248 | tf_op jit(solution)/shard_map/ppermute | solution.py:470
  66.1 1.4 shard_map.96
  67.4 14.5 %shard_map.97 = (bf16[256,768]{1,0:T(8,128)(2,1)}, bf16[256,768]{1,0:T(8,128)(2,1)}, bf16[256,768]{1,0:T(8,128)(2,1)S(1)}, bf16[256,768]{1,0:T(8,128)(2,1)S(1)},...) custom-call(s32[2,11]{1,0:T(2,128)S(1)} %broadcast_select_fusion.see, ...), custom_call_target="tpu_custom_call" | custom-call | tf_op jit(solution)/shard_map/pallas_call | solution.py:359
  82.0 2.8 %collective-permute-start.7 = (bf16[256,768]{1,0:T(8,128)(2,1)S(1)}, bf16[256,768]{1,0:T(8,128)(2,1)S(1)}, u32[]{:S(2)}, u32[]{:S(2)}) collective-permute-start(bf16[256,768]{1,0:T(8,128)(2,1)S(1)} %get-tuple-element.43), channel_id=1, source_target_pairs={{0,4},{4,8},{8,12},{12,16},{16,20},{20,24},{24,28},{28,32},{32,36}... | collective-permute-start | bytes 1179656 | tf_op jit(solution)/shard_map/ppermute | solution.py:476
  84.8 27.2 %collective-permute-start.8 = (bf16[256,768]{1,0:T(8,128)(2,1)S(1)}, bf16[256,768]{1,0:T(8,128)(2,1)S(1)}, u32[]{:S(2)}, u32[]{:S(2)}) collective-permute-start(bf16[256,768]{1,0:T(8,128)(2,1)S(1)} %get-tuple-element.44), channel_id=1, source_target_pairs={{4,0},{8,4},{12,8},{16,12},{20,16},{24,20},{28,24},{32,28},{36,32}... | collective-permute-start | bytes 1179656 | tf_op jit(solution)/shard_map/ppermute | solution.py:476
  112.0 1.9 %collective-permute-start.9 = (bf16[512,768]{1,0:T(8,128)(2,1)S(1)}, bf16[512,768]{1,0:T(8,128)(2,1)S(1)}, u32[]{:S(2)}, u32[]{:S(2)}) collective-permute-start(bf16[512,768]{1,0:T(8,128)(2,1)S(1)} %get-tuple-element.45), channel_id=1, source_target_pairs={{0,1},{1,2},{2,3},{4,5},{5,6},{6,7},{8,9},{9,10},{10,11},{12,13},{... | collective-permute-start | bytes 2359304 | tf_op jit(solution)/shard_map/ppermute | solution.py:476
  113.9 2.5 %collective-permute-start.10 = (bf16[512,768]{1,0:T(8,128)(2,1)S(1)}, bf16[512,768]{1,0:T(8,128)(2,1)S(1)}, u32[]{:S(2)}, u32[]{:S(2)}) collective-permute-start(bf16[512,768]{1,0:T(8,128)(2,1)S(1)} %get-tuple-element.46), channel_id=1, source_target_pairs={{1,0},{2,1},{3,2},{5,4},{6,5},{7,6},{9,8},{10,9},{11,10},{13,12},{... | collective-permute-start | bytes 2359304 | tf_op jit(solution)/shard_map/ppermute | solution.py:476
  116.4 5.9 %collective-permute-start.11 = (bf16[256,768]{1,0:T(8,128)(2,1)S(1)}, bf16[256,768]{1,0:T(8,128)(2,1)S(1)}, u32[]{:S(2)}, u32[]{:S(2)}) collective-permute-start(bf16[256,768]{1,0:T(8,128)(2,1)S(1)} %get-tuple-element.47), channel_id=1, source_target_pairs={{0,256},{4,260},{8,264},{12,268},{16,272},{20,276},{24,280},{28,28... | collective-permute-start | bytes 1179656 | tf_op jit(solution)/shard_map/ppermute | solution.py:470
  122.3 1.9 %collective-permute-start.12 = (bf16[256,768]{1,0:T(8,128)(2,1)S(1)}, bf16[256,768]{1,0:T(8,128)(2,1)S(1)}, u32[]{:S(2)}, u32[]{:S(2)}) collective-permute-start(bf16[256,768]{1,0:T(8,128)(2,1)S(1)} %get-tuple-element.48), channel_id=1, source_target_pairs={{0,128},{4,132},{8,136},{12,140},{16,144},{20,148},{24,152},{28,15... | collective-permute-start | bytes 1179656 | tf_op jit(solution)/shard_map/ppermute | solution.py:470
  124.2 13.7 %collective-permute-start.13 = (bf16[256,768]{1,0:T(8,128)(2,1)S(1)}, bf16[256,768]{1,0:T(8,128)(2,1)S(1)}, u32[]{:S(2)}, u32[]{:S(2)}) collective-permute-start(bf16[256,768]{1,0:T(8,128)(2,1)S(1)} %get-tuple-element.49), channel_id=1, source_target_pairs={{0,64},{4,68},{8,72},{12,76},{16,80},{20,84},{24,88},{28,92},{32,9... | collective-permute-start | bytes 1179656 | tf_op jit(solution)/shard_map/ppermute | solution.py:470
  138.3 34.5 %collective-permute-done.13.far2 = bf16[256,768]{1,0:T(8,128)(2,1)S(1)} collective-permute-done((bf16[256,768]{1,0:T(8,128)(2,1)S(1)}, bf16[256,768]{1,0:T(8,128)(2,1)S(1)}, u32[]{:S(2)}, u32[]{:S(2)}) %collective-permute-start.13) | collective-permute-done | bytes 393248 | tf_op jit(solution)/shard_map/ppermute | solution.py:470
  173.4 2.1 %shard_map.98 = (bf16[256,768]{1,0:T(8,128)(2,1)}, bf16[256,768]{1,0:T(8,128)(2,1)}) custom-call(s32[1,3]{1,0:T(1,128)S(1)} %copy-done.10, bf16[256,768]{1,0:T(8,128)(2,1)S(1)} %get-tuple-element.41.own_key, bf16[256,768]{1,0:T(8,128)(2,1)S(1)} %get-tuple-element.42.own_value, bf16[256,768]{1,0:T(8,128)(2,1)S(1)} %collective-permute-done.7.low_block, ...), custom_call_target="tpu_custom_call" | custom-call | tf_op jit(solution)/shard_map/pallas_call | solution.py:359
  (36 shorter events, 5.1 us)
Async XLA Ops:
  0.6 1.0 copy-start
  1.6 1.0 copy-start.2
  3.3 53.3 %copy-start.5 = (bf16[256,768]{1,0:T(8,128)(2,1)S(1)}, bf16[256,768]{1,0:T(8,128)(2,1)}, u32[]{:S(2)}) copy-start(bf16[256,768]{1,0:T(8,128)(2,1)} %upward.5) | copy-start | bytes 1179652
  4.6 52.0 %copy-start.1 = (bf16[256,768]{1,0:T(8,128)(2,1)S(1)}, bf16[256,768]{1,0:T(8,128)(2,1)}, u32[]{:S(2)}) copy-start(bf16[256,768]{1,0:T(8,128)(2,1)} %key.7) | copy-start | bytes 1179652
  4.6 52.0 %copy-start.3 = (bf16[256,768]{1,0:T(8,128)(2,1)S(1)}, bf16[256,768]{1,0:T(8,128)(2,1)}, u32[]{:S(2)}) copy-start(bf16[256,768]{1,0:T(8,128)(2,1)} %value.7) | copy-start | bytes 1179652
  4.6 52.0 %copy-start.4 = (bf16[256,768]{1,0:T(8,128)(2,1)S(1)}, bf16[256,768]{1,0:T(8,128)(2,1)}, u32[]{:S(2)}) copy-start(bf16[256,768]{1,0:T(8,128)(2,1)} %query.5) | copy-start | bytes 1179652
  6.4 23.8 %collective-permute-start = (bf16[256,768]{1,0:T(8,128)(2,1)S(1)}, bf16[256,768]{1,0:T(8,128)(2,1)S(1)}, u32[]{:S(2)}, u32[]{:S(2)}) collective-permute-start(bf16[256,768]{1,0:T(8,128)(2,1)S(1)} %get-tuple-element.28), channel_id=1, source_target_pairs={{0,4},{4,8},{8,12},{12,16},{16,20},{20,24},{24,28},{28,32},{32,36}... | collective-permute-start | bytes 1179656 | tf_op jit(solution)/shard_map/ppermute | solution.py:476
  11.1 45.4 %collective-permute-start.3 = (bf16[512,768]{1,0:T(8,128)(2,1)}, bf16[512,768]{1,0:T(8,128)(2,1)S(1)}, u32[]{:S(2)}, u32[]{:S(2)}) collective-permute-start(bf16[512,768]{1,0:T(8,128)(2,1)} %get-tuple-element.30), channel_id=1, source_target_pairs={{1,0},{2,1},{3,2},{5,4},{6,5},{7,6},{9,8},{10,9},{11,10},{13,12},{... | collective-permute-start | bytes 2359304 | tf_op jit(solution)/shard_map/ppermute | solution.py:476
  14.0 42.6 %collective-permute-start.2 = (bf16[512,768]{1,0:T(8,128)(2,1)}, bf16[512,768]{1,0:T(8,128)(2,1)S(1)}, u32[]{:S(2)}, u32[]{:S(2)}) collective-permute-start(bf16[512,768]{1,0:T(8,128)(2,1)} %get-tuple-element.30), channel_id=1, source_target_pairs={{0,1},{1,2},{2,3},{4,5},{5,6},{6,7},{8,9},{9,10},{10,11},{12,13},{... | collective-permute-start | bytes 2359304 | tf_op jit(solution)/shard_map/ppermute | solution.py:476
  16.7 20.9 %collective-permute-start.1 = (bf16[256,768]{1,0:T(8,128)(2,1)S(1)}, bf16[256,768]{1,0:T(8,128)(2,1)S(1)}, u32[]{:S(2)}, u32[]{:S(2)}) collective-permute-start(bf16[256,768]{1,0:T(8,128)(2,1)S(1)} %get-tuple-element.29), channel_id=1, source_target_pairs={{4,0},{8,4},{12,8},{16,12},{20,16},{24,20},{28,24},{32,28},{36,32}... | collective-permute-start | bytes 1179656 | tf_op jit(solution)/shard_map/ppermute | solution.py:476
  27.7 28.8 %collective-permute-start.4 = (bf16[256,768]{1,0:T(8,128)(2,1)}, bf16[256,768]{1,0:T(8,128)(2,1)}, u32[]{:S(2)}, u32[]{:S(2)}) collective-permute-start(bf16[256,768]{1,0:T(8,128)(2,1)} %get-tuple-element.31), channel_id=1, source_target_pairs={{0,256},{4,260},{8,264},{12,268},{16,272},{20,276},{24,280},{28,28... | collective-permute-start | bytes 1179656 | tf_op jit(solution)/shard_map/ppermute | solution.py:470
  30.3 26.2 %collective-permute-start.5 = (bf16[256,768]{1,0:T(8,128)(2,1)}, bf16[256,768]{1,0:T(8,128)(2,1)}, u32[]{:S(2)}, u32[]{:S(2)}) collective-permute-start(bf16[256,768]{1,0:T(8,128)(2,1)} %get-tuple-element.32), channel_id=1, source_target_pairs={{0,128},{4,132},{8,136},{12,140},{16,144},{20,148},{24,152},{28,15... | collective-permute-start | bytes 1179656 | tf_op jit(solution)/shard_map/ppermute | solution.py:470
  37.6 0.7 copy-start.6
  38.3 27.8 %collective-permute-start.6 = (bf16[256,768]{1,0:T(8,128)(2,1)}, bf16[256,768]{1,0:T(8,128)(2,1)}, u32[]{:S(2)}, u32[]{:S(2)}) collective-permute-start(bf16[256,768]{1,0:T(8,128)(2,1)} %shard_map.93.after), channel_id=1, source_target_pairs={{0,64},{4,68},{8,72},{12,76},{16,80},{20,84},{24,88},{28,92},{32,9... | collective-permute-start | bytes 1179656 | tf_op jit(solution)/shard_map/ppermute | solution.py:470
  55.8 0.7 copy-start.11
  56.6 1.0 copy-start.7
  66.1 1.4 copy-start.8
  82.0 40.3 %collective-permute-start.7 = (bf16[256,768]{1,0:T(8,128)(2,1)S(1)}, bf16[256,768]{1,0:T(8,128)(2,1)S(1)}, u32[]{:S(2)}, u32[]{:S(2)}) collective-permute-start(bf16[256,768]{1,0:T(8,128)(2,1)S(1)} %get-tuple-element.43), channel_id=1, source_target_pairs={{0,4},{4,8},{8,12},{12,16},{16,20},{20,24},{24,28},{28,32},{32,36}... | collective-permute-start | bytes 1179656 | tf_op jit(solution)/shard_map/ppermute | solution.py:476
  84.8 39.4 %collective-permute-start.8 = (bf16[256,768]{1,0:T(8,128)(2,1)S(1)}, bf16[256,768]{1,0:T(8,128)(2,1)S(1)}, u32[]{:S(2)}, u32[]{:S(2)}) collective-permute-start(bf16[256,768]{1,0:T(8,128)(2,1)S(1)} %get-tuple-element.44), channel_id=1, source_target_pairs={{4,0},{8,4},{12,8},{16,12},{20,16},{24,20},{28,24},{32,28},{36,32}... | collective-permute-start | bytes 1179656 | tf_op jit(solution)/shard_map/ppermute | solution.py:476
  112.0 60.8 %collective-permute-start.9 = (bf16[512,768]{1,0:T(8,128)(2,1)S(1)}, bf16[512,768]{1,0:T(8,128)(2,1)S(1)}, u32[]{:S(2)}, u32[]{:S(2)}) collective-permute-start(bf16[512,768]{1,0:T(8,128)(2,1)S(1)} %get-tuple-element.45), channel_id=1, source_target_pairs={{0,1},{1,2},{2,3},{4,5},{5,6},{6,7},{8,9},{9,10},{10,11},{12,13},{... | collective-permute-start | bytes 2359304 | tf_op jit(solution)/shard_map/ppermute | solution.py:476
  113.9 58.9 %collective-permute-start.10 = (bf16[512,768]{1,0:T(8,128)(2,1)S(1)}, bf16[512,768]{1,0:T(8,128)(2,1)S(1)}, u32[]{:S(2)}, u32[]{:S(2)}) collective-permute-start(bf16[512,768]{1,0:T(8,128)(2,1)S(1)} %get-tuple-element.46), channel_id=1, source_target_pairs={{1,0},{2,1},{3,2},{5,4},{6,5},{7,6},{9,8},{10,9},{11,10},{13,12},{... | collective-permute-start | bytes 2359304 | tf_op jit(solution)/shard_map/ppermute | solution.py:476
  116.4 21.6 %collective-permute-start.11 = (bf16[256,768]{1,0:T(8,128)(2,1)S(1)}, bf16[256,768]{1,0:T(8,128)(2,1)S(1)}, u32[]{:S(2)}, u32[]{:S(2)}) collective-permute-start(bf16[256,768]{1,0:T(8,128)(2,1)S(1)} %get-tuple-element.47), channel_id=1, source_target_pairs={{0,256},{4,260},{8,264},{12,268},{16,272},{20,276},{24,280},{28,28... | collective-permute-start | bytes 1179656 | tf_op jit(solution)/shard_map/ppermute | solution.py:470
  122.3 16.0 %collective-permute-start.12 = (bf16[256,768]{1,0:T(8,128)(2,1)S(1)}, bf16[256,768]{1,0:T(8,128)(2,1)S(1)}, u32[]{:S(2)}, u32[]{:S(2)}) collective-permute-start(bf16[256,768]{1,0:T(8,128)(2,1)S(1)} %get-tuple-element.48), channel_id=1, source_target_pairs={{0,128},{4,132},{8,136},{12,140},{16,144},{20,148},{24,152},{28,15... | collective-permute-start | bytes 1179656 | tf_op jit(solution)/shard_map/ppermute | solution.py:470
  124.2 48.6 %collective-permute-start.13 = (bf16[256,768]{1,0:T(8,128)(2,1)S(1)}, bf16[256,768]{1,0:T(8,128)(2,1)S(1)}, u32[]{:S(2)}, u32[]{:S(2)}) collective-permute-start(bf16[256,768]{1,0:T(8,128)(2,1)S(1)} %get-tuple-element.49), channel_id=1, source_target_pairs={{0,64},{4,68},{8,72},{12,76},{16,80},{20,84},{24,88},{28,92},{32,9... | collective-permute-start | bytes 1179656 | tf_op jit(solution)/shard_map/ppermute | solution.py:470
  (2 other events, 1.3 us)

commit v2 on v1

v2 whole, which is shorter than its diff:
```python
import jax
import jax.numpy as jnp
from jax import lax
from jax.experimental import pallas as pl
from jax.experimental.pallas import tpu as pltpu
from jax.sharding import PartitionSpec as P

D = 768
HD = 64
BLK = 128
BW = 2
EXP = 3
ROWS = BW * BLK
PAIRS = D // BLK
GROUP = 6
SCALE = HD ** (-0.5)
LOG2 = SCALE * 1.4426950408889634
HIDDEN = -1e30

VMEM_LIMIT = 24 * 1024 * 1024
NT = (((1,), (1,)), ((), ()))
NN = (((1,), (0,)), ((), ()))
f32 = jnp.float32
bf16 = jnp.bfloat16


def vmem():
    return pl.BlockSpec(memory_space=pltpu.VMEM)


def smem():
    return pl.BlockSpec(memory_space=pltpu.SMEM)


def dot(a, b, dims):
    return lax.dot_general(a, b, dims, preferred_element_type=f32)


def lanes(pair):
    return pl.ds(pl.multiple_of(pair * BLK, BLK), BLK)


def low_lane(shape):
    return lax.broadcasted_iota(jnp.int32, shape, 1) < HD


def low_row(shape):
    return lax.broadcasted_iota(jnp.int32, shape, 0) < HD


def stacked(tile):
    low = low_lane(tile.shape)
    zero = jnp.zeros_like(tile)
    return jnp.concatenate([jnp.where(low, tile, zero), jnp.where(low, zero, tile)], axis=0)


def stacked_t(tile):
    turned = tile.astype(f32).T
    low = low_row(turned.shape)
    zero = jnp.zeros_like(turned)
    return jnp.concatenate(
        [jnp.where(low, turned, zero), jnp.where(low, zero, turned)], axis=1
    ).astype(bf16)


def by_head(stat):
    return jnp.concatenate(
        [jnp.broadcast_to(stat[0:1], (BLK, ROWS)), jnp.broadcast_to(stat[1:2], (BLK, ROWS))], axis=0
    )


def by_feature(stat):
    return jnp.concatenate(
        [jnp.broadcast_to(stat[0:1], (HD, ROWS)), jnp.broadcast_to(stat[1:2], (HD, ROWS))], axis=0
    )


def seen_row(seen0, seen1):
    first = lax.broadcasted_iota(jnp.int32, (1, ROWS), 1) < BLK
    return jnp.where(first, seen0, seen1) > 0


def head_reduce(fn, tile):
    half = tile.shape[0] // 2
    return jnp.concatenate(
        [fn(tile[:half], axis=0, keepdims=True), fn(tile[half:], axis=0, keepdims=True)], axis=0
    )


def scores_t(key_tile, query_tile):
    return dot(stacked(key_tile), query_tile, NT)


def online(keys, values, queries, row, stat_ref, acc_ref, pairs):
    scores = [scores_t(k, q) for k, q in zip(keys, queries)]
    turned = [stacked_t(v) for v in values]
    probs, decays = [], []
    for pair, tile in zip(pairs, scores):
        old = stat_ref[pair, 0:2, :]
        new = jnp.where(row, jnp.maximum(old, head_reduce(jnp.max, tile) * LOG2), old)
        decay = jnp.exp2(old - new)
        weight = jnp.exp2(tile * LOG2 - by_head(jnp.where(row, new, -HIDDEN)))
        stat_ref[pair, 0:2, :] = new
        stat_ref[pair, 2:4, :] = stat_ref[pair, 2:4, :] * decay + head_reduce(jnp.sum, weight)
        probs.append(weight.astype(bf16))
        decays.append(decay)
    for i, pair in enumerate(pairs):
        acc_ref[pair] = acc_ref[pair] * by_feature(decays[i]) + dot(turned[i], probs[i], NN)


def own_head(product):
    return jnp.where(low_lane((BLK, BLK)), product[:BLK], product[BLK:])


def backward(keys, values, queries, upwards, row, stats):
    scores = [scores_t(k, q) for k, q in zip(keys, queries)]
    products = [dot(stacked(v), u, NT) for v, u in zip(values, upwards)]
    weights, grads = [], []
    for tile, product, stat in zip(scores, products, stats):
        weight = jnp.exp2(tile * LOG2 - by_head(jnp.where(row, stat[0:2], -HIDDEN)))
        weights.append(weight.astype(bf16))
        grads.append((weight * (product - by_head(stat[2:4]))).astype(bf16))
    value_terms = [own_head(dot(w, u, NN)).astype(bf16) for w, u in zip(weights, upwards)]
    key_terms = [(own_head(dot(g, q, NN)) * SCALE).astype(bf16) for g, q in zip(grads, queries)]
    query_ts = [dot(stacked_t(k), g, NN) for k, g in zip(keys, grads)]
    return key_terms, value_terms, query_ts


def groups():
    return [range(first, first + GROUP) for first in range(0, PAIRS, GROUP)]


def own_slots(key, value):
    return [(b, key, b * BLK, value, b * BLK) for b in range(BW)]


def side_slots(chip, cross):
    return [
        (4 + BW * i + b, ref, b * BLK, ref, ROWS + b * BLK)
        for i, ref in enumerate((chip, cross))
        for b in range(BW)
    ]


def pair_slots(columns, *refs):
    return [(j, ref, 0, ref, BLK) for j, ref in zip(columns, refs)]


def rest_slots(left, right, far0, far1):
    return pair_slots((2, 3, 8, 9), left, right, far0, far1)


def rows_at(start):
    return pl.ds(start if isinstance(start, int) else pl.multiple_of(start, BLK), BLK)


def feature(pair):
    return slice(pair * BLK, (pair + 1) * BLK)


def load_seen(seen, slots, held, place):
    count = jnp.int32(0)
    for j, k_ref, k_row, v_ref, v_row in slots:
        used = seen[0, j] + seen[1, j] > 0
        at = count

        @pl.when(used)
        def _():
            place[at] = j
            held[at, 0:BLK] = k_ref[rows_at(k_row)]
            held[at, BLK : 2 * BLK] = v_ref[rows_at(v_row)]

        count = count + used.astype(jnp.int32)
    return count


def forward_over(slots, seen, query, stat, acc, held, place):
    count = load_seen(seen, slots, held, place)

    def step(at, carry):
        j = place[at]
        row = seen_row(seen[0, j], seen[1, j])
        for pairs in groups():
            online(
                [held[at, 0:BLK, feature(p)] for p in pairs],
                [held[at, BLK : 2 * BLK, feature(p)] for p in pairs],
                [query[:, feature(p)] for p in pairs],
                row,
                stat,
                acc,
                pairs,
            )
        return carry

    lax.fori_loop(0, count, step, 0)


def first_kernel(seen, query, upward, key, value, chip, cross, stat, acc, upward_t, held, place):
    for pair in range(PAIRS):
        stat[pair, 0:2, :] = jnp.full((2, ROWS), HIDDEN, f32)
        stat[pair, 2:4, :] = jnp.zeros((2, ROWS), f32)
        acc[pair] = jnp.zeros((BLK, ROWS), f32)
        upward_t[pair] = upward[:, feature(pair)].astype(f32).T
    forward_over(
        own_slots(key, value) + side_slots(chip, cross), seen, query, stat, acc, held, place
    )


def far_kernel(far2, seen, query, stat_in, acc_in, stat, acc, held, place):
    stat[...] = stat_in[...]
    acc[...] = acc_in[...]
    forward_over(pair_slots((10,), far2), seen, query, stat, acc, held, place)


def clear_unseen(slots, seen):
    for j, k_ref, k_row, v_ref, v_row in slots:

        @pl.when(seen[0, j] + seen[1, j] == 0)
        def _():
            k_ref[k_row : k_row + BLK] = jnp.zeros((BLK, D), bf16)
            v_ref[v_row : v_row + BLK] = jnp.zeros((BLK, D), bf16)


def backward_over(sources, seen, query, upward, stat, query_t, held, place, terms, store):
    count = load_seen(seen, sources, held, place)

    def step(at, carry):
        j = place[at]
        row = seen_row(seen[0, j], seen[1, j])
        for pairs in groups():
            key_terms, value_terms, grads = backward(
                [held[at, 0:BLK, feature(p)] for p in pairs],
                [held[at, BLK : 2 * BLK, feature(p)] for p in pairs],
                [query[:, feature(p)] for p in pairs],
                [upward[:, feature(p)] for p in pairs],
                row,
                [stat[p] for p in pairs],
            )
            for i, pair in enumerate(pairs):
                terms[0:BLK, feature(pair)] = key_terms[i]
                terms[BLK : 2 * BLK, feature(pair)] = value_terms[i]
                query_t[pair] = query_t[pair] + grads[i]
        store(j)
        return carry

    lax.fori_loop(0, count, step, 0)


def store_terms(slots, terms, j):
    for slot, k_ref, k_row, v_ref, v_row in slots:

        @pl.when(j == slot)
        def _():
            k_ref[k_row : k_row + BLK] = terms[0:BLK]
            v_ref[v_row : v_row + BLK] = terms[BLK : 2 * BLK]


def middle_kernel(
    far2,
    seen,
    query,
    upward,
    chip,
    cross,
    left,
    right,
    far0,
    far1,
    stat_in,
    acc_in,
    upward_t,
    stat,
    out_t,
    query_t,
    far2_term,
    chip_term,
    cross_term,
    acc,
    terms,
    held,
    place,
):
    stat[...] = stat_in[...]
    acc[...] = acc_in[...]
    forward_over(rest_slots(left, right, far0, far1), seen, query, stat, acc, held, place)

    for pair in range(PAIRS):
        total = stat[pair, 2:4, :]
        attended = (acc[pair] * by_feature(1.0 / total)).astype(bf16)
        out_t[pair] = attended
        stat[pair, 0:2, :] = stat[pair, 0:2, :] + jnp.log2(total)
        stat[pair, 2:4, :] = head_reduce(jnp.sum, upward_t[pair] * attended.astype(f32))

    query_t[...] = jnp.zeros_like(query_t)
    targets = pair_slots((10,), far2_term) + side_slots(chip_term, cross_term)
    clear_unseen(targets, seen)
    backward_over(
        pair_slots((10,), far2) + side_slots(chip, cross),
        seen,
        query,
        upward,
        stat,
        query_t,
        held,
        place,
        terms,
        lambda j: store_terms(targets, terms, j),
    )


def backward_kernel(
    seen,
    query,
    upward,
    key,
    value,
    left,
    right,
    far0,
    far1,
    chip_back,
    cross_back,
    stat,
    out_t,
    query_t_in,
    attention,
    query_grad,
    key_sum,
    value_sum,
    left_term,
    right_term,
    far0_term,
    far1_term,
    query_t,
    terms,
    held,
    place,
):
    query_t[...] = query_t_in[...]
    for pair in range(PAIRS):
        attention[:, feature(pair)] = out_t[pair].astype(f32).T.astype(bf16)
    targets = rest_slots(left_term, right_term, far0_term, far1_term)
    clear_unseen(targets, seen)

    def store(j):
        for b in range(BW):

            @pl.when(j == b)
            def _():
                for half, out in enumerate((key_sum, value_sum)):
                    side = slice(half * ROWS + b * BLK, half * ROWS + (b + 1) * BLK)
                    out[b * BLK : (b + 1) * BLK] = (
                        terms[half * BLK : (half + 1) * BLK].astype(f32)
                        + chip_back[side].astype(f32)
                        + cross_back[side].astype(f32)
                    )

        store_terms(targets, terms, j)

    backward_over(
        own_slots(key, value) + rest_slots(left, right, far0, far1),
        seen,
        query,
        upward,
        stat,
        query_t,
        held,
        place,
        terms,
        store,
    )
    for pair in range(PAIRS):
        query_grad[:, feature(pair)] = (query_t[pair] * SCALE).T.astype(bf16)


def first_sum_kernel(far2, pick, key_near, value_near, key_sum, value_sum):
    for half, (near, out) in enumerate(((key_near, key_sum), (value_near, value_sum))):
        far_part = far2[half * BLK : (half + 1) * BLK].astype(f32)
        for b in range(BW):
            rows = slice(b * BLK, (b + 1) * BLK)
            out[rows] = near[rows] + jnp.where(pick[0, 2] == b, far_part, 0.0)


def second_sum_kernel(pick, key_sum, value_sum, low_block, high_block, far0, far1, key_grad, value_grad):
    for half, (near, out) in enumerate(((key_sum, key_grad), (value_sum, value_grad))):
        part = slice(half * BLK, (half + 1) * BLK)
        for b in range(BW):
            rows = slice(b * BLK, (b + 1) * BLK)
            total = near[rows]
            if b == 0:
                total = total + low_block[part].astype(f32)
            if b == BW - 1:
                total = total + high_block[part].astype(f32)
            for slot, far in enumerate((far0, far1)):
                total = total + jnp.where(pick[0, slot] == b, far[part].astype(f32), 0.0)
            out[rows] = total.astype(bf16)


def call(kernel, shapes, specs, args, scratch=(), outs=None, cost=None):
    return pl.pallas_call(
        kernel,
        out_shape=shapes,
        in_specs=specs,
        out_specs=outs if outs is not None else jax.tree.map(lambda _: vmem(), shapes),
        scratch_shapes=list(scratch),
        compiler_params=pltpu.CompilerParams(vmem_limit_bytes=VMEM_LIMIT),
        cost_estimate=cost,
    )(*args)


def shape(dims, dtype):
    return jax.ShapeDtypeStruct(dims, dtype)


def hbm():
    return pl.BlockSpec(memory_space=pl.ANY)


STATE = [shape((PAIRS, 8, ROWS), f32), shape((PAIRS, BLK, ROWS), f32)]
RIM = shape((2 * BLK, D), bf16)
SIDE = shape((2 * ROWS, D), bf16)


def block_of(key, value, start, out):
    rows = pl.ds(pl.multiple_of(start, BLK), BLK)
    out[0:BLK] = key[rows]
    out[BLK : 2 * BLK] = value[rows]


def pack_first_kernel(pick, key, value, far2, whole):
    block_of(key, value, pick[0, 2] * BLK, far2)
    whole[0:ROWS] = key[...]
    whole[ROWS : 2 * ROWS] = value[...]


def pack_rest_kernel(pick, chip, cross, key, value, right, left, far0, far1):
    block_of(key, value, 0, right)
    block_of(key, value, ROWS - BLK, left)
    block_of(key, value, pick[0, 0] * BLK, far0)
    block_of(key, value, pick[0, 1] * BLK, far1)


def pack_first(pick, key, value):
    return call(pack_first_kernel, [RIM, SIDE], [smem(), vmem(), vmem()], (pick, key, value))


def pack_rest(pick, chip, cross, key, value):
    return call(
        pack_rest_kernel,
        [RIM] * 4,
        [smem(), hbm(), hbm(), vmem(), vmem()],
        (pick, chip, cross, key, value),
    )


def seen_scratch(slots):
    return [pltpu.VMEM((slots, 2 * BLK, D), bf16), pltpu.SMEM((16,), jnp.int32)]


def run_first(plan, queries, upstream, *near):
    return call(
        first_kernel,
        STATE + [shape((PAIRS, BLK, ROWS), f32)],
        [smem()] + [vmem()] * 6,
        (plan, queries, upstream, *near),
        scratch=seen_scratch(6),
    )


def run_far(far2, plan, queries, stat, acc):
    return call(
        far_kernel,
        STATE,
        [vmem(), smem()] + [vmem()] * 3,
        (far2, plan, queries, stat, acc),
        scratch=seen_scratch(1),
    )


def run_middle(far2, plan, *rest):
    return call(
        middle_kernel,
        [STATE[0], shape((PAIRS, BLK, ROWS), bf16), STATE[1], RIM, SIDE, SIDE],
        [vmem(), smem()] + [vmem()] * 11,
        (far2, plan, *rest),
        scratch=[pltpu.VMEM((PAIRS, BLK, ROWS), f32), pltpu.VMEM((2 * BLK, D), bf16)]
        + seen_scratch(5),
    )


def run_backward(plan, *rest):
    whole = shape((ROWS, D), bf16)
    total = shape((ROWS, D), f32)
    return call(
        backward_kernel,
        [whole, whole, total, total] + [RIM] * 4,
        [smem()] + [vmem()] * 13,
        (plan, *rest),
        scratch=[pltpu.VMEM((PAIRS, BLK, ROWS), f32), pltpu.VMEM((2 * BLK, D), bf16)]
        + seen_scratch(6),
    )


def run_first_sum(far2, pick, *rest):
    whole = shape((ROWS, D), f32)
    return call(
        first_sum_kernel, [whole, whole], [vmem(), smem()] + [vmem()] * 2, (far2, pick, *rest)
    )


def run_second_sum(pick, *rest):
    whole = shape((ROWS, D), bf16)
    return call(second_sum_kernel, [whole, whole], [smem()] + [vmem()] * 6, (pick, *rest))


def sides(chip, cross):
    count = lax.axis_size("narrow")
    across = [(i, i + 1) for i in range(1, count - 1, 2)]
    return (
        lax.ppermute(chip, "narrow", [(i, i ^ 1) for i in range(count)]),
        lax.ppermute(cross, "narrow", across + [(b, a) for a, b in across]),
    )


def partner(value, distance):
    mask = 2**distance
    return lax.ppermute(value, "wide", [(s, s ^ mask) for s in range(lax.axis_size("wide"))])


def shift(value, axis, step):
    count = lax.axis_size(axis)
    pairs = [(s, s + step) for s in range(count) if 0 <= s + step < count]
    return lax.ppermute(value, axis, pairs)


def on_device(queries, key_rows, value_rows, upstream, pattern, expander_pick):
    wide_total = lax.axis_size("wide")
    narrow_total = lax.axis_size("narrow")
    wide_pos = lax.axis_index("wide")
    narrow_pos = lax.axis_index("narrow")
    top_bit = wide_total.bit_length() - 1

    even = narrow_pos & 1 == 0
    near_side = jnp.where(even, pattern[:, 6:8], pattern[:, 4:6])
    far_side = jnp.where(even, pattern[:, 4:6], pattern[:, 6:8])
    inner = (narrow_pos > 0) & (narrow_pos < narrow_total - 1)
    plan = jnp.concatenate(
        [
            pattern[:, 0:2],
            jnp.where(wide_pos > 0, pattern[:, 2:3], 0),
            jnp.where(wide_pos < wide_total - 1, pattern[:, 3:4], 0),
            near_side,
            jnp.where(inner, far_side, 0),
            pattern[:, 8:],
        ],
        axis=1,
    )

    far2_pair, whole = pack_first(expander_pick, key_rows, value_rows)
    chip, cross = sides(whole, whole)
    far2 = partner(far2_pair, top_bit - EXP)
    right_pair, left_pair, far0_pair, far1_pair = pack_rest(
        expander_pick, chip, cross, key_rows, value_rows
    )
    rest = (
        shift(left_pair, "wide", 1),
        shift(right_pair, "wide", -1),
        partner(far0_pair, top_bit - 1),
        partner(far1_pair, top_bit - 2),
    )
    stat, acc, upward_t = run_first(plan, queries, upstream, key_rows, value_rows, chip, cross)
    stat, acc = run_far(far2, plan, queries, stat, acc)
    stat, out_t, query_t, far2_term, chip_term, cross_term = run_middle(
        far2, plan, queries, upstream, chip, cross, *rest, stat, acc, upward_t
    )
    far2_back = partner(far2_term, top_bit - EXP)
    attention, query_grad, key_near, value_near, left_term, right_term, far0_term, far1_term = (
        run_backward(
            plan,
            queries,
            upstream,
            key_rows,
            value_rows,
            *rest,
            *sides(chip_term, cross_term),
            stat,
            out_t,
            query_t,
        )
    )
    key_sum, value_sum = run_first_sum(far2_back, expander_pick, key_near, value_near)
    key_grad, value_grad = run_second_sum(
        expander_pick,
        key_sum,
        value_sum,
        shift(right_term, "wide", 1),
        shift(left_term, "wide", -1),
        partner(far0_term, top_bit - 1),
        partner(far1_term, top_bit - 2),
    )
    return (attention, query_grad, key_grad, value_grad)


def solution(mesh):
    placed = P(("wide", "narrow"), None)
    return jax.shard_map(
        on_device,
        mesh=mesh,
        in_specs=(placed,) * 6,
        out_specs=(placed,) * 4,
        check_vma=False,
    )
```

time: 178 us -> 142 us (0.80)
  the two profiles are of different devices: /device:TPU:25 before, /device:TPU:1 now
where the time goes in v2:
time: 142 us; the launch traced here: 141 us
  starting transfers between devices  86.4 us (61%)
  waiting for transfers between devices  29.5 us (21%)
  Pallas kernels  18.5 us (13%)
  local copies, waits for them, and re-layouts  5.39 us (4%)
    ppermute x6, starting transfers between devices, partner(): lax.ppermute(value, 'wide', [(s, s ^ mask) for s in range(lax.axis_size('...  49.5 us
    ppermute x6, waiting for transfers between devices, partner(): lax.ppermute(value, 'wide', [(s, s ^ mask) for s in range(lax.axis_size('...  29.5 us
    pallas_call x8, Pallas kernels, call(): pl.pallas_call(kernel, out_shape=shapes, in_specs=specs, out_specs=outs i...  18.5 us
    ppermute x2, starting transfers between devices, sides(): lax.ppermute(chip, 'narrow', [(i, i ^ 1) for i in range(count)])  17.1 us
    ppermute x4, starting transfers between devices, shift(): return lax.ppermute(value, axis, pairs)  13.3 us
    ppermute x2, starting transfers between devices, sides(): lax.ppermute(cross, 'narrow', across + [(b, a) for a, b in across])  6.42 us
    unnamed x18, local copies, waits for them, and re-layouts  3.94 us
  transfers between devices with their start and end apart: 14, of which 5 were waited for; matrix products, arithmetic and copies ran while one was open for 2% of the time, Pallas kernels for 9%

profile of v2, /device:TPU:1, one launch (start us, length us, event | category | flops | bytes accessed | tf_op | source)
XLA Modules:
  0.0 141.4 jit_solution(1161545300380089355)
XLA Ops:
  3.3 1.6 %shard_map.93 = (bf16[256,768]{1,0:T(8,128)(2,1)}, bf16[512,768]{1,0:T(8,128)(2,1)}) custom-call(s32[1,3]{1,0:T(1,128)S(1)} %copy-done.6, bf16[256,768]{1,0:T(8,128)(2,1)S(1)} %copy-done.1, bf16[256,768]{1,0:T(8,128)(2,1)S(1)} %copy-done.3), custom_call_target="tpu_custom_call" | custom-call | tf_op jit(solution)/shard_map/pallas_call | solution.py:400
  4.9 4.5 %collective-permute-start.1 = (bf16[512,768]{1,0:T(8,128)(2,1)}, bf16[512,768]{1,0:T(8,128)(2,1)S(1)}, u32[]{:S(2)}, u32[]{:S(2)}) collective-permute-start(bf16[512,768]{1,0:T(8,128)(2,1)} %get-tuple-element.33), channel_id=1, source_target_pairs={{1,2},{2,1},{5,6},{6,5},{9,10},{10,9},{13,14},{14,13},{17,18},{18,... | collective-permute-start | bytes 2359304 | tf_op jit(solution)/shard_map/ppermute | solution.py:521
  9.4 5.0 %collective-permute-start = (bf16[512,768]{1,0:T(8,128)(2,1)}, bf16[512,768]{1,0:T(8,128)(2,1)S(1)}, u32[]{:S(2)}, u32[]{:S(2)}) collective-permute-start(bf16[512,768]{1,0:T(8,128)(2,1)} %get-tuple-element.33), channel_id=1, source_target_pairs={{0,1},{1,0},{2,3},{3,2},{4,5},{5,4},{6,7},{7,6},{8,9},{9,8},{10,11... | collective-permute-start | bytes 2359304 | tf_op jit(solution)/shard_map/ppermute | solution.py:520
  14.4 12.4 %collective-permute-start.6 = (bf16[256,768]{1,0:T(8,128)(2,1)}, bf16[256,768]{1,0:T(8,128)(2,1)}, u32[]{:S(2)}, u32[]{:S(2)}) collective-permute-start(bf16[256,768]{1,0:T(8,128)(2,1)} %get-tuple-element.38), channel_id=1, source_target_pairs={{0,64},{4,68},{8,72},{12,76},{16,80},{20,84},{24,88},{28,92},{32,9... | collective-permute-start | bytes 1179656 | tf_op jit(solution)/shard_map/ppermute | solution.py:527
  28.8 1.8 %shard_map.94 = (bf16[256,768]{1,0:T(8,128)(2,1)}, bf16[256,768]{1,0:T(8,128)(2,1)}, bf16[256,768]{1,0:T(8,128)(2,1)}, bf16[256,768]{1,0:T(8,128)(2,1)}) custom-call(s32[1,3]{1,0:T(1,128)S(1)} %copy-done.7, bf16[512,768]{1,0:T(8,128)(2,1)S(1)} %collective-permute-done.chip, bf16[512,768]{1,0:T(8,128)(2,1)S(1)} %collective-permute-done.1.cross, ...), custom_call_target="tpu_custom_call" | custom-call | tf_op jit(solution)/shard_map/pallas_call | solution.py:400
  30.6 4.4 %collective-permute-start.2 = (bf16[256,768]{1,0:T(8,128)(2,1)}, bf16[256,768]{1,0:T(8,128)(2,1)S(1)}, u32[]{:S(2)}, u32[]{:S(2)}) collective-permute-start(bf16[256,768]{1,0:T(8,128)(2,1)} %get-tuple-element.34), channel_id=1, source_target_pairs={{0,4},{4,8},{8,12},{12,16},{16,20},{20,24},{24,28},{28,32},{32,36}... | collective-permute-start | bytes 1179656 | tf_op jit(solution)/shard_map/ppermute | solution.py:533
  35.0 1.3 collective-permute-start.3
  36.3 9.0 %collective-permute-start.4 = (bf16[256,768]{1,0:T(8,128)(2,1)}, bf16[256,768]{1,0:T(8,128)(2,1)}, u32[]{:S(2)}, u32[]{:S(2)}) collective-permute-start(bf16[256,768]{1,0:T(8,128)(2,1)} %get-tuple-element.36), channel_id=1, source_target_pairs={{0,256},{4,260},{8,264},{12,268},{16,272},{20,276},{24,280},{28,28... | collective-permute-start | bytes 1179656 | tf_op jit(solution)/shard_map/ppermute | solution.py:527
  45.2 2.3 %collective-permute-start.5 = (bf16[256,768]{1,0:T(8,128)(2,1)}, bf16[256,768]{1,0:T(8,128)(2,1)}, u32[]{:S(2)}, u32[]{:S(2)}) collective-permute-start(bf16[256,768]{1,0:T(8,128)(2,1)} %get-tuple-element.37), channel_id=1, source_target_pairs={{0,128},{4,132},{8,136},{12,140},{16,144},{20,148},{24,152},{28,15... | collective-permute-start | bytes 1179656 | tf_op jit(solution)/shard_map/ppermute | solution.py:527
  49.1 2.5 %shard_map.95 = (f32[6,8,256]{2,1,0:T(8,128)S(1)}, f32[6,128,256]{2,1,0:T(8,128)S(1)}, f32[6,128,256]{2,1,0:T(8,128)S(1)}) custom-call(s32[2,11]{1,0:T(2,128)S(1)} %concatenate.3.seen, bf16[256,768]{1,0:T(8,128)(2,1)S(1)} %copy-done, bf16[256,768]{1,0:T(8,128)(2,1)S(1)} %copy-done.5, bf16[256,768]{1,0:T(8,128)(2,1)S(1)} %copy-done.2, ...), custom_call_target="tpu_custom_call" | custom-call | tf_op jit(solution)/shard_map/pallas_call | solution.py:400
  53.7 8.5 %collective-permute-done.5.far1 = bf16[256,768]{1,0:T(8,128)(2,1)} collective-permute-done((bf16[256,768]{1,0:T(8,128)(2,1)}, bf16[256,768]{1,0:T(8,128)(2,1)}, u32[]{:S(2)}, u32[]{:S(2)}) %collective-permute-start.5) | collective-permute-done | bytes 393248 | tf_op jit(solution)/shard_map/ppermute | solution.py:527
  62.2 2.7 %shard_map.97 = (f32[6,8,256]{2,1,0:T(8,128)S(1)}, bf16[6,128,256]{2,1,0:T(8,128)(2,1)S(1)}, f32[6,128,256]{2,1,0:T(8,128)S(1)}, bf16[256,768]{1,0:T(8,128)(2,1)...) custom-call(bf16[256,768]{1,0:T(8,128)(2,1)} %collective-permute-done.6.far2, ...), custom_call_target="tpu_custom_call" | custom-call | tf_op jit(solution)/shard_map/pallas_call | solution.py:400
  64.9 12.1 %collective-permute-start.7 = (bf16[512,768]{1,0:T(8,128)(2,1)S(1)}, bf16[512,768]{1,0:T(8,128)(2,1)S(1)}, u32[]{:S(2)}, u32[]{:S(2)}) collective-permute-start(bf16[512,768]{1,0:T(8,128)(2,1)S(1)} %get-tuple-element.44), channel_id=1, source_target_pairs={{0,1},{1,0},{2,3},{3,2},{4,5},{5,4},{6,7},{7,6},{8,9},{9,8},{10,11... | collective-permute-start | bytes 2359304 | tf_op jit(solution)/shard_map/ppermute | solution.py:520
  77.1 1.9 %collective-permute-start.8 = (bf16[512,768]{1,0:T(8,128)(2,1)S(1)}, bf16[512,768]{1,0:T(8,128)(2,1)S(1)}, u32[]{:S(2)}, u32[]{:S(2)}) collective-permute-start(bf16[512,768]{1,0:T(8,128)(2,1)S(1)} %get-tuple-element.45), channel_id=1, source_target_pairs={{1,2},{2,1},{5,6},{6,5},{9,10},{10,9},{13,14},{14,13},{17,18},{18,... | collective-permute-start | bytes 2359304 | tf_op jit(solution)/shard_map/ppermute | solution.py:521
  79.0 13.0 %collective-permute-start.9 = (bf16[256,768]{1,0:T(8,128)(2,1)S(1)}, bf16[256,768]{1,0:T(8,128)(2,1)S(1)}, u32[]{:S(2)}, u32[]{:S(2)}) collective-permute-start(bf16[256,768]{1,0:T(8,128)(2,1)S(1)} %get-tuple-element.51), channel_id=1, source_target_pairs={{0,64},{4,68},{8,72},{12,76},{16,80},{20,84},{24,88},{28,92},{32,9... | collective-permute-start | bytes 1179656 | tf_op jit(solution)/shard_map/ppermute | solution.py:527
  92.0 6.4 %shard_map.98 = (bf16[256,768]{1,0:T(8,128)(2,1)}, bf16[256,768]{1,0:T(8,128)(2,1)}, f32[256,768]{1,0:T(8,128)S(1)}, f32[256,768]{1,0:T(8,128)S(1)}, bf16[256,76...) custom-call(s32[2,11]{1,0:T(2,128)S(1)} %concatenate.3.seen, ...), custom_call_target="tpu_custom_call" | custom-call | tf_op jit(solution)/shard_map/pallas_call | solution.py:400
  98.4 6.4 %collective-permute-start.10 = (bf16[256,768]{1,0:T(8,128)(2,1)S(1)}, bf16[256,768]{1,0:T(8,128)(2,1)S(1)}, u32[]{:S(2)}, u32[]{:S(2)}) collective-permute-start(bf16[256,768]{1,0:T(8,128)(2,1)S(1)} %get-tuple-element.56), channel_id=1, source_target_pairs={{0,4},{4,8},{8,12},{12,16},{16,20},{20,24},{24,28},{28,32},{32,36}... | collective-permute-start | bytes 1179656 | tf_op jit(solution)/shard_map/ppermute | solution.py:533
  104.8 1.3 collective-permute-start.11
  106.1 9.5 %collective-permute-start.12 = (bf16[256,768]{1,0:T(8,128)(2,1)S(1)}, bf16[256,768]{1,0:T(8,128)(2,1)S(1)}, u32[]{:S(2)}, u32[]{:S(2)}) collective-permute-start(bf16[256,768]{1,0:T(8,128)(2,1)S(1)} %get-tuple-element.58), channel_id=1, source_target_pairs={{0,256},{4,260},{8,264},{12,268},{16,272},{20,276},{24,280},{28,28... | collective-permute-start | bytes 1179656 | tf_op jit(solution)/shard_map/ppermute | solution.py:527
  115.7 3.3 %collective-permute-start.13 = (bf16[256,768]{1,0:T(8,128)(2,1)S(1)}, bf16[256,768]{1,0:T(8,128)(2,1)S(1)}, u32[]{:S(2)}, u32[]{:S(2)}) collective-permute-start(bf16[256,768]{1,0:T(8,128)(2,1)S(1)} %get-tuple-element.59), channel_id=1, source_target_pairs={{0,128},{4,132},{8,136},{12,140},{16,144},{20,148},{24,152},{28,15... | collective-permute-start | bytes 1179656 | tf_op jit(solution)/shard_map/ppermute | solution.py:527
  119.0 7.0 %collective-permute-done.9.far2 = bf16[256,768]{1,0:T(8,128)(2,1)S(1)} collective-permute-done((bf16[256,768]{1,0:T(8,128)(2,1)S(1)}, bf16[256,768]{1,0:T(8,128)(2,1)S(1)}, u32[]{:S(2)}, u32[]{:S(2)}) %collective-permute-start.9) | collective-permute-done | bytes 393248 | tf_op jit(solution)/shard_map/ppermute | solution.py:527
  126.7 6.8 %collective-permute-done.12.far0 = bf16[256,768]{1,0:T(8,128)(2,1)S(1)} collective-permute-done((bf16[256,768]{1,0:T(8,128)(2,1)S(1)}, bf16[256,768]{1,0:T(8,128)(2,1)S(1)}, u32[]{:S(2)}, u32[]{:S(2)}) %collective-permute-start.12) | collective-permute-done | bytes 393248 | tf_op jit(solution)/shard_map/ppermute | solution.py:527
  133.5 6.2 %collective-permute-done.13.far1 = bf16[256,768]{1,0:T(8,128)(2,1)S(1)} collective-permute-done((bf16[256,768]{1,0:T(8,128)(2,1)S(1)}, bf16[256,768]{1,0:T(8,128)(2,1)S(1)}, u32[]{:S(2)}, u32[]{:S(2)}) %collective-permute-start.13) | collective-permute-done | bytes 393248 | tf_op jit(solution)/shard_map/ppermute | solution.py:527
  139.7 1.7 %shard_map.100 = (bf16[256,768]{1,0:T(8,128)(2,1)}, bf16[256,768]{1,0:T(8,128)(2,1)}) custom-call(s32[1,3]{1,0:T(1,128)S(1)} %copy-done.7, f32[256,768]{1,0:T(8,128)S(1)} %get-tuple-element.54.key_sum, f32[256,768]{1,0:T(8,128)S(1)} %get-tuple-element.55.value_sum, bf16[256,768]{1,0:T(8,128)(2,1)S(1)} %collective-permute-done.10.low_block, ...), custom_call_target="tpu_custom_call" | custom-call | tf_op jit(solution)/shard_map/pallas_call | solution.py:400
  (34 shorter events, 8.9 us)
Async XLA Ops:
  0.6 1.0 copy-start.1
  1.6 1.0 copy-start.3
  2.6 0.7 copy-start.6
  3.3 24.9 %copy-start.2 = (bf16[256,768]{1,0:T(8,128)(2,1)S(1)}, bf16[256,768]{1,0:T(8,128)(2,1)}, u32[]{:S(2)}) copy-start(bf16[256,768]{1,0:T(8,128)(2,1)} %key.7) | copy-start | bytes 1179652
  3.3 24.9 %copy-start.4 = (bf16[256,768]{1,0:T(8,128)(2,1)S(1)}, bf16[256,768]{1,0:T(8,128)(2,1)}, u32[]{:S(2)}) copy-start(bf16[256,768]{1,0:T(8,128)(2,1)} %value.7) | copy-start | bytes 1179652
  4.9 23.3 %collective-permute-start.1 = (bf16[512,768]{1,0:T(8,128)(2,1)}, bf16[512,768]{1,0:T(8,128)(2,1)S(1)}, u32[]{:S(2)}, u32[]{:S(2)}) collective-permute-start(bf16[512,768]{1,0:T(8,128)(2,1)} %get-tuple-element.33), channel_id=1, source_target_pairs={{1,2},{2,1},{5,6},{6,5},{9,10},{10,9},{13,14},{14,13},{17,18},{18,... | collective-permute-start | bytes 2359304 | tf_op jit(solution)/shard_map/ppermute | solution.py:521
  9.4 18.8 %collective-permute-start = (bf16[512,768]{1,0:T(8,128)(2,1)}, bf16[512,768]{1,0:T(8,128)(2,1)S(1)}, u32[]{:S(2)}, u32[]{:S(2)}) collective-permute-start(bf16[512,768]{1,0:T(8,128)(2,1)} %get-tuple-element.33), channel_id=1, source_target_pairs={{0,1},{1,0},{2,3},{3,2},{4,5},{5,4},{6,7},{7,6},{8,9},{9,8},{10,11... | collective-permute-start | bytes 2359304 | tf_op jit(solution)/shard_map/ppermute | solution.py:520
  14.4 37.1 %collective-permute-start.6 = (bf16[256,768]{1,0:T(8,128)(2,1)}, bf16[256,768]{1,0:T(8,128)(2,1)}, u32[]{:S(2)}, u32[]{:S(2)}) collective-permute-start(bf16[256,768]{1,0:T(8,128)(2,1)} %get-tuple-element.38), channel_id=1, source_target_pairs={{0,64},{4,68},{8,72},{12,76},{16,80},{20,84},{24,88},{28,92},{32,9... | collective-permute-start | bytes 1179656 | tf_op jit(solution)/shard_map/ppermute | solution.py:527
  26.8 0.7 copy-start.8
  28.2 0.7 copy-start.7
  28.2 20.9 %copy-start = (bf16[256,768]{1,0:T(8,128)(2,1)S(1)}, bf16[256,768]{1,0:T(8,128)(2,1)}, u32[]{:S(2)}) copy-start(bf16[256,768]{1,0:T(8,128)(2,1)} %query.7) | copy-start | bytes 1179652
  28.2 20.9 %copy-start.5 = (bf16[256,768]{1,0:T(8,128)(2,1)S(1)}, bf16[256,768]{1,0:T(8,128)(2,1)}, u32[]{:S(2)}) copy-start(bf16[256,768]{1,0:T(8,128)(2,1)} %upward.5) | copy-start | bytes 1179652
  30.6 22.0 %collective-permute-start.2 = (bf16[256,768]{1,0:T(8,128)(2,1)}, bf16[256,768]{1,0:T(8,128)(2,1)S(1)}, u32[]{:S(2)}, u32[]{:S(2)}) collective-permute-start(bf16[256,768]{1,0:T(8,128)(2,1)} %get-tuple-element.34), channel_id=1, source_target_pairs={{0,4},{4,8},{8,12},{12,16},{16,20},{20,24},{24,28},{28,32},{32,36}... | collective-permute-start | bytes 1179656 | tf_op jit(solution)/shard_map/ppermute | solution.py:533
  35.0 17.6 %collective-permute-start.3 = (bf16[256,768]{1,0:T(8,128)(2,1)}, bf16[256,768]{1,0:T(8,128)(2,1)}, u32[]{:S(2)}, u32[]{:S(2)}) collective-permute-start(bf16[256,768]{1,0:T(8,128)(2,1)} %get-tuple-element.35), channel_id=1, source_target_pairs={{4,0},{8,4},{12,8},{16,12},{20,16},{24,20},{28,24},{32,28},{36,32}... | collective-permute-start | bytes 1179656 | tf_op jit(solution)/shard_map/ppermute | solution.py:533
  36.3 17.4 %collective-permute-start.4 = (bf16[256,768]{1,0:T(8,128)(2,1)}, bf16[256,768]{1,0:T(8,128)(2,1)}, u32[]{:S(2)}, u32[]{:S(2)}) collective-permute-start(bf16[256,768]{1,0:T(8,128)(2,1)} %get-tuple-element.36), channel_id=1, source_target_pairs={{0,256},{4,260},{8,264},{12,268},{16,272},{20,276},{24,280},{28,28... | collective-permute-start | bytes 1179656 | tf_op jit(solution)/shard_map/ppermute | solution.py:527
  45.2 16.9 %collective-permute-start.5 = (bf16[256,768]{1,0:T(8,128)(2,1)}, bf16[256,768]{1,0:T(8,128)(2,1)}, u32[]{:S(2)}, u32[]{:S(2)}) collective-permute-start(bf16[256,768]{1,0:T(8,128)(2,1)} %get-tuple-element.37), channel_id=1, source_target_pairs={{0,128},{4,132},{8,136},{12,140},{16,144},{20,148},{24,152},{28,15... | collective-permute-start | bytes 1179656 | tf_op jit(solution)/shard_map/ppermute | solution.py:527
  64.9 27.1 %collective-permute-start.7 = (bf16[512,768]{1,0:T(8,128)(2,1)S(1)}, bf16[512,768]{1,0:T(8,128)(2,1)S(1)}, u32[]{:S(2)}, u32[]{:S(2)}) collective-permute-start(bf16[512,768]{1,0:T(8,128)(2,1)S(1)} %get-tuple-element.44), channel_id=1, source_target_pairs={{0,1},{1,0},{2,3},{3,2},{4,5},{5,4},{6,7},{7,6},{8,9},{9,8},{10,11... | collective-permute-start | bytes 2359304 | tf_op jit(solution)/shard_map/ppermute | solution.py:520
  77.1 14.9 %collective-permute-start.8 = (bf16[512,768]{1,0:T(8,128)(2,1)S(1)}, bf16[512,768]{1,0:T(8,128)(2,1)S(1)}, u32[]{:S(2)}, u32[]{:S(2)}) collective-permute-start(bf16[512,768]{1,0:T(8,128)(2,1)S(1)} %get-tuple-element.45), channel_id=1, source_target_pairs={{1,2},{2,1},{5,6},{6,5},{9,10},{10,9},{13,14},{14,13},{17,18},{18,... | collective-permute-start | bytes 2359304 | tf_op jit(solution)/shard_map/ppermute | solution.py:521
  79.0 47.0 %collective-permute-start.9 = (bf16[256,768]{1,0:T(8,128)(2,1)S(1)}, bf16[256,768]{1,0:T(8,128)(2,1)S(1)}, u32[]{:S(2)}, u32[]{:S(2)}) collective-permute-start(bf16[256,768]{1,0:T(8,128)(2,1)S(1)} %get-tuple-element.51), channel_id=1, source_target_pairs={{0,64},{4,68},{8,72},{12,76},{16,80},{20,84},{24,88},{28,92},{32,9... | collective-permute-start | bytes 1179656 | tf_op jit(solution)/shard_map/ppermute | solution.py:527
  98.4 28.2 %collective-permute-start.10 = (bf16[256,768]{1,0:T(8,128)(2,1)S(1)}, bf16[256,768]{1,0:T(8,128)(2,1)S(1)}, u32[]{:S(2)}, u32[]{:S(2)}) collective-permute-start(bf16[256,768]{1,0:T(8,128)(2,1)S(1)} %get-tuple-element.56), channel_id=1, source_target_pairs={{0,4},{4,8},{8,12},{12,16},{16,20},{20,24},{24,28},{28,32},{32,36}... | collective-permute-start | bytes 1179656 | tf_op jit(solution)/shard_map/ppermute | solution.py:533
  104.8 21.9 %collective-permute-start.11 = (bf16[256,768]{1,0:T(8,128)(2,1)S(1)}, bf16[256,768]{1,0:T(8,128)(2,1)S(1)}, u32[]{:S(2)}, u32[]{:S(2)}) collective-permute-start(bf16[256,768]{1,0:T(8,128)(2,1)S(1)} %get-tuple-element.57), channel_id=1, source_target_pairs={{4,0},{8,4},{12,8},{16,12},{20,16},{24,20},{28,24},{32,28},{36,32}... | collective-permute-start | bytes 1179656 | tf_op jit(solution)/shard_map/ppermute | solution.py:533
  106.1 27.4 %collective-permute-start.12 = (bf16[256,768]{1,0:T(8,128)(2,1)S(1)}, bf16[256,768]{1,0:T(8,128)(2,1)S(1)}, u32[]{:S(2)}, u32[]{:S(2)}) collective-permute-start(bf16[256,768]{1,0:T(8,128)(2,1)S(1)} %get-tuple-element.58), channel_id=1, source_target_pairs={{0,256},{4,260},{8,264},{12,268},{16,272},{20,276},{24,280},{28,28... | collective-permute-start | bytes 1179656 | tf_op jit(solution)/shard_map/ppermute | solution.py:527
  115.7 24.0 %collective-permute-start.13 = (bf16[256,768]{1,0:T(8,128)(2,1)S(1)}, bf16[256,768]{1,0:T(8,128)(2,1)S(1)}, u32[]{:S(2)}, u32[]{:S(2)}) collective-permute-start(bf16[256,768]{1,0:T(8,128)(2,1)S(1)} %get-tuple-element.59), channel_id=1, source_target_pairs={{0,128},{4,132},{8,136},{12,140},{16,144},{20,148},{24,152},{28,15... | collective-permute-start | bytes 1179656 | tf_op jit(solution)/shard_map/ppermute | solution.py:527

commit v3 on v2

--- a/solution.py
+++ b/solution.py
@@ -130,24 +130,21 @@
     return [range(first, first + GROUP) for first in range(0, PAIRS, GROUP)]
 
 
-def own_slots(key, value):
-    return [(b, key, b * BLK, value, b * BLK) for b in range(BW)]
-
-
-def side_slots(chip, cross):
-    return [
+def own_slots(whole):
+    return [(b, whole, b * BLK, whole, ROWS + b * BLK) for b in range(BW)]
+
+
+def near_slots(chip, cross, left, right):
+    sides = [
         (4 + BW * i + b, ref, b * BLK, ref, ROWS + b * BLK)
         for i, ref in enumerate((chip, cross))
         for b in range(BW)
     ]
+    return pair_slots((2, 3), left, right) + sides
 
 
 def pair_slots(columns, *refs):
     return [(j, ref, 0, ref, BLK) for j, ref in zip(columns, refs)]
-
-
-def rest_slots(left, right, far0, far1):
-    return pair_slots((2, 3, 8, 9), left, right, far0, far1)
 
 
 def rows_at(start):
@@ -195,14 +192,16 @@
     lax.fori_loop(0, count, step, 0)
 
 
-def first_kernel(seen, query, upward, key, value, chip, cross, stat, acc, upward_t, held, place):
+def first_kernel(
+    seen, query, upward, whole, chip, cross, left, right, stat, acc, upward_t, held, place
+):
     for pair in range(PAIRS):
         stat[pair, 0:2, :] = jnp.full((2, ROWS), HIDDEN, f32)
         stat[pair, 2:4, :] = jnp.zeros((2, ROWS), f32)
         acc[pair] = jnp.zeros((BLK, ROWS), f32)
         upward_t[pair] = upward[:, feature(pair)].astype(f32).T
     forward_over(
-        own_slots(key, value) + side_slots(chip, cross), seen, query, stat, acc, held, place
+        own_slots(whole) + near_slots(chip, cross, left, right), seen, query, stat, acc, held, place
     )
 
 
@@ -275,6 +274,8 @@
     far2_term,
     chip_term,
     cross_term,
+    left_term,
+    right_term,
     acc,
     terms,
     held,
@@ -282,7 +283,7 @@
 ):
     stat[...] = stat_in[...]
     acc[...] = acc_in[...]
-    forward_over(rest_slots(left, right, far0, far1), seen, query, stat, acc, held, place)
+    forward_over(pair_slots((8, 9), far0, far1), seen, query, stat, acc, held, place)
 
     for pair in range(PAIRS):
         total = stat[pair, 2:4, :]
@@ -292,10 +293,12 @@
         stat[pair, 2:4, :] = head_reduce(jnp.sum, upward_t[pair] * attended.astype(f32))
 
     query_t[...] = jnp.zeros_like(query_t)
-    targets = pair_slots((10,), far2_term) + side_slots(chip_term, cross_term)
+    targets = pair_slots((10,), far2_term) + near_slots(
+        chip_term, cross_term, left_term, right_term
+    )
     clear_unseen(targets, seen)
     backward_over(
-        pair_slots((10,), far2) + side_slots(chip, cross),
+        pair_slots((10,), far2) + near_slots(chip, cross, left, right),
         seen,
         query,
         upward,
@@ -312,14 +315,13 @@
     seen,
     query,
     upward,
-    key,
-    value,
-    left,
-    right,
+    whole,
     far0,
     far1,
     chip_back,
     cross_back,
+    low_block,
+    high_block,
     stat,
     out_t,
     query_t_in,
@@ -327,8 +329,6 @@
     query_grad,
     key_sum,
     value_sum,
-    left_term,
-    right_term,
     far0_term,
     far1_term,
     query_t,
@@ -339,7 +339,7 @@
     query_t[...] = query_t_in[...]
     for pair in range(PAIRS):
         attention[:, feature(pair)] = out_t[pair].astype(f32).T.astype(bf16)
-    targets = rest_slots(left_term, right_term, far0_term, far1_term)
+    targets = pair_slots((8, 9), far0_term, far1_term)
     clear_unseen(targets, seen)
 
     def store(j):
@@ -349,16 +349,19 @@
             def _():
                 for half, out in enumerate((key_sum, value_sum)):
                     side = slice(half * ROWS + b * BLK, half * ROWS + (b + 1) * BLK)
-                    out[b * BLK : (b + 1) * BLK] = (
-                        terms[half * BLK : (half + 1) * BLK].astype(f32)
-                        + chip_back[side].astype(f32)
-                        + cross_back[side].astype(f32)
-                    )
+                    part = slice(half * BLK, (half + 1) * BLK)
+                    total = terms[part].astype(f32)
+                    total = total + chip_back[side].astype(f32) + cross_back[side].astype(f32)
+                    if b == 0:
+                        total = total + low_block[part].astype(f32)
+                    if b == BW - 1:
+                        total = total + high_block[part].astype(f32)
+                    out[b * BLK : (b + 1) * BLK] = total
 
         store_terms(targets, terms, j)
 
     backward_over(
-        own_slots(key, value) + rest_slots(left, right, far0, far1),
+        own_slots(whole) + pair_slots((8, 9), far0, far1),
         seen,
         query,
         upward,
@@ -381,16 +384,12 @@
             out[rows] = near[rows] + jnp.where(pick[0, 2] == b, far_part, 0.0)
 
 
-def second_sum_kernel(pick, key_sum, value_sum, low_block, high_block, far0, far1, key_grad, value_grad):
+def second_sum_kernel(pick, key_sum, value_sum, far0, far1, key_grad, value_grad):
     for half, (near, out) in enumerate(((key_sum, key_grad), (value_sum, value_grad))):
         part = slice(half * BLK, (half + 1) * BLK)
         for b in range(BW):
             rows = slice(b * BLK, (b + 1) * BLK)
             total = near[rows]
-            if b == 0:
-                total = total + low_block[part].astype(f32)
-            if b == BW - 1:
-                total = total + high_block[part].astype(f32)
             for slot, far in enumerate((far0, far1)):
                 total = total + jnp.where(pick[0, slot] == b, far[part].astype(f32), 0.0)
             out[rows] = total.astype(bf16)
@@ -421,35 +420,44 @@
 SIDE = shape((2 * ROWS, D), bf16)
 
 
-def block_of(key, value, start, out):
-    rows = pl.ds(pl.multiple_of(start, BLK), BLK)
-    out[0:BLK] = key[rows]
-    out[BLK : 2 * BLK] = value[rows]
-
-
-def pack_first_kernel(pick, key, value, far2, whole):
-    block_of(key, value, pick[0, 2] * BLK, far2)
-    whole[0:ROWS] = key[...]
-    whole[ROWS : 2 * ROWS] = value[...]
-
-
-def pack_rest_kernel(pick, chip, cross, key, value, right, left, far0, far1):
-    block_of(key, value, 0, right)
-    block_of(key, value, ROWS - BLK, left)
-    block_of(key, value, pick[0, 0] * BLK, far0)
-    block_of(key, value, pick[0, 1] * BLK, far1)
+def block_of(whole, start, out):
+    for half in range(2):
+        rows = pl.ds(pl.multiple_of(half * ROWS + start, BLK), BLK)
+        out[half * BLK : (half + 1) * BLK] = whole[rows]
+
+
+def pack_first_kernel(pick, key, value, whole, right, left, far2, sems):
+    copies = [
+        pltpu.make_async_copy(ref, whole.at[pl.ds(half * ROWS, ROWS)], sems.at[half])
+        for half, ref in enumerate((key, value))
+    ]
+    for one in copies:
+        one.start()
+    for one in copies:
+        one.wait()
+    block_of(whole, 0, right)
+    block_of(whole, ROWS - BLK, left)
+    block_of(whole, pick[0, 2] * BLK, far2)
+
+
+def pack_rest_kernel(pick, chip, cross, left, right, whole, far0, far1):
+    block_of(whole, pick[0, 0] * BLK, far0)
+    block_of(whole, pick[0, 1] * BLK, far1)
 
 
 def pack_first(pick, key, value):
-    return call(pack_first_kernel, [RIM, SIDE], [smem(), vmem(), vmem()], (pick, key, value))
-
-
-def pack_rest(pick, chip, cross, key, value):
     return call(
-        pack_rest_kernel,
-        [RIM] * 4,
-        [smem(), hbm(), hbm(), vmem(), vmem()],
-        (pick, chip, cross, key, value),
+        pack_first_kernel,
+        [SIDE, RIM, RIM, RIM],
+        [smem(), hbm(), hbm()],
+        (pick, key, value),
+        scratch=[pltpu.SemaphoreType.DMA((2,))],
+    )
+
+
+def pack_rest(pick, *rest):
+    return call(
+        pack_rest_kernel, [RIM] * 2, [smem()] + [hbm()] * 4 + [vmem()], (pick, *rest)
     )
 
 
@@ -457,13 +465,13 @@
     return [pltpu.VMEM((slots, 2 * BLK, D), bf16), pltpu.SMEM((16,), jnp.int32)]
 
 
-def run_first(plan, queries, upstream, *near):
+def run_first(plan, *rest):
     return call(
         first_kernel,
         STATE + [shape((PAIRS, BLK, ROWS), f32)],
-        [smem()] + [vmem()] * 6,
-        (plan, queries, upstream, *near),
-        scratch=seen_scratch(6),
+        [smem()] + [vmem()] * 7,
+        (plan, *rest),
+        scratch=seen_scratch(8),
     )
 
 
@@ -480,11 +488,11 @@
 def run_middle(far2, plan, *rest):
     return call(
         middle_kernel,
-        [STATE[0], shape((PAIRS, BLK, ROWS), bf16), STATE[1], RIM, SIDE, SIDE],
+        [STATE[0], shape((PAIRS, BLK, ROWS), bf16), STATE[1], RIM, SIDE, SIDE, RIM, RIM],
         [vmem(), smem()] + [vmem()] * 11,
         (far2, plan, *rest),
         scratch=[pltpu.VMEM((PAIRS, BLK, ROWS), f32), pltpu.VMEM((2 * BLK, D), bf16)]
-        + seen_scratch(5),
+        + seen_scratch(7),
     )
 
 
@@ -493,11 +501,11 @@
     total = shape((ROWS, D), f32)
     return call(
         backward_kernel,
-        [whole, whole, total, total] + [RIM] * 4,
-        [smem()] + [vmem()] * 13,
+        [whole, whole, total, total, RIM, RIM],
+        [smem()] + [vmem()] * 12,
         (plan, *rest),
         scratch=[pltpu.VMEM((PAIRS, BLK, ROWS), f32), pltpu.VMEM((2 * BLK, D), bf16)]
-        + seen_scratch(6),
+        + seen_scratch(4),
     )
 
 
@@ -510,7 +518,7 @@
 
 def run_second_sum(pick, *rest):
     whole = shape((ROWS, D), bf16)
-    return call(second_sum_kernel, [whole, whole], [smem()] + [vmem()] * 6, (pick, *rest))
+    return call(second_sum_kernel, [whole, whole], [smem()] + [vmem()] * 4, (pick, *rest))
 
 
 def sides(chip, cross):
@@ -556,45 +564,35 @@
         axis=1,
     )
 
-    far2_pair, whole = pack_first(expander_pick, key_rows, value_rows)
-    chip, cross = sides(whole, whole)
+    whole, right_pair, left_pair, far2_pair = pack_first(expander_pick, key_rows, value_rows)
+    near = (*sides(whole, whole), shift(left_pair, "wide", 1), shift(right_pair, "wide", -1))
     far2 = partner(far2_pair, top_bit - EXP)
-    right_pair, left_pair, far0_pair, far1_pair = pack_rest(
-        expander_pick, chip, cross, key_rows, value_rows
-    )
-    rest = (
-        shift(left_pair, "wide", 1),
-        shift(right_pair, "wide", -1),
-        partner(far0_pair, top_bit - 1),
-        partner(far1_pair, top_bit - 2),
-    )
-    stat, acc, upward_t = run_first(plan, queries, upstream, key_rows, value_rows, chip, cross)
+    far0_pair, far1_pair = pack_rest(expander_pick, *near, whole)
+    far = (partner(far0_pair, top_bit - 1), partner(far1_pair, top_bit - 2))
+    stat, acc, upward_t = run_first(plan, queries, upstream, whole, *near)
     stat, acc = run_far(far2, plan, queries, stat, acc)
-    stat, out_t, query_t, far2_term, chip_term, cross_term = run_middle(
-        far2, plan, queries, upstream, chip, cross, *rest, stat, acc, upward_t
+    stat, out_t, query_t, far2_term, chip_term, cross_term, left_term, right_term = run_middle(
+        far2, plan, queries, upstream, *near, *far, stat, acc, upward_t
     )
     far2_back = partner(far2_term, top_bit - EXP)
-    attention, query_grad, key_near, value_near, left_term, right_term, far0_term, far1_term = (
-        run_backward(
-            plan,
-            queries,
-            upstream,
-            key_rows,
-            value_rows,
-            *rest,
-            *sides(chip_term, cross_term),
-            stat,
-            out_t,
-            query_t,
-        )
+    attention, query_grad, key_near, value_near, far0_term, far1_term = run_backward(
+        plan,
+        queries,
+        upstream,
+        whole,
+        *far,
+        *sides(chip_term, cross_term),
+        shift(right_term, "wide", 1),
+        shift(left_term, "wide", -1),
+        stat,
+        out_t,
+        query_t,
     )
     key_sum, value_sum = run_first_sum(far2_back, expander_pick, key_near, value_near)
     key_grad, value_grad = run_second_sum(
         expander_pick,
         key_sum,
         value_sum,
-        shift(right_term, "wide", 1),
-        shift(left_term, "wide", -1),
         partner(far0_term, top_bit - 1),
         partner(far1_term, top_bit - 2),
     )

time: 142 us -> 173 us (1.22)
  the two profiles are of different devices: /device:TPU:1 before, /device:TPU:25 now
where the time goes in v3:
time: 173 us; the launch traced here: 170 us
  starting transfers between devices  79.1 us (46%)
  waiting for transfers between devices  56.9 us (33%)
  Pallas kernels  27.2 us (16%)
  local copies, waits for them, and re-layouts  5.37 us (3%)
    ppermute x6, starting transfers between devices, partner(): lax.ppermute(value, 'wide', [(s, s ^ mask) for s in range(lax.axis_size('...  37.2 us
    ppermute x6, waiting for transfers between devices, partner(): lax.ppermute(value, 'wide', [(s, s ^ mask) for s in range(lax.axis_size('...  34.6 us
    ppermute x4, starting transfers between devices, shift(): return lax.ppermute(value, axis, pairs)  31 us
    pallas_call x8, Pallas kernels, call(): pl.pallas_call(kernel, out_shape=shapes, in_specs=specs, out_specs=outs i...  27.2 us
    ppermute x4, waiting for transfers between devices, shift(): return lax.ppermute(value, axis, pairs)  22.2 us
    ppermute x2, starting transfers between devices, sides(): lax.ppermute(cross, 'narrow', across + [(b, a) for a, b in across])  5.6 us
    ppermute x2, starting transfers between devices, sides(): lax.ppermute(chip, 'narrow', [(i, i ^ 1) for i in range(count)])  5.29 us
    unnamed x14, local copies, waits for them, and re-layouts  3.93 us
  transfers between devices with their start and end apart: 14, of which 4 were waited for; matrix products, arithmetic and copies ran while one was open for 1% of the time, Pallas kernels for 9%

profile of v3, /device:TPU:25, one launch (start us, length us, event | category | flops | bytes accessed | tf_op | source)
XLA Modules:
  0.0 170.2 jit_solution(9558016841476894510)
XLA Ops:
  3.3 2.0 %shard_map.93 = (bf16[512,768]{1,0:T(8,128)(2,1)S(1)}, bf16[256,768]{1,0:T(8,128)(2,1)}, bf16[256,768]{1,0:T(8,128)(2,1)}, bf16[256,768]{1,0:T(8,128)(2,1)}) custom-call(s32[1,3]{1,0:T(1,128)S(1)} %copy-done.4, bf16[256,768]{1,0:T(8,128)(2,1)S(1)} %copy-done.2, bf16[256,768]{1,0:T(8,128)(2,1)S(1)} %copy-done.3), custom_call_target="tpu_custom_call" | custom-call | tf_op jit(solution)/shard_map/pallas_call | solution.py:399
  5.3 3.7 %collective-permute-start.1 = (bf16[512,768]{1,0:T(8,128)(2,1)S(1)}, bf16[512,768]{1,0:T(8,128)(2,1)S(1)}, u32[]{:S(2)}, u32[]{:S(2)}) collective-permute-start(bf16[512,768]{1,0:T(8,128)(2,1)S(1)} %get-tuple-element.33.whole), channel_id=1, source_target_pairs={{1,2},{2,1},{5,6},{6,5},{9,10},{10,9},{13,14},{14,13},{17,18},{18,... | collective-permute-start | bytes 2359304 | tf_op jit(solution)/shard_map/ppermute | solution.py:529
  9.0 1.9 %collective-permute-start = (bf16[512,768]{1,0:T(8,128)(2,1)S(1)}, bf16[512,768]{1,0:T(8,128)(2,1)S(1)}, u32[]{:S(2)}, u32[]{:S(2)}) collective-permute-start(bf16[512,768]{1,0:T(8,128)(2,1)S(1)} %get-tuple-element.33.whole), channel_id=1, source_target_pairs={{0,1},{1,0},{2,3},{3,2},{4,5},{5,4},{6,7},{7,6},{8,9},{9,8},{10,11... | collective-permute-start | bytes 2359304 | tf_op jit(solution)/shard_map/ppermute | solution.py:528
  10.9 4.4 %collective-permute-start.2 = (bf16[256,768]{1,0:T(8,128)(2,1)}, bf16[256,768]{1,0:T(8,128)(2,1)S(1)}, u32[]{:S(2)}, u32[]{:S(2)}) collective-permute-start(bf16[256,768]{1,0:T(8,128)(2,1)} %get-tuple-element.34), channel_id=1, source_target_pairs={{0,4},{4,8},{8,12},{12,16},{16,20},{20,24},{24,28},{28,32},{32,36}... | collective-permute-start | bytes 1179656 | tf_op jit(solution)/shard_map/ppermute | solution.py:541
  15.3 11.0 %collective-permute-start.3 = (bf16[256,768]{1,0:T(8,128)(2,1)}, bf16[256,768]{1,0:T(8,128)(2,1)}, u32[]{:S(2)}, u32[]{:S(2)}) collective-permute-start(bf16[256,768]{1,0:T(8,128)(2,1)} %get-tuple-element.35), channel_id=1, source_target_pairs={{4,0},{8,4},{12,8},{16,12},{20,16},{24,20},{28,24},{32,28},{36,32}... | collective-permute-start | bytes 1179656 | tf_op jit(solution)/shard_map/ppermute | solution.py:541
  26.3 9.0 %collective-permute-start.6 = (bf16[256,768]{1,0:T(8,128)(2,1)}, bf16[256,768]{1,0:T(8,128)(2,1)}, u32[]{:S(2)}, u32[]{:S(2)}) collective-permute-start(bf16[256,768]{1,0:T(8,128)(2,1)} %get-tuple-element.38), channel_id=1, source_target_pairs={{0,64},{4,68},{8,72},{12,76},{16,80},{20,84},{24,88},{28,92},{32,9... | collective-permute-start | bytes 1179656 | tf_op jit(solution)/shard_map/ppermute | solution.py:535
  37.3 1.5 shard_map.94
  38.8 2.9 %collective-permute-start.4 = (bf16[256,768]{1,0:T(8,128)(2,1)}, bf16[256,768]{1,0:T(8,128)(2,1)}, u32[]{:S(2)}, u32[]{:S(2)}) collective-permute-start(bf16[256,768]{1,0:T(8,128)(2,1)} %get-tuple-element.36), channel_id=1, source_target_pairs={{0,256},{4,260},{8,264},{12,268},{16,272},{20,276},{24,280},{28,28... | collective-permute-start | bytes 1179656 | tf_op jit(solution)/shard_map/ppermute | solution.py:535
  41.6 1.9 %collective-permute-start.5 = (bf16[256,768]{1,0:T(8,128)(2,1)}, bf16[256,768]{1,0:T(8,128)(2,1)}, u32[]{:S(2)}, u32[]{:S(2)}) collective-permute-start(bf16[256,768]{1,0:T(8,128)(2,1)} %get-tuple-element.37), channel_id=1, source_target_pairs={{0,128},{4,132},{8,136},{12,140},{16,144},{20,148},{24,152},{28,15... | collective-permute-start | bytes 1179656 | tf_op jit(solution)/shard_map/ppermute | solution.py:535
  45.1 6.3 %shard_map.95 = (f32[6,8,256]{2,1,0:T(8,128)S(1)}, f32[6,128,256]{2,1,0:T(8,128)S(1)}, f32[6,128,256]{2,1,0:T(8,128)S(1)}) custom-call(s32[2,11]{1,0:T(2,128)S(1)} %concatenate.3.seen, bf16[256,768]{1,0:T(8,128)(2,1)S(1)} %copy-done, bf16[256,768]{1,0:T(8,128)(2,1)S(1)} %copy-done.1, bf16[512,768]{1,0:T(8,128)(2,1)S(1)} %get-tuple-element.33.whole, ...), custom_call_target="tpu_custom_call" | custom-call | tf_op jit(solution)/shard_map/pallas_call | solution.py:399
  51.4 20.8 %collective-permute-done.6.far2 = bf16[256,768]{1,0:T(8,128)(2,1)} collective-permute-done((bf16[256,768]{1,0:T(8,128)(2,1)}, bf16[256,768]{1,0:T(8,128)(2,1)}, u32[]{:S(2)}, u32[]{:S(2)}) %collective-permute-start.6) | collective-permute-done | bytes 393248 | tf_op jit(solution)/shard_map/ppermute | solution.py:535
  73.2 7.7 %shard_map.97 = (f32[6,8,256]{2,1,0:T(8,128)S(1)}, bf16[6,128,256]{2,1,0:T(8,128)(2,1)S(1)}, f32[6,128,256]{2,1,0:T(8,128)S(1)}, bf16[256,768]{1,0:T(8,128)(2,1)...) custom-call(bf16[256,768]{1,0:T(8,128)(2,1)} %collective-permute-don, ...), custom_call_target="tpu_custom_call" | custom-call | tf_op jit(solution)/shard_map/pallas_call | solution.py:399
  80.9 3.4 %collective-permute-start.7 = (bf16[512,768]{1,0:T(8,128)(2,1)S(1)}, bf16[512,768]{1,0:T(8,128)(2,1)S(1)}, u32[]{:S(2)}, u32[]{:S(2)}) collective-permute-start(bf16[512,768]{1,0:T(8,128)(2,1)S(1)} %get-tuple-element.44), channel_id=1, source_target_pairs={{0,1},{1,0},{2,3},{3,2},{4,5},{5,4},{6,7},{7,6},{8,9},{9,8},{10,11... | collective-permute-start | bytes 2359304 | tf_op jit(solution)/shard_map/ppermute | solution.py:528
  84.3 1.9 %collective-permute-start.8 = (bf16[512,768]{1,0:T(8,128)(2,1)S(1)}, bf16[512,768]{1,0:T(8,128)(2,1)S(1)}, u32[]{:S(2)}, u32[]{:S(2)}) collective-permute-start(bf16[512,768]{1,0:T(8,128)(2,1)S(1)} %get-tuple-element.45), channel_id=1, source_target_pairs={{1,2},{2,1},{5,6},{6,5},{9,10},{10,9},{13,14},{14,13},{17,18},{18,... | collective-permute-start | bytes 2359304 | tf_op jit(solution)/shard_map/ppermute | solution.py:529
  86.3 1.9 %collective-permute-start.9 = (bf16[256,768]{1,0:T(8,128)(2,1)S(1)}, bf16[256,768]{1,0:T(8,128)(2,1)S(1)}, u32[]{:S(2)}, u32[]{:S(2)}) collective-permute-start(bf16[256,768]{1,0:T(8,128)(2,1)S(1)} %get-tuple-element.46), channel_id=1, source_target_pairs={{0,4},{4,8},{8,12},{12,16},{16,20},{20,24},{24,28},{28,32},{32,36}... | collective-permute-start | bytes 1179656 | tf_op jit(solution)/shard_map/ppermute | solution.py:541
  88.2 13.7 %collective-permute-start.10 = (bf16[256,768]{1,0:T(8,128)(2,1)S(1)}, bf16[256,768]{1,0:T(8,128)(2,1)S(1)}, u32[]{:S(2)}, u32[]{:S(2)}) collective-permute-start(bf16[256,768]{1,0:T(8,128)(2,1)S(1)} %get-tuple-element.47), channel_id=1, source_target_pairs={{4,0},{8,4},{12,8},{16,12},{20,16},{24,20},{28,24},{32,28},{36,32}... | collective-permute-start | bytes 1179656 | tf_op jit(solution)/shard_map/ppermute | solution.py:541
  101.9 16.8 %collective-permute-start.11 = (bf16[256,768]{1,0:T(8,128)(2,1)S(1)}, bf16[256,768]{1,0:T(8,128)(2,1)S(1)}, u32[]{:S(2)}, u32[]{:S(2)}) collective-permute-start(bf16[256,768]{1,0:T(8,128)(2,1)S(1)} %get-tuple-element.53), channel_id=1, source_target_pairs={{0,64},{4,68},{8,72},{12,76},{16,80},{20,84},{24,88},{28,92},{32,9... | collective-permute-start | bytes 1179656 | tf_op jit(solution)/shard_map/ppermute | solution.py:535
  118.7 22.2 %collective-permute-done.9.low_block = bf16[256,768]{1,0:T(8,128)(2,1)S(1)} collective-permute-done((bf16[256,768]{1,0:T(8,128)(2,1)S(1)}, bf16[256,768]{1,0:T(8,128)(2,1)S(1)}, u32[]{:S(2)}, u32[]{:S(2)}) %collective-permute-start.9) | collective-permute-done | bytes 393248 | tf_op jit(solution)/shard_map/ppermute | solution.py:541
  141.0 6.3 %shard_map.98 = (bf16[256,768]{1,0:T(8,128)(2,1)}, bf16[256,768]{1,0:T(8,128)(2,1)}, f32[256,768]{1,0:T(8,128)S(1)}, f32[256,768]{1,0:T(8,128)S(1)}, bf16[256,76...) custom-call(s32[2,11]{1,0:T(2,128)S(1)} %concatenate.3.seen, bf16[256,768]{1,0:T(8,128)(2,1)S(1)} %copy-done, ...), custom_call_target="tpu_custom_call" | custom-call | tf_op jit(solution)/shard_map/pallas_call | solution.py:399
  147.3 4.7 %collective-permute-start.12 = (bf16[256,768]{1,0:T(8,128)(2,1)S(1)}, bf16[256,768]{1,0:T(8,128)(2,1)S(1)}, u32[]{:S(2)}, u32[]{:S(2)}) collective-permute-start(bf16[256,768]{1,0:T(8,128)(2,1)S(1)} %get-tuple-element.58), channel_id=1, source_target_pairs={{0,256},{4,260},{8,264},{12,268},{16,272},{20,276},{24,280},{28,28... | collective-permute-start | bytes 1179656 | tf_op jit(solution)/shard_map/ppermute | solution.py:535
  152.0 1.9 %collective-permute-start.13 = (bf16[256,768]{1,0:T(8,128)(2,1)S(1)}, bf16[256,768]{1,0:T(8,128)(2,1)S(1)}, u32[]{:S(2)}, u32[]{:S(2)}) collective-permute-start(bf16[256,768]{1,0:T(8,128)(2,1)S(1)} %get-tuple-element.59), channel_id=1, source_target_pairs={{0,128},{4,132},{8,136},{12,140},{16,144},{20,148},{24,152},{28,15... | collective-permute-start | bytes 1179656 | tf_op jit(solution)/shard_map/ppermute | solution.py:535
  154.7 5.4 %collective-permute-done.12.far0 = bf16[256,768]{1,0:T(8,128)(2,1)S(1)} collective-permute-done((bf16[256,768]{1,0:T(8,128)(2,1)S(1)}, bf16[256,768]{1,0:T(8,128)(2,1)S(1)}, u32[]{:S(2)}, u32[]{:S(2)}) %collective-permute-start.12) | collective-permute-done | bytes 393248 | tf_op jit(solution)/shard_map/ppermute | solution.py:535
  160.1 8.4 %collective-permute-done.13.far1 = bf16[256,768]{1,0:T(8,128)(2,1)S(1)} collective-permute-done((bf16[256,768]{1,0:T(8,128)(2,1)S(1)}, bf16[256,768]{1,0:T(8,128)(2,1)S(1)}, u32[]{:S(2)}, u32[]{:S(2)}) %collective-permute-start.13) | collective-permute-done | bytes 393248 | tf_op jit(solution)/shard_map/ppermute | solution.py:535
  168.5 1.7 shard_map.100
  (30 shorter events, 7.9 us)
Async XLA Ops:
  0.6 1.0 copy-start.2
  1.6 1.0 copy-start.3
  2.6 0.7 copy-start.4
  5.3 31.4 %collective-permute-start.1 = (bf16[512,768]{1,0:T(8,128)(2,1)S(1)}, bf16[512,768]{1,0:T(8,128)(2,1)S(1)}, u32[]{:S(2)}, u32[]{:S(2)}) collective-permute-start(bf16[512,768]{1,0:T(8,128)(2,1)S(1)} %get-tuple-element.33.whole), channel_id=1, source_target_pairs={{1,2},{2,1},{5,6},{6,5},{9,10},{10,9},{13,14},{14,13},{17,18},{18,... | collective-permute-start | bytes 2359304 | tf_op jit(solution)/shard_map/ppermute | solution.py:529
  9.0 27.7 %collective-permute-start = (bf16[512,768]{1,0:T(8,128)(2,1)S(1)}, bf16[512,768]{1,0:T(8,128)(2,1)S(1)}, u32[]{:S(2)}, u32[]{:S(2)}) collective-permute-start(bf16[512,768]{1,0:T(8,128)(2,1)S(1)} %get-tuple-element.33.whole), channel_id=1, source_target_pairs={{0,1},{1,0},{2,3},{3,2},{4,5},{5,4},{6,7},{7,6},{8,9},{9,8},{10,11... | collective-permute-start | bytes 2359304 | tf_op jit(solution)/shard_map/ppermute | solution.py:528
  10.9 25.7 %collective-permute-start.2 = (bf16[256,768]{1,0:T(8,128)(2,1)}, bf16[256,768]{1,0:T(8,128)(2,1)S(1)}, u32[]{:S(2)}, u32[]{:S(2)}) collective-permute-start(bf16[256,768]{1,0:T(8,128)(2,1)} %get-tuple-element.34), channel_id=1, source_target_pairs={{0,4},{4,8},{8,12},{12,16},{16,20},{20,24},{24,28},{28,32},{32,36}... | collective-permute-start | bytes 1179656 | tf_op jit(solution)/shard_map/ppermute | solution.py:541
  15.3 21.4 %collective-permute-start.3 = (bf16[256,768]{1,0:T(8,128)(2,1)}, bf16[256,768]{1,0:T(8,128)(2,1)}, u32[]{:S(2)}, u32[]{:S(2)}) collective-permute-start(bf16[256,768]{1,0:T(8,128)(2,1)} %get-tuple-element.35), channel_id=1, source_target_pairs={{4,0},{8,4},{12,8},{16,12},{20,16},{24,20},{28,24},{32,28},{36,32}... | collective-permute-start | bytes 1179656 | tf_op jit(solution)/shard_map/ppermute | solution.py:541
  26.3 45.8 %collective-permute-start.6 = (bf16[256,768]{1,0:T(8,128)(2,1)}, bf16[256,768]{1,0:T(8,128)(2,1)}, u32[]{:S(2)}, u32[]{:S(2)}) collective-permute-start(bf16[256,768]{1,0:T(8,128)(2,1)} %get-tuple-element.38), channel_id=1, source_target_pairs={{0,64},{4,68},{8,72},{12,76},{16,80},{20,84},{24,88},{28,92},{32,9... | collective-permute-start | bytes 1179656 | tf_op jit(solution)/shard_map/ppermute | solution.py:535
  35.3 0.7 copy-start.6
  36.6 0.7 copy-start.5
  36.6 8.4 %copy-start = (bf16[256,768]{1,0:T(8,128)(2,1)S(1)}, bf16[256,768]{1,0:T(8,128)(2,1)}, u32[]{:S(2)}) copy-start(bf16[256,768]{1,0:T(8,128)(2,1)} %query.7) | copy-start | bytes 1179652
  36.6 8.4 %copy-start.1 = (bf16[256,768]{1,0:T(8,128)(2,1)S(1)}, bf16[256,768]{1,0:T(8,128)(2,1)}, u32[]{:S(2)}) copy-start(bf16[256,768]{1,0:T(8,128)(2,1)} %upward.5) | copy-start | bytes 1179652
  38.8 34.4 %collective-permute-start.4 = (bf16[256,768]{1,0:T(8,128)(2,1)}, bf16[256,768]{1,0:T(8,128)(2,1)}, u32[]{:S(2)}, u32[]{:S(2)}) collective-permute-start(bf16[256,768]{1,0:T(8,128)(2,1)} %get-tuple-element.36), channel_id=1, source_target_pairs={{0,256},{4,260},{8,264},{12,268},{16,272},{20,276},{24,280},{28,28... | collective-permute-start | bytes 1179656 | tf_op jit(solution)/shard_map/ppermute | solution.py:535
  41.6 31.6 %collective-permute-start.5 = (bf16[256,768]{1,0:T(8,128)(2,1)}, bf16[256,768]{1,0:T(8,128)(2,1)}, u32[]{:S(2)}, u32[]{:S(2)}) collective-permute-start(bf16[256,768]{1,0:T(8,128)(2,1)} %get-tuple-element.37), channel_id=1, source_target_pairs={{0,128},{4,132},{8,136},{12,140},{16,144},{20,148},{24,152},{28,15... | collective-permute-start | bytes 1179656 | tf_op jit(solution)/shard_map/ppermute | solution.py:535
  80.9 60.0 %collective-permute-start.7 = (bf16[512,768]{1,0:T(8,128)(2,1)S(1)}, bf16[512,768]{1,0:T(8,128)(2,1)S(1)}, u32[]{:S(2)}, u32[]{:S(2)}) collective-permute-start(bf16[512,768]{1,0:T(8,128)(2,1)S(1)} %get-tuple-element.44), channel_id=1, source_target_pairs={{0,1},{1,0},{2,3},{3,2},{4,5},{5,4},{6,7},{7,6},{8,9},{9,8},{10,11... | collective-permute-start | bytes 2359304 | tf_op jit(solution)/shard_map/ppermute | solution.py:528
  84.3 56.7 %collective-permute-start.8 = (bf16[512,768]{1,0:T(8,128)(2,1)S(1)}, bf16[512,768]{1,0:T(8,128)(2,1)S(1)}, u32[]{:S(2)}, u32[]{:S(2)}) collective-permute-start(bf16[512,768]{1,0:T(8,128)(2,1)S(1)} %get-tuple-element.45), channel_id=1, source_target_pairs={{1,2},{2,1},{5,6},{6,5},{9,10},{10,9},{13,14},{14,13},{17,18},{18,... | collective-permute-start | bytes 2359304 | tf_op jit(solution)/shard_map/ppermute | solution.py:529
  86.3 54.7 %collective-permute-start.9 = (bf16[256,768]{1,0:T(8,128)(2,1)S(1)}, bf16[256,768]{1,0:T(8,128)(2,1)S(1)}, u32[]{:S(2)}, u32[]{:S(2)}) collective-permute-start(bf16[256,768]{1,0:T(8,128)(2,1)S(1)} %get-tuple-element.46), channel_id=1, source_target_pairs={{0,4},{4,8},{8,12},{12,16},{16,20},{20,24},{24,28},{28,32},{32,36}... | collective-permute-start | bytes 1179656 | tf_op jit(solution)/shard_map/ppermute | solution.py:541
  88.2 52.8 %collective-permute-start.10 = (bf16[256,768]{1,0:T(8,128)(2,1)S(1)}, bf16[256,768]{1,0:T(8,128)(2,1)S(1)}, u32[]{:S(2)}, u32[]{:S(2)}) collective-permute-start(bf16[256,768]{1,0:T(8,128)(2,1)S(1)} %get-tuple-element.47), channel_id=1, source_target_pairs={{4,0},{8,4},{12,8},{16,12},{20,16},{24,20},{28,24},{32,28},{36,32}... | collective-permute-start | bytes 1179656 | tf_op jit(solution)/shard_map/ppermute | solution.py:541
  101.9 52.1 %collective-permute-start.11 = (bf16[256,768]{1,0:T(8,128)(2,1)S(1)}, bf16[256,768]{1,0:T(8,128)(2,1)S(1)}, u32[]{:S(2)}, u32[]{:S(2)}) collective-permute-start(bf16[256,768]{1,0:T(8,128)(2,1)S(1)} %get-tuple-element.53), channel_id=1, source_target_pairs={{0,64},{4,68},{8,72},{12,76},{16,80},{20,84},{24,88},{28,92},{32,9... | collective-permute-start | bytes 1179656 | tf_op jit(solution)/shard_map/ppermute | solution.py:535
  147.3 12.8 %collective-permute-start.12 = (bf16[256,768]{1,0:T(8,128)(2,1)S(1)}, bf16[256,768]{1,0:T(8,128)(2,1)S(1)}, u32[]{:S(2)}, u32[]{:S(2)}) collective-permute-start(bf16[256,768]{1,0:T(8,128)(2,1)S(1)} %get-tuple-element.58), channel_id=1, source_target_pairs={{0,256},{4,260},{8,264},{12,268},{16,272},{20,276},{24,280},{28,28... | collective-permute-start | bytes 1179656 | tf_op jit(solution)/shard_map/ppermute | solution.py:535
  152.0 16.5 %collective-permute-start.13 = (bf16[256,768]{1,0:T(8,128)(2,1)S(1)}, bf16[256,768]{1,0:T(8,128)(2,1)S(1)}, u32[]{:S(2)}, u32[]{:S(2)}) collective-permute-start(bf16[256,768]{1,0:T(8,128)(2,1)S(1)} %get-tuple-element.59), channel_id=1, source_target_pairs={{0,128},{4,132},{8,136},{12,140},{16,144},{20,148},{24,152},{28,15... | collective-permute-start | bytes 1179656 | tf_op jit(solution)/shard_map/ppermute | solution.py:535

commit v4 on v2

--- a/solution.py
+++ b/solution.py
@@ -308,12 +308,10 @@
     )
 
 
-def backward_kernel(
+def rest_kernel(
     seen,
     query,
     upward,
-    key,
-    value,
     left,
     right,
     far0,
@@ -321,12 +319,7 @@
     chip_back,
     cross_back,
     stat,
-    out_t,
     query_t_in,
-    attention,
-    query_grad,
-    key_sum,
-    value_sum,
     left_term,
     right_term,
     far0_term,
@@ -337,10 +330,45 @@
     place,
 ):
     query_t[...] = query_t_in[...]
+    targets = rest_slots(left_term, right_term, far0_term, far1_term)
+    clear_unseen(targets, seen)
+    backward_over(
+        rest_slots(left, right, far0, far1),
+        seen,
+        query,
+        upward,
+        stat,
+        query_t,
+        held,
+        place,
+        terms,
+        lambda j: store_terms(targets, terms, j),
+    )
+
+
+def own_kernel(
+    seen,
+    query,
+    upward,
+    key,
+    value,
+    chip_back,
+    cross_back,
+    stat,
+    out_t,
+    query_t_in,
+    attention,
+    query_grad,
+    key_sum,
+    value_sum,
+    query_t,
+    terms,
+    held,
+    place,
+):
+    query_t[...] = query_t_in[...]
     for pair in range(PAIRS):
         attention[:, feature(pair)] = out_t[pair].astype(f32).T.astype(bf16)
-    targets = rest_slots(left_term, right_term, far0_term, far1_term)
-    clear_unseen(targets, seen)
 
     def store(j):
         for b in range(BW):
@@ -355,19 +383,8 @@
                         + cross_back[side].astype(f32)
                     )
 
-        store_terms(targets, terms, j)
-
     backward_over(
-        own_slots(key, value) + rest_slots(left, right, far0, far1),
-        seen,
-        query,
-        upward,
-        stat,
-        query_t,
-        held,
-        place,
-        terms,
-        store,
+        own_slots(key, value), seen, query, upward, stat, query_t, held, place, terms, store
     )
     for pair in range(PAIRS):
         query_grad[:, feature(pair)] = (query_t[pair] * SCALE).T.astype(bf16)
@@ -381,7 +398,7 @@
             out[rows] = near[rows] + jnp.where(pick[0, 2] == b, far_part, 0.0)
 
 
-def second_sum_kernel(pick, key_sum, value_sum, low_block, high_block, far0, far1, key_grad, value_grad):
+def second_sum_kernel(pick, key_sum, value_sum, far0, far1, low_block, high_block, key_grad, value_grad):
     for half, (near, out) in enumerate(((key_sum, key_grad), (value_sum, value_grad))):
         part = slice(half * BLK, (half + 1) * BLK)
         for b in range(BW):
@@ -488,16 +505,26 @@
     )
 
 
-def run_backward(plan, *rest):
+def run_rest(plan, *rest):
+    return call(
+        rest_kernel,
+        [RIM] * 4 + [STATE[1]],
+        [smem()] + [vmem()] * 6 + [hbm()] * 2 + [vmem()] * 2,
+        (plan, *rest),
+        scratch=[pltpu.VMEM((2 * BLK, D), bf16)] + seen_scratch(4),
+    )
+
+
+def run_own(plan, *rest):
     whole = shape((ROWS, D), bf16)
     total = shape((ROWS, D), f32)
     return call(
-        backward_kernel,
-        [whole, whole, total, total] + [RIM] * 4,
-        [smem()] + [vmem()] * 13,
+        own_kernel,
+        [whole, whole, total, total],
+        [smem()] + [vmem()] * 9,
         (plan, *rest),
         scratch=[pltpu.VMEM((PAIRS, BLK, ROWS), f32), pltpu.VMEM((2 * BLK, D), bf16)]
-        + seen_scratch(6),
+        + seen_scratch(2),
     )
 
 
@@ -574,29 +601,22 @@
         far2, plan, queries, upstream, chip, cross, *rest, stat, acc, upward_t
     )
     far2_back = partner(far2_term, top_bit - EXP)
-    attention, query_grad, key_near, value_near, left_term, right_term, far0_term, far1_term = (
-        run_backward(
-            plan,
-            queries,
-            upstream,
-            key_rows,
-            value_rows,
-            *rest,
-            *sides(chip_term, cross_term),
-            stat,
-            out_t,
-            query_t,
-        )
+    back = sides(chip_term, cross_term)
+    left_term, right_term, far0_term, far1_term, query_t = run_rest(
+        plan, queries, upstream, *rest, *back, stat, query_t
+    )
+    attention, query_grad, key_near, value_near = run_own(
+        plan, queries, upstream, key_rows, value_rows, *back, stat, out_t, query_t
     )
     key_sum, value_sum = run_first_sum(far2_back, expander_pick, key_near, value_near)
     key_grad, value_grad = run_second_sum(
         expander_pick,
         key_sum,
         value_sum,
+        partner(far0_term, top_bit - 1),
+        partner(far1_term, top_bit - 2),
         shift(right_term, "wide", 1),
         shift(left_term, "wide", -1),
-        partner(far0_term, top_bit - 1),
-        partner(far1_term, top_bit - 2),
     )
     return (attention, query_grad, key_grad, value_grad)
 

time: 142 us -> 135 us (0.951)
  the two profiles are of different devices: /device:TPU:1 before, /device:TPU:25 now
where the time goes in v4:
time: 135 us; the launch traced here: 134 us
  starting transfers between devices  68.1 us (50%)
  waiting for transfers between devices  38.4 us (28%)
  Pallas kernels  20.9 us (15%)
  local copies, waits for them, and re-layouts  5.31 us (4%)
    ppermute x6, starting transfers between devices, partner(): lax.ppermute(value, 'wide', [(s, s ^ mask) for s in range(lax.axis_size('...  37.5 us
    ppermute x4, waiting for transfers between devices, shift(): return lax.ppermute(value, axis, pairs)  32.8 us
    pallas_call x9, Pallas kernels, call(): pl.pallas_call(kernel, out_shape=shapes, in_specs=specs, out_specs=outs i...  20.9 us
    ppermute x4, starting transfers between devices, shift(): return lax.ppermute(value, axis, pairs)  19.8 us
    ppermute x2, starting transfers between devices, sides(): lax.ppermute(cross, 'narrow', across + [(b, a) for a, b in across])  6.47 us
    ppermute x6, waiting for transfers between devices, partner(): lax.ppermute(value, 'wide', [(s, s ^ mask) for s in range(lax.axis_size('...  4.65 us
    ppermute x2, starting transfers between devices, sides(): lax.ppermute(chip, 'narrow', [(i, i ^ 1) for i in range(count)])  4.32 us
    unnamed x18, local copies, waits for them, and re-layouts  3.94 us
  transfers between devices with their start and end apart: 14, of which 4 were waited for; matrix products, arithmetic and copies ran while one was open for 2% of the time, Pallas kernels for 10%

profile of v4, /device:TPU:25, one launch (start us, length us, event | category | flops | bytes accessed | tf_op | source)
XLA Modules:
  0.0 134.4 jit_solution(5248733742887796531)
XLA Ops:
  3.3 1.7 %shard_map.93 = (bf16[256,768]{1,0:T(8,128)(2,1)}, bf16[512,768]{1,0:T(8,128)(2,1)}) custom-call(s32[1,3]{1,0:T(1,128)S(1)} %copy-done.6, bf16[256,768]{1,0:T(8,128)(2,1)S(1)} %copy-done.1, bf16[256,768]{1,0:T(8,128)(2,1)S(1)} %copy-done.3), custom_call_target="tpu_custom_call" | custom-call | tf_op jit(solution)/shard_map/pallas_call | solution.py:417
  4.9 3.7 %collective-permute-start.2 = (bf16[512,768]{1,0:T(8,128)(2,1)}, bf16[512,768]{1,0:T(8,128)(2,1)S(1)}, u32[]{:S(2)}, u32[]{:S(2)}) collective-permute-start(bf16[512,768]{1,0:T(8,128)(2,1)} %get-tuple-element.35), channel_id=1, source_target_pairs={{1,2},{2,1},{5,6},{6,5},{9,10},{10,9},{13,14},{14,13},{17,18},{18,... | collective-permute-start | bytes 2359304 | tf_op jit(solution)/shard_map/ppermute | solution.py:548
  8.6 1.9 %collective-permute-start.1 = (bf16[512,768]{1,0:T(8,128)(2,1)}, bf16[512,768]{1,0:T(8,128)(2,1)S(1)}, u32[]{:S(2)}, u32[]{:S(2)}) collective-permute-start(bf16[512,768]{1,0:T(8,128)(2,1)} %get-tuple-element.35), channel_id=1, source_target_pairs={{0,1},{1,0},{2,3},{3,2},{4,5},{5,4},{6,7},{7,6},{8,9},{9,8},{10,11... | collective-permute-start | bytes 2359304 | tf_op jit(solution)/shard_map/ppermute | solution.py:547
  10.5 15.4 %collective-permute-start = (bf16[256,768]{1,0:T(8,128)(2,1)}, bf16[256,768]{1,0:T(8,128)(2,1)S(1)}, u32[]{:S(2)}, u32[]{:S(2)}) collective-permute-start(bf16[256,768]{1,0:T(8,128)(2,1)} %get-tuple-element.34), channel_id=1, source_target_pairs={{0,64},{4,68},{8,72},{12,76},{16,80},{20,84},{24,88},{28,92},{32,9... | collective-permute-start | bytes 1179656 | tf_op jit(solution)/shard_map/ppermute | solution.py:554
  27.9 1.8 %shard_map.94 = (bf16[256,768]{1,0:T(8,128)(2,1)}, bf16[256,768]{1,0:T(8,128)(2,1)}, bf16[256,768]{1,0:T(8,128)(2,1)}, bf16[256,768]{1,0:T(8,128)(2,1)}) custom-call(s32[1,3]{1,0:T(1,128)S(1)} %copy-done.7, bf16[512,768]{1,0:T(8,128)(2,1)S(1)} %collective-permute-done.1.chip, bf16[512,768]{1,0:T(8,128)(2,1)S(1)} %collective-permute-done.2.cross, ...), custom_call_target="tpu_custom_call" | custom-call | tf_op jit(solution)/shard_map/pallas_call | solution.py:417
  29.7 4.3 %collective-permute-start.3 = (bf16[256,768]{1,0:T(8,128)(2,1)}, bf16[256,768]{1,0:T(8,128)(2,1)}, u32[]{:S(2)}, u32[]{:S(2)}) collective-permute-start(bf16[256,768]{1,0:T(8,128)(2,1)} %get-tuple-element.36), channel_id=1, source_target_pairs={{0,4},{4,8},{8,12},{12,16},{16,20},{20,24},{24,28},{28,32},{32,36}... | collective-permute-start | bytes 1179656 | tf_op jit(solution)/shard_map/ppermute | solution.py:560
  34.1 5.4 %collective-permute-start.4 = (bf16[256,768]{1,0:T(8,128)(2,1)}, bf16[256,768]{1,0:T(8,128)(2,1)}, u32[]{:S(2)}, u32[]{:S(2)}) collective-permute-start(bf16[256,768]{1,0:T(8,128)(2,1)} %get-tuple-element.37), channel_id=1, source_target_pairs={{4,0},{8,4},{12,8},{16,12},{20,16},{24,20},{28,24},{32,28},{36,32}... | collective-permute-start | bytes 1179656 | tf_op jit(solution)/shard_map/ppermute | solution.py:560
  39.5 2.9 %collective-permute-start.5 = (bf16[256,768]{1,0:T(8,128)(2,1)}, bf16[256,768]{1,0:T(8,128)(2,1)}, u32[]{:S(2)}, u32[]{:S(2)}) collective-permute-start(bf16[256,768]{1,0:T(8,128)(2,1)} %get-tuple-element.38), channel_id=1, source_target_pairs={{0,256},{4,260},{8,264},{12,268},{16,272},{20,276},{24,280},{28,28... | collective-permute-start | bytes 1179656 | tf_op jit(solution)/shard_map/ppermute | solution.py:554
  42.4 1.9 %collective-permute-start.6 = (bf16[256,768]{1,0:T(8,128)(2,1)}, bf16[256,768]{1,0:T(8,128)(2,1)}, u32[]{:S(2)}, u32[]{:S(2)}) collective-permute-start(bf16[256,768]{1,0:T(8,128)(2,1)} %get-tuple-element.39), channel_id=1, source_target_pairs={{0,128},{4,132},{8,136},{12,140},{16,144},{20,148},{24,152},{28,15... | collective-permute-start | bytes 1179656 | tf_op jit(solution)/shard_map/ppermute | solution.py:554
  45.8 2.5 %shard_map.95 = (f32[6,8,256]{2,1,0:T(8,128)S(1)}, f32[6,128,256]{2,1,0:T(8,128)S(1)}, f32[6,128,256]{2,1,0:T(8,128)S(1)}) custom-call(s32[2,11]{1,0:T(2,128)S(1)} %concatenate.3.seen, bf16[256,768]{1,0:T(8,128)(2,1)S(1)} %copy-done, bf16[256,768]{1,0:T(8,128)(2,1)S(1)} %copy-done.5, bf16[256,768]{1,0:T(8,128)(2,1)S(1)} %copy-done.2, ...), custom_call_target="tpu_custom_call" | custom-call | tf_op jit(solution)/shard_map/pallas_call | solution.py:417
  48.9 21.5 %collective-permute-done.3.left = bf16[256,768]{1,0:T(8,128)(2,1)} collective-permute-done((bf16[256,768]{1,0:T(8,128)(2,1)}, bf16[256,768]{1,0:T(8,128)(2,1)}, u32[]{:S(2)}, u32[]{:S(2)}) %collective-permute-start.3) | collective-permute-done | bytes 393248 | tf_op jit(solution)/shard_map/ppermute | solution.py:560
  70.4 3.6 %shard_map.97 = (f32[6,8,256]{2,1,0:T(8,128)S(1)}, bf16[6,128,256]{2,1,0:T(8,128)(2,1)S(1)}, f32[6,128,256]{2,1,0:T(8,128)S(1)}, bf16[256,768]{1,0:T(8,128)(2,1)...) custom-call(bf16[256,768]{1,0:T(8,128)(2,1)S(1)} %collective-permute-done.far2, ...), custom_call_target="tpu_custom_call" | custom-call | tf_op jit(solution)/shard_map/pallas_call | solution.py:417
  74.0 2.4 %collective-permute-start.7 = (bf16[512,768]{1,0:T(8,128)(2,1)S(1)}, bf16[512,768]{1,0:T(8,128)(2,1)S(1)}, u32[]{:S(2)}, u32[]{:S(2)}) collective-permute-start(bf16[512,768]{1,0:T(8,128)(2,1)S(1)} %get-tuple-element.45), channel_id=1, source_target_pairs={{0,1},{1,0},{2,3},{3,2},{4,5},{5,4},{6,7},{7,6},{8,9},{9,8},{10,11... | collective-permute-start | bytes 2359304 | tf_op jit(solution)/shard_map/ppermute | solution.py:547
  76.4 2.8 %collective-permute-start.8 = (bf16[512,768]{1,0:T(8,128)(2,1)S(1)}, bf16[512,768]{1,0:T(8,128)(2,1)S(1)}, u32[]{:S(2)}, u32[]{:S(2)}) collective-permute-start(bf16[512,768]{1,0:T(8,128)(2,1)S(1)} %get-tuple-element.46), channel_id=1, source_target_pairs={{1,2},{2,1},{5,6},{6,5},{9,10},{10,9},{13,14},{14,13},{17,18},{18,... | collective-permute-start | bytes 2359304 | tf_op jit(solution)/shard_map/ppermute | solution.py:548
  79.2 9.5 %collective-permute-start.9 = (bf16[256,768]{1,0:T(8,128)(2,1)S(1)}, bf16[256,768]{1,0:T(8,128)(2,1)S(1)}, u32[]{:S(2)}, u32[]{:S(2)}) collective-permute-start(bf16[256,768]{1,0:T(8,128)(2,1)S(1)} %get-tuple-element.53), channel_id=1, source_target_pairs={{0,64},{4,68},{8,72},{12,76},{16,80},{20,84},{24,88},{28,92},{32,9... | collective-permute-start | bytes 1179656 | tf_op jit(solution)/shard_map/ppermute | solution.py:554
  89.7 4.0 %shard_map.98 = (bf16[256,768]{1,0:T(8,128)(2,1)S(1)}, bf16[256,768]{1,0:T(8,128)(2,1)S(1)}, bf16[256,768]{1,0:T(8,128)(2,1)S(1)}, bf16[256,768]{1,0:T(8,128)(2,1)S(1)}, f32[6,128,256]{2,1,0:T(8,128)S(1)}) custom-call(s32[2,11]{1,0:T(2,128)S(1)} %concatenate.3.seen, bf16[256,768]{1,0:T(8,128)(2,1)S(1)} %copy-done, bf16[256,768]{1,0:T(8,128)(2,1)S(1)} %copy-done.5, ...), custom_call_target="tpu_custom_call" | custom-call | tf_op jit(solution)/shard_map/pallas_call | solution.py:417
  93.7 5.8 %collective-permute-start.10 = (bf16[256,768]{1,0:T(8,128)(2,1)S(1)}, bf16[256,768]{1,0:T(8,128)(2,1)S(1)}, u32[]{:S(2)}, u32[]{:S(2)}) collective-permute-start(bf16[256,768]{1,0:T(8,128)(2,1)S(1)} %get-tuple-element.58), channel_id=1, source_target_pairs={{0,256},{4,260},{8,264},{12,268},{16,272},{20,276},{24,280},{28,28... | collective-permute-start | bytes 1179656 | tf_op jit(solution)/shard_map/ppermute | solution.py:554
  99.5 1.9 %collective-permute-start.11 = (bf16[256,768]{1,0:T(8,128)(2,1)S(1)}, bf16[256,768]{1,0:T(8,128)(2,1)S(1)}, u32[]{:S(2)}, u32[]{:S(2)}) collective-permute-start(bf16[256,768]{1,0:T(8,128)(2,1)S(1)} %get-tuple-element.59), channel_id=1, source_target_pairs={{0,128},{4,132},{8,136},{12,140},{16,144},{20,148},{24,152},{28,15... | collective-permute-start | bytes 1179656 | tf_op jit(solution)/shard_map/ppermute | solution.py:554
  101.5 5.3 %collective-permute-start.12 = (bf16[256,768]{1,0:T(8,128)(2,1)S(1)}, bf16[256,768]{1,0:T(8,128)(2,1)S(1)}, u32[]{:S(2)}, u32[]{:S(2)}) collective-permute-start(bf16[256,768]{1,0:T(8,128)(2,1)S(1)} %get-tuple-element.60), channel_id=1, source_target_pairs={{0,4},{4,8},{8,12},{12,16},{16,20},{20,24},{24,28},{28,32},{32,36}... | collective-permute-start | bytes 1179656 | tf_op jit(solution)/shard_map/ppermute | solution.py:560
  106.7 4.8 %collective-permute-start.13 = (bf16[256,768]{1,0:T(8,128)(2,1)S(1)}, bf16[256,768]{1,0:T(8,128)(2,1)S(1)}, u32[]{:S(2)}, u32[]{:S(2)}) collective-permute-start(bf16[256,768]{1,0:T(8,128)(2,1)S(1)} %get-tuple-element.61), channel_id=1, source_target_pairs={{4,0},{8,4},{12,8},{16,12},{20,16},{24,20},{28,24},{32,28},{36,32}... | collective-permute-start | bytes 1179656 | tf_op jit(solution)/shard_map/ppermute | solution.py:560
  111.5 4.4 %shard_map.99 = (bf16[256,768]{1,0:T(8,128)(2,1)}, bf16[256,768]{1,0:T(8,128)(2,1)}, f32[256,768]{1,0:T(8,128)S(1)}, f32[256,768]{1,0:T(8,128)S(1)}) custom-call(s32[2,11]{1,0:T(2,128)S(1)} %concatenate.3.seen, bf16[256,768]{1,0:T(8,128)(2,1)S(1)} %copy-done, bf16[256,768]{1,0:T(8,128)(2,1)S(1)} %copy-done.5, bf16[256,768]{1,0:T(8,128)(2,1)S(1)} %copy-done.2, ...), custom_call_target="tpu_custom_call" | custom-call | tf_op jit(solution)/shard_map/pallas_call | solution.py:417
  115.9 4.6 %collective-permute-done.9.far2 = bf16[256,768]{1,0:T(8,128)(2,1)S(1)} collective-permute-done((bf16[256,768]{1,0:T(8,128)(2,1)S(1)}, bf16[256,768]{1,0:T(8,128)(2,1)S(1)}, u32[]{:S(2)}, u32[]{:S(2)}) %collective-permute-start.9) | collective-permute-done | bytes 393248 | tf_op jit(solution)/shard_map/ppermute | solution.py:554
  121.3 11.4 %collective-permute-done.12.low_block = bf16[256,768]{1,0:T(8,128)(2,1)S(1)} collective-permute-done((bf16[256,768]{1,0:T(8,128)(2,1)S(1)}, bf16[256,768]{1,0:T(8,128)(2,1)S(1)}, u32[]{:S(2)}, u32[]{:S(2)}) %collective-permute-start.12) | collective-permute-done | bytes 393248 | tf_op jit(solution)/shard_map/ppermute | solution.py:560
  132.6 1.7 %shard_map.101 = (bf16[256,768]{1,0:T(8,128)(2,1)}, bf16[256,768]{1,0:T(8,128)(2,1)}) custom-call(s32[1,3]{1,0:T(1,128)S(1)} %copy-done.7, f32[256,768]{1,0:T(8,128)S(1)} %get-tuple-element.56.key_sum, f32[256,768]{1,0:T(8,128)S(1)} %get-tuple-element.57.value_sum, bf16[256,768]{1,0:T(8,128)(2,1)S(1)} %collective-permute-done.10.far0, ...), custom_call_target="tpu_custom_call" | custom-call | tf_op jit(solution)/shard_map/pallas_call | solution.py:417
  (35 shorter events, 8.3 us)
Async XLA Ops:
  0.6 1.0 copy-start.1
  1.6 1.0 copy-start.3
  2.6 0.7 copy-start.6
  3.3 24.0 %copy-start.2 = (bf16[256,768]{1,0:T(8,128)(2,1)S(1)}, bf16[256,768]{1,0:T(8,128)(2,1)}, u32[]{:S(2)}) copy-start(bf16[256,768]{1,0:T(8,128)(2,1)} %key.7) | copy-start | bytes 1179652
  3.3 24.0 %copy-start.4 = (bf16[256,768]{1,0:T(8,128)(2,1)S(1)}, bf16[256,768]{1,0:T(8,128)(2,1)}, u32[]{:S(2)}) copy-start(bf16[256,768]{1,0:T(8,128)(2,1)} %value.7) | copy-start | bytes 1179652
  4.9 22.4 %collective-permute-start.2 = (bf16[512,768]{1,0:T(8,128)(2,1)}, bf16[512,768]{1,0:T(8,128)(2,1)S(1)}, u32[]{:S(2)}, u32[]{:S(2)}) collective-permute-start(bf16[512,768]{1,0:T(8,128)(2,1)} %get-tuple-element.35), channel_id=1, source_target_pairs={{1,2},{2,1},{5,6},{6,5},{9,10},{10,9},{13,14},{14,13},{17,18},{18,... | collective-permute-start | bytes 2359304 | tf_op jit(solution)/shard_map/ppermute | solution.py:548
  8.6 18.7 %collective-permute-start.1 = (bf16[512,768]{1,0:T(8,128)(2,1)}, bf16[512,768]{1,0:T(8,128)(2,1)S(1)}, u32[]{:S(2)}, u32[]{:S(2)}) collective-permute-start(bf16[512,768]{1,0:T(8,128)(2,1)} %get-tuple-element.35), channel_id=1, source_target_pairs={{0,1},{1,0},{2,3},{3,2},{4,5},{5,4},{6,7},{7,6},{8,9},{9,8},{10,11... | collective-permute-start | bytes 2359304 | tf_op jit(solution)/shard_map/ppermute | solution.py:547
  10.5 37.8 %collective-permute-start = (bf16[256,768]{1,0:T(8,128)(2,1)}, bf16[256,768]{1,0:T(8,128)(2,1)S(1)}, u32[]{:S(2)}, u32[]{:S(2)}) collective-permute-start(bf16[256,768]{1,0:T(8,128)(2,1)} %get-tuple-element.34), channel_id=1, source_target_pairs={{0,64},{4,68},{8,72},{12,76},{16,80},{20,84},{24,88},{28,92},{32,9... | collective-permute-start | bytes 1179656 | tf_op jit(solution)/shard_map/ppermute | solution.py:554
  26.0 0.7 copy-start.8
  27.3 0.7 copy-start.7
  27.3 18.5 %copy-start = (bf16[256,768]{1,0:T(8,128)(2,1)S(1)}, bf16[256,768]{1,0:T(8,128)(2,1)}, u32[]{:S(2)}) copy-start(bf16[256,768]{1,0:T(8,128)(2,1)} %query.9) | copy-start | bytes 1179652
  27.3 18.5 %copy-start.5 = (bf16[256,768]{1,0:T(8,128)(2,1)S(1)}, bf16[256,768]{1,0:T(8,128)(2,1)}, u32[]{:S(2)}) copy-start(bf16[256,768]{1,0:T(8,128)(2,1)} %upward.7) | copy-start | bytes 1179652
  29.7 40.7 %collective-permute-start.3 = (bf16[256,768]{1,0:T(8,128)(2,1)}, bf16[256,768]{1,0:T(8,128)(2,1)}, u32[]{:S(2)}, u32[]{:S(2)}) collective-permute-start(bf16[256,768]{1,0:T(8,128)(2,1)} %get-tuple-element.36), channel_id=1, source_target_pairs={{0,4},{4,8},{8,12},{12,16},{16,20},{20,24},{24,28},{28,32},{32,36}... | collective-permute-start | bytes 1179656 | tf_op jit(solution)/shard_map/ppermute | solution.py:560
  34.1 36.3 %collective-permute-start.4 = (bf16[256,768]{1,0:T(8,128)(2,1)}, bf16[256,768]{1,0:T(8,128)(2,1)}, u32[]{:S(2)}, u32[]{:S(2)}) collective-permute-start(bf16[256,768]{1,0:T(8,128)(2,1)} %get-tuple-element.37), channel_id=1, source_target_pairs={{4,0},{8,4},{12,8},{16,12},{20,16},{24,20},{28,24},{32,28},{36,32}... | collective-permute-start | bytes 1179656 | tf_op jit(solution)/shard_map/ppermute | solution.py:560
  39.5 30.9 %collective-permute-start.5 = (bf16[256,768]{1,0:T(8,128)(2,1)}, bf16[256,768]{1,0:T(8,128)(2,1)}, u32[]{:S(2)}, u32[]{:S(2)}) collective-permute-start(bf16[256,768]{1,0:T(8,128)(2,1)} %get-tuple-element.38), channel_id=1, source_target_pairs={{0,256},{4,260},{8,264},{12,268},{16,272},{20,276},{24,280},{28,28... | collective-permute-start | bytes 1179656 | tf_op jit(solution)/shard_map/ppermute | solution.py:554
  42.4 28.0 %collective-permute-start.6 = (bf16[256,768]{1,0:T(8,128)(2,1)}, bf16[256,768]{1,0:T(8,128)(2,1)}, u32[]{:S(2)}, u32[]{:S(2)}) collective-permute-start(bf16[256,768]{1,0:T(8,128)(2,1)} %get-tuple-element.39), channel_id=1, source_target_pairs={{0,128},{4,132},{8,136},{12,140},{16,144},{20,148},{24,152},{28,15... | collective-permute-start | bytes 1179656 | tf_op jit(solution)/shard_map/ppermute | solution.py:554
  74.0 14.8 %collective-permute-start.7 = (bf16[512,768]{1,0:T(8,128)(2,1)S(1)}, bf16[512,768]{1,0:T(8,128)(2,1)S(1)}, u32[]{:S(2)}, u32[]{:S(2)}) collective-permute-start(bf16[512,768]{1,0:T(8,128)(2,1)S(1)} %get-tuple-element.45), channel_id=1, source_target_pairs={{0,1},{1,0},{2,3},{3,2},{4,5},{5,4},{6,7},{7,6},{8,9},{9,8},{10,11... | collective-permute-start | bytes 2359304 | tf_op jit(solution)/shard_map/ppermute | solution.py:547
  76.4 13.3 %collective-permute-start.8 = (bf16[512,768]{1,0:T(8,128)(2,1)S(1)}, bf16[512,768]{1,0:T(8,128)(2,1)S(1)}, u32[]{:S(2)}, u32[]{:S(2)}) collective-permute-start(bf16[512,768]{1,0:T(8,128)(2,1)S(1)} %get-tuple-element.46), channel_id=1, source_target_pairs={{1,2},{2,1},{5,6},{6,5},{9,10},{10,9},{13,14},{14,13},{17,18},{18,... | collective-permute-start | bytes 2359304 | tf_op jit(solution)/shard_map/ppermute | solution.py:548
  79.2 41.3 %collective-permute-start.9 = (bf16[256,768]{1,0:T(8,128)(2,1)S(1)}, bf16[256,768]{1,0:T(8,128)(2,1)S(1)}, u32[]{:S(2)}, u32[]{:S(2)}) collective-permute-start(bf16[256,768]{1,0:T(8,128)(2,1)S(1)} %get-tuple-element.53), channel_id=1, source_target_pairs={{0,64},{4,68},{8,72},{12,76},{16,80},{20,84},{24,88},{28,92},{32,9... | collective-permute-start | bytes 1179656 | tf_op jit(solution)/shard_map/ppermute | solution.py:554
  93.7 27.5 %collective-permute-start.10 = (bf16[256,768]{1,0:T(8,128)(2,1)S(1)}, bf16[256,768]{1,0:T(8,128)(2,1)S(1)}, u32[]{:S(2)}, u32[]{:S(2)}) collective-permute-start(bf16[256,768]{1,0:T(8,128)(2,1)S(1)} %get-tuple-element.58), channel_id=1, source_target_pairs={{0,256},{4,260},{8,264},{12,268},{16,272},{20,276},{24,280},{28,28... | collective-permute-start | bytes 1179656 | tf_op jit(solution)/shard_map/ppermute | solution.py:554
  99.5 21.7 %collective-permute-start.11 = (bf16[256,768]{1,0:T(8,128)(2,1)S(1)}, bf16[256,768]{1,0:T(8,128)(2,1)S(1)}, u32[]{:S(2)}, u32[]{:S(2)}) collective-permute-start(bf16[256,768]{1,0:T(8,128)(2,1)S(1)} %get-tuple-element.59), channel_id=1, source_target_pairs={{0,128},{4,132},{8,136},{12,140},{16,144},{20,148},{24,152},{28,15... | collective-permute-start | bytes 1179656 | tf_op jit(solution)/shard_map/ppermute | solution.py:554
  101.5 31.2 %collective-permute-start.12 = (bf16[256,768]{1,0:T(8,128)(2,1)S(1)}, bf16[256,768]{1,0:T(8,128)(2,1)S(1)}, u32[]{:S(2)}, u32[]{:S(2)}) collective-permute-start(bf16[256,768]{1,0:T(8,128)(2,1)S(1)} %get-tuple-element.60), channel_id=1, source_target_pairs={{0,4},{4,8},{8,12},{12,16},{16,20},{20,24},{24,28},{28,32},{32,36}... | collective-permute-start | bytes 1179656 | tf_op jit(solution)/shard_map/ppermute | solution.py:560
  106.7 25.9 %collective-permute-start.13 = (bf16[256,768]{1,0:T(8,128)(2,1)S(1)}, bf16[256,768]{1,0:T(8,128)(2,1)S(1)}, u32[]{:S(2)}, u32[]{:S(2)}) collective-permute-start(bf16[256,768]{1,0:T(8,128)(2,1)S(1)} %get-tuple-element.61), channel_id=1, source_target_pairs={{4,0},{8,4},{12,8},{16,12},{20,16},{24,20},{28,24},{32,28},{36,32}... | collective-permute-start | bytes 1179656 | tf_op jit(solution)/shard_map/ppermute | solution.py:560

commit v5 on v2

--- a/solution.py
+++ b/solution.py
@@ -130,8 +130,8 @@
     return [range(first, first + GROUP) for first in range(0, PAIRS, GROUP)]
 
 
-def own_slots(key, value):
-    return [(b, key, b * BLK, value, b * BLK) for b in range(BW)]
+def own_slots(whole):
+    return [(b, whole, b * BLK, whole, ROWS + b * BLK) for b in range(BW)]
 
 
 def side_slots(chip, cross):
@@ -195,14 +195,14 @@
     lax.fori_loop(0, count, step, 0)
 
 
-def first_kernel(seen, query, upward, key, value, chip, cross, stat, acc, upward_t, held, place):
+def first_kernel(seen, query, upward, whole, chip, cross, stat, acc, upward_t, held, place):
     for pair in range(PAIRS):
         stat[pair, 0:2, :] = jnp.full((2, ROWS), HIDDEN, f32)
         stat[pair, 2:4, :] = jnp.zeros((2, ROWS), f32)
         acc[pair] = jnp.zeros((BLK, ROWS), f32)
         upward_t[pair] = upward[:, feature(pair)].astype(f32).T
     forward_over(
-        own_slots(key, value) + side_slots(chip, cross), seen, query, stat, acc, held, place
+        own_slots(whole) + side_slots(chip, cross), seen, query, stat, acc, held, place
     )
 
 
@@ -308,16 +308,33 @@
     )
 
 
-def backward_kernel(
+def terms_kernel(columns, gates):
+    def kernel(seen, query, upward, one, two, stat, query_t_in, *refs):
+        one_term, two_term, query_t, terms, held, place = refs[gates:]
+        query_t[...] = query_t_in[...]
+        targets = pair_slots(columns, one_term, two_term)
+        clear_unseen(targets, seen)
+        backward_over(
+            pair_slots(columns, one, two),
+            seen,
+            query,
+            upward,
+            stat,
+            query_t,
+            held,
+            place,
+            terms,
+            lambda j: store_terms(targets, terms, j),
+        )
+
+    return kernel
+
+
+def own_kernel(
     seen,
     query,
     upward,
-    key,
-    value,
-    left,
-    right,
-    far0,
-    far1,
+    whole,
     chip_back,
     cross_back,
     stat,
@@ -327,10 +344,6 @@
     query_grad,
     key_sum,
     value_sum,
-    left_term,
-    right_term,
-    far0_term,
-    far1_term,
     query_t,
     terms,
     held,
@@ -339,8 +352,6 @@
     query_t[...] = query_t_in[...]
     for pair in range(PAIRS):
         attention[:, feature(pair)] = out_t[pair].astype(f32).T.astype(bf16)
-    targets = rest_slots(left_term, right_term, far0_term, far1_term)
-    clear_unseen(targets, seen)
 
     def store(j):
         for b in range(BW):
@@ -355,19 +366,8 @@
                         + cross_back[side].astype(f32)
                     )
 
-        store_terms(targets, terms, j)
-
     backward_over(
-        own_slots(key, value) + rest_slots(left, right, far0, far1),
-        seen,
-        query,
-        upward,
-        stat,
-        query_t,
-        held,
-        place,
-        terms,
-        store,
+        own_slots(whole), seen, query, upward, stat, query_t, held, place, terms, store
     )
     for pair in range(PAIRS):
         query_grad[:, feature(pair)] = (query_t[pair] * SCALE).T.astype(bf16)
@@ -421,35 +421,37 @@
 SIDE = shape((2 * ROWS, D), bf16)
 
 
-def block_of(key, value, start, out):
-    rows = pl.ds(pl.multiple_of(start, BLK), BLK)
-    out[0:BLK] = key[rows]
-    out[BLK : 2 * BLK] = value[rows]
-
-
-def pack_first_kernel(pick, key, value, far2, whole):
-    block_of(key, value, pick[0, 2] * BLK, far2)
+def block_of(whole, start, out):
+    for half in range(2):
+        rows = pl.ds(pl.multiple_of(half * ROWS + start, BLK), BLK)
+        out[half * BLK : (half + 1) * BLK] = whole[rows]
+
+
+def pack_first_kernel(pick, key, value, whole, far2, right, left):
     whole[0:ROWS] = key[...]
     whole[ROWS : 2 * ROWS] = value[...]
-
-
-def pack_rest_kernel(pick, chip, cross, key, value, right, left, far0, far1):
-    block_of(key, value, 0, right)
-    block_of(key, value, ROWS - BLK, left)
-    block_of(key, value, pick[0, 0] * BLK, far0)
-    block_of(key, value, pick[0, 1] * BLK, far1)
+    block_of(whole, pick[0, 2] * BLK, far2)
+    block_of(whole, 0, right)
+    block_of(whole, ROWS - BLK, left)
+
+
+def pack_rest_kernel(pick, chip, cross, whole, far0, far1):
+    block_of(whole, pick[0, 0] * BLK, far0)
+    block_of(whole, pick[0, 1] * BLK, far1)
 
 
 def pack_first(pick, key, value):
-    return call(pack_first_kernel, [RIM, SIDE], [smem(), vmem(), vmem()], (pick, key, value))
-
-
-def pack_rest(pick, chip, cross, key, value):
+    return call(
+        pack_first_kernel, [SIDE, RIM, RIM, RIM], [smem(), vmem(), vmem()], (pick, key, value)
+    )
+
+
+def pack_rest(pick, chip, cross, whole):
     return call(
         pack_rest_kernel,
-        [RIM] * 4,
-        [smem(), hbm(), hbm(), vmem(), vmem()],
-        (pick, chip, cross, key, value),
+        [RIM] * 2,
+        [smem(), hbm(), hbm(), vmem()],
+        (pick, chip, cross, whole),
     )
 
 
@@ -457,12 +459,12 @@
     return [pltpu.VMEM((slots, 2 * BLK, D), bf16), pltpu.SMEM((16,), jnp.int32)]
 
 
-def run_first(plan, queries, upstream, *near):
+def run_first(plan, *rest):
     return call(
         first_kernel,
         STATE + [shape((PAIRS, BLK, ROWS), f32)],
-        [smem()] + [vmem()] * 6,
-        (plan, queries, upstream, *near),
+        [smem()] + [vmem()] * 5,
+        (plan, *rest),
         scratch=seen_scratch(6),
     )
 
@@ -488,16 +490,26 @@
     )
 
 
-def run_backward(plan, *rest):
+def run_terms(columns, plan, queries, upstream, one, two, stat, query_t, *gates):
+    return call(
+        terms_kernel(columns, len(gates)),
+        [RIM, RIM, STATE[1]],
+        [smem()] + [vmem()] * 6 + [hbm()] * len(gates),
+        (plan, queries, upstream, one, two, stat, query_t, *gates),
+        scratch=[pltpu.VMEM((2 * BLK, D), bf16)] + seen_scratch(2),
+    )
+
+
+def run_own(plan, *rest):
     whole = shape((ROWS, D), bf16)
     total = shape((ROWS, D), f32)
     return call(
-        backward_kernel,
-        [whole, whole, total, total] + [RIM] * 4,
-        [smem()] + [vmem()] * 13,
+        own_kernel,
+        [whole, whole, total, total],
+        [smem()] + [vmem()] * 8,
         (plan, *rest),
         scratch=[pltpu.VMEM((PAIRS, BLK, ROWS), f32), pltpu.VMEM((2 * BLK, D), bf16)]
-        + seen_scratch(6),
+        + seen_scratch(2),
     )
 
 
@@ -556,37 +568,29 @@
         axis=1,
     )
 
-    far2_pair, whole = pack_first(expander_pick, key_rows, value_rows)
+    whole, far2_pair, right_pair, left_pair = pack_first(expander_pick, key_rows, value_rows)
     chip, cross = sides(whole, whole)
     far2 = partner(far2_pair, top_bit - EXP)
-    right_pair, left_pair, far0_pair, far1_pair = pack_rest(
-        expander_pick, chip, cross, key_rows, value_rows
-    )
-    rest = (
-        shift(left_pair, "wide", 1),
-        shift(right_pair, "wide", -1),
-        partner(far0_pair, top_bit - 1),
-        partner(far1_pair, top_bit - 2),
-    )
-    stat, acc, upward_t = run_first(plan, queries, upstream, key_rows, value_rows, chip, cross)
+    left = shift(left_pair, "wide", 1)
+    right = shift(right_pair, "wide", -1)
+    far0_pair, far1_pair = pack_rest(expander_pick, chip, cross, whole)
+    far0 = partner(far0_pair, top_bit - 1)
+    far1 = partner(far1_pair, top_bit - 2)
+    stat, acc, upward_t = run_first(plan, queries, upstream, whole, chip, cross)
     stat, acc = run_far(far2, plan, queries, stat, acc)
     stat, out_t, query_t, far2_term, chip_term, cross_term = run_middle(
-        far2, plan, queries, upstream, chip, cross, *rest, stat, acc, upward_t
+        far2, plan, queries, upstream, chip, cross, left, right, far0, far1, stat, acc, upward_t
     )
     far2_back = partner(far2_term, top_bit - EXP)
-    attention, query_grad, key_near, value_near, left_term, right_term, far0_term, far1_term = (
-        run_backward(
-            plan,
-            queries,
-            upstream,
-            key_rows,
-            value_rows,
-            *rest,
-            *sides(chip_term, cross_term),
-            stat,
-            out_t,
-            query_t,
-        )
+    back = sides(chip_term, cross_term)
+    left_term, right_term, query_t = run_terms(
+        (2, 3), plan, queries, upstream, left, right, stat, query_t
+    )
+    far0_term, far1_term, query_t = run_terms(
+        (8, 9), plan, queries, upstream, far0, far1, stat, query_t, *back
+    )
+    attention, query_grad, key_near, value_near = run_own(
+        plan, queries, upstream, whole, *back, stat, out_t, query_t
     )
     key_sum, value_sum = run_first_sum(far2_back, expander_pick, key_near, value_near)
     key_grad, value_grad = run_second_sum(

time: 142 us -> 138 us (0.972)
  the two profiles are of different devices: /device:TPU:1 before, /device:TPU:10 now
where the time goes in v5:
time: 138 us; the launch traced here: 137 us
  starting transfers between devices  69.6 us (50%)
  waiting for transfers between devices  36.6 us (27%)
  Pallas kernels  23.9 us (17%)
  local copies, waits for them, and re-layouts  5.4 us (4%)
    ppermute x6, starting transfers between devices, partner(): lax.ppermute(value, 'wide', [(s, s ^ mask) for s in range(lax.axis_size('...  38.6 us
    pallas_call x10, Pallas kernels, call(): pl.pallas_call(kernel, out_shape=shapes, in_specs=specs, out_specs=outs i...  23.9 us
    ppermute x4, waiting for transfers between devices, shift(): return lax.ppermute(value, axis, pairs)  22.8 us
    ppermute x4, starting transfers between devices, shift(): return lax.ppermute(value, axis, pairs)  20.7 us
    ppermute x6, waiting for transfers between devices, partner(): lax.ppermute(value, 'wide', [(s, s ^ mask) for s in range(lax.axis_size('...  13.8 us
    ppermute x2, starting transfers between devices, sides(): lax.ppermute(cross, 'narrow', across + [(b, a) for a, b in across])  6.44 us
    unnamed x14, local copies, waits for them, and re-layouts  3.95 us
    ppermute x2, starting transfers between devices, sides(): lax.ppermute(chip, 'narrow', [(i, i ^ 1) for i in range(count)])  3.84 us
  transfers between devices with their start and end apart: 14, of which 5 were waited for; matrix products, arithmetic and copies ran while one was open for 2% of the time, Pallas kernels for 12%

profile of v5, /device:TPU:10, one launch (start us, length us, event | category | flops | bytes accessed | tf_op | source)
XLA Modules:
  0.0 137.1 jit_solution(6970391258090883808)
XLA Ops:
  4.9 1.9 %collective-permute-start.2 = (bf16[512,768]{1,0:T(8,128)(2,1)S(1)}, bf16[512,768]{1,0:T(8,128)(2,1)S(1)}, u32[]{:S(2)}, u32[]{:S(2)}) collective-permute-start(bf16[512,768]{1,0:T(8,128)(2,1)S(1)} %get-tuple-element.35.whole), channel_id=1, source_target_pairs={{1,2},{2,1},{5,6},{6,5},{9,10},{10,9},{13,14},{14,13},{17,18},{18,... | collective-permute-start | bytes 2359304 | tf_op jit(solution)/shard_map/ppermute | solution.py:533
  6.8 1.9 %collective-permute-start.1 = (bf16[512,768]{1,0:T(8,128)(2,1)S(1)}, bf16[512,768]{1,0:T(8,128)(2,1)S(1)}, u32[]{:S(2)}, u32[]{:S(2)}) collective-permute-start(bf16[512,768]{1,0:T(8,128)(2,1)S(1)} %get-tuple-element.35.whole), channel_id=1, source_target_pairs={{0,1},{1,0},{2,3},{3,2},{4,5},{5,4},{6,7},{7,6},{8,9},{9,8},{10,11... | collective-permute-start | bytes 2359304 | tf_op jit(solution)/shard_map/ppermute | solution.py:532
  8.7 15.7 %collective-permute-start = (bf16[256,768]{1,0:T(8,128)(2,1)}, bf16[256,768]{1,0:T(8,128)(2,1)}, u32[]{:S(2)}, u32[]{:S(2)}) collective-permute-start(bf16[256,768]{1,0:T(8,128)(2,1)} %get-tuple-element.36), channel_id=1, source_target_pairs={{0,64},{4,68},{8,72},{12,76},{16,80},{20,84},{24,88},{28,92},{32,9... | collective-permute-start | bytes 1179656 | tf_op jit(solution)/shard_map/ppermute | solution.py:539
  24.5 4.3 %collective-permute-start.3 = (bf16[256,768]{1,0:T(8,128)(2,1)}, bf16[256,768]{1,0:T(8,128)(2,1)}, u32[]{:S(2)}, u32[]{:S(2)}) collective-permute-start(bf16[256,768]{1,0:T(8,128)(2,1)} %get-tuple-element.37), channel_id=1, source_target_pairs={{0,4},{4,8},{8,12},{12,16},{16,20},{20,24},{24,28},{28,32},{32,36}... | collective-permute-start | bytes 1179656 | tf_op jit(solution)/shard_map/ppermute | solution.py:545
  28.8 6.1 %collective-permute-start.4 = (bf16[256,768]{1,0:T(8,128)(2,1)}, bf16[256,768]{1,0:T(8,128)(2,1)}, u32[]{:S(2)}, u32[]{:S(2)}) collective-permute-start(bf16[256,768]{1,0:T(8,128)(2,1)} %get-tuple-element.38), channel_id=1, source_target_pairs={{4,0},{8,4},{12,8},{16,12},{20,16},{24,20},{28,24},{32,28},{36,32}... | collective-permute-start | bytes 1179656 | tf_op jit(solution)/shard_map/ppermute | solution.py:545
  38.3 4.2 %collective-permute-start.5 = (bf16[256,768]{1,0:T(8,128)(2,1)}, bf16[256,768]{1,0:T(8,128)(2,1)S(1)}, u32[]{:S(2)}, u32[]{:S(2)}) collective-permute-start(bf16[256,768]{1,0:T(8,128)(2,1)} %get-tuple-element.39), channel_id=1, source_target_pairs={{0,256},{4,260},{8,264},{12,268},{16,272},{20,276},{24,280},{28,28... | collective-permute-start | bytes 1179656 | tf_op jit(solution)/shard_map/ppermute | solution.py:539
  42.5 3.3 %collective-permute-start.6 = (bf16[256,768]{1,0:T(8,128)(2,1)}, bf16[256,768]{1,0:T(8,128)(2,1)}, u32[]{:S(2)}, u32[]{:S(2)}) collective-permute-start(bf16[256,768]{1,0:T(8,128)(2,1)} %get-tuple-element.40), channel_id=1, source_target_pairs={{0,128},{4,132},{8,136},{12,140},{16,144},{20,148},{24,152},{28,15... | collective-permute-start | bytes 1179656 | tf_op jit(solution)/shard_map/ppermute | solution.py:539
  47.3 2.5 %shard_map.95 = (f32[6,8,256]{2,1,0:T(8,128)S(1)}, f32[6,128,256]{2,1,0:T(8,128)S(1)}, f32[6,128,256]{2,1,0:T(8,128)S(1)}) custom-call(s32[2,11]{1,0:T(2,128)S(1)} %concatenate.3.seen, bf16[256,768]{1,0:T(8,128)(2,1)S(1)} %copy-done, bf16[256,768]{1,0:T(8,128)(2,1)S(1)} %copy-done.1, bf16[512,768]{1,0:T(8,128)(2,1)S(1)} %get-tuple-element.35.whole, ...), custom_call_target="tpu_custom_call" | custom-call | tf_op jit(solution)/shard_map/pallas_call | solution.py:400
  50.9 17.6 %collective-permute-done.3.left.one = bf16[256,768]{1,0:T(8,128)(2,1)} collective-permute-done((bf16[256,768]{1,0:T(8,128)(2,1)}, bf16[256,768]{1,0:T(8,128)(2,1)}, u32[]{:S(2)}, u32[]{:S(2)}) %collective-permute-start.3) | collective-permute-done | bytes 393248 | tf_op jit(solution)/shard_map/ppermute | solution.py:545
  69.5 4.4 %shard_map.97 = (f32[6,8,256]{2,1,0:T(8,128)S(1)}, bf16[6,128,256]{2,1,0:T(8,128)(2,1)S(1)}, f32[6,128,256]{2,1,0:T(8,128)S(1)}, bf16[256,768]{1,0:T(8,128)(2,1)...) custom-call(bf16[256,768]{1,0:T(8,128)(2,1)} %collective-permute-done.far2, ...), custom_call_target="tpu_custom_call" | custom-call | tf_op jit(solution)/shard_map/pallas_call | solution.py:400
  74.0 1.9 %collective-permute-start.7 = (bf16[512,768]{1,0:T(8,128)(2,1)S(1)}, bf16[512,768]{1,0:T(8,128)(2,1)S(1)}, u32[]{:S(2)}, u32[]{:S(2)}) collective-permute-start(bf16[512,768]{1,0:T(8,128)(2,1)S(1)} %get-tuple-element.46), channel_id=1, source_target_pairs={{0,1},{1,0},{2,3},{3,2},{4,5},{5,4},{6,7},{7,6},{8,9},{9,8},{10,11... | collective-permute-start | bytes 2359304 | tf_op jit(solution)/shard_map/ppermute | solution.py:532
  75.9 4.5 %collective-permute-start.8 = (bf16[512,768]{1,0:T(8,128)(2,1)S(1)}, bf16[512,768]{1,0:T(8,128)(2,1)S(1)}, u32[]{:S(2)}, u32[]{:S(2)}) collective-permute-start(bf16[512,768]{1,0:T(8,128)(2,1)S(1)} %get-tuple-element.47), channel_id=1, source_target_pairs={{1,2},{2,1},{5,6},{6,5},{9,10},{10,9},{13,14},{14,13},{17,18},{18,... | collective-permute-start | bytes 2359304 | tf_op jit(solution)/shard_map/ppermute | solution.py:533
  80.4 8.9 %collective-permute-start.9 = (bf16[256,768]{1,0:T(8,128)(2,1)S(1)}, bf16[256,768]{1,0:T(8,128)(2,1)S(1)}, u32[]{:S(2)}, u32[]{:S(2)}) collective-permute-start(bf16[256,768]{1,0:T(8,128)(2,1)S(1)} %get-tuple-element.55), channel_id=1, source_target_pairs={{0,64},{4,68},{8,72},{12,76},{16,80},{20,84},{24,88},{28,92},{32,9... | collective-permute-start | bytes 1179656 | tf_op jit(solution)/shard_map/ppermute | solution.py:539
  89.3 3.7 %shard_map.98 = (bf16[256,768]{1,0:T(8,128)(2,1)S(1)}, bf16[256,768]{1,0:T(8,128)(2,1)S(1)}, f32[6,128,256]{2,1,0:T(8,128)S(1)}) custom-call(s32[2,11]{1,0:T(2,128)S(1)} %concatenate.3.seen, bf16[256,768]{1,0:T(8,128)(2,1)S(1)} %copy-done, bf16[256,768]{1,0:T(8,128)(2,1)S(1)} %copy-done.1, bf16[256,768]{1,0:T(8,128)(2,1)} %collective-permute-done.3.left.one, ...), custom_call_target="tpu_custom_call" | custom-call | tf_op jit(solution)/shard_map/pallas_call | solution.py:400
  93.0 1.9 %collective-permute-start.10 = (bf16[256,768]{1,0:T(8,128)(2,1)S(1)}, bf16[256,768]{1,0:T(8,128)(2,1)S(1)}, u32[]{:S(2)}, u32[]{:S(2)}) collective-permute-start(bf16[256,768]{1,0:T(8,128)(2,1)S(1)} %get-tuple-element.60), channel_id=1, source_target_pairs={{0,4},{4,8},{8,12},{12,16},{16,20},{20,24},{24,28},{28,32},{32,36}... | collective-permute-start | bytes 1179656 | tf_op jit(solution)/shard_map/ppermute | solution.py:545
  94.9 8.4 %collective-permute-start.11 = (bf16[256,768]{1,0:T(8,128)(2,1)S(1)}, bf16[256,768]{1,0:T(8,128)(2,1)S(1)}, u32[]{:S(2)}, u32[]{:S(2)}) collective-permute-start(bf16[256,768]{1,0:T(8,128)(2,1)S(1)} %get-tuple-element.61), channel_id=1, source_target_pairs={{4,0},{8,4},{12,8},{16,12},{20,16},{24,20},{28,24},{32,28},{36,32}... | collective-permute-start | bytes 1179656 | tf_op jit(solution)/shard_map/ppermute | solution.py:545
  103.4 2.4 %shard_map.99 = (bf16[256,768]{1,0:T(8,128)(2,1)S(1)}, bf16[256,768]{1,0:T(8,128)(2,1)S(1)}, f32[6,128,256]{2,1,0:T(8,128)S(1)}) custom-call(s32[2,11]{1,0:T(2,128)S(1)} %concatenate.3.seen, bf16[256,768]{1,0:T(8,128)(2,1)S(1)} %copy-done, bf16[256,768]{1,0:T(8,128)(2,1)S(1)} %copy-done.1, bf16[256,768]{1,0:T(8,128)(2,1)S(1)} %collective-permute-done.5.far0.one, ...), custom_call_target="tpu_custom_call" | custom-call | tf_op jit(solution)/shard_map/pallas_call | solution.py:400
  105.8 4.6 %collective-permute-start.12 = (bf16[256,768]{1,0:T(8,128)(2,1)S(1)}, bf16[256,768]{1,0:T(8,128)(2,1)S(1)}, u32[]{:S(2)}, u32[]{:S(2)}) collective-permute-start(bf16[256,768]{1,0:T(8,128)(2,1)S(1)} %get-tuple-element.62), channel_id=1, source_target_pairs={{0,256},{4,260},{8,264},{12,268},{16,272},{20,276},{24,280},{28,28... | collective-permute-start | bytes 1179656 | tf_op jit(solution)/shard_map/ppermute | solution.py:539
  110.4 1.9 %collective-permute-start.13 = (bf16[256,768]{1,0:T(8,128)(2,1)S(1)}, bf16[256,768]{1,0:T(8,128)(2,1)S(1)}, u32[]{:S(2)}, u32[]{:S(2)}) collective-permute-start(bf16[256,768]{1,0:T(8,128)(2,1)S(1)} %get-tuple-element.63), channel_id=1, source_target_pairs={{0,128},{4,132},{8,136},{12,140},{16,144},{20,148},{24,152},{28,15... | collective-permute-start | bytes 1179656 | tf_op jit(solution)/shard_map/ppermute | solution.py:539
  112.3 4.4 %shard_map.100 = (bf16[256,768]{1,0:T(8,128)(2,1)}, bf16[256,768]{1,0:T(8,128)(2,1)}, f32[256,768]{1,0:T(8,128)S(1)}, f32[256,768]{1,0:T(8,128)S(1)}) custom-call(s32[2,11]{1,0:T(2,128)S(1)} %concatenate.3.seen, bf16[256,768]{1,0:T(8,128)(2,1)S(1)} %copy-done, bf16[256,768]{1,0:T(8,128)(2,1)S(1)} %copy-done.1, bf16[512,768]{1,0:T(8,128)(2,1)S(1)} %get-tuple-element.35.whole, ...), custom_call_target="tpu_custom_call" | custom-call | tf_op jit(solution)/shard_map/pallas_call | solution.py:400
  116.7 7.3 %collective-permute-done.9.far2 = bf16[256,768]{1,0:T(8,128)(2,1)S(1)} collective-permute-done((bf16[256,768]{1,0:T(8,128)(2,1)S(1)}, bf16[256,768]{1,0:T(8,128)(2,1)S(1)}, u32[]{:S(2)}, u32[]{:S(2)}) %collective-permute-start.9) | collective-permute-done | bytes 393248 | tf_op jit(solution)/shard_map/ppermute | solution.py:539
  124.7 5.1 %collective-permute-done.10.low_block = bf16[256,768]{1,0:T(8,128)(2,1)S(1)} collective-permute-done((bf16[256,768]{1,0:T(8,128)(2,1)S(1)}, bf16[256,768]{1,0:T(8,128)(2,1)S(1)}, u32[]{:S(2)}, u32[]{:S(2)}) %collective-permute-start.10) | collective-permute-done | bytes 393248 | tf_op jit(solution)/shard_map/ppermute | solution.py:545
  129.8 5.5 %collective-permute-done.13.far1 = bf16[256,768]{1,0:T(8,128)(2,1)S(1)} collective-permute-done((bf16[256,768]{1,0:T(8,128)(2,1)S(1)}, bf16[256,768]{1,0:T(8,128)(2,1)S(1)}, u32[]{:S(2)}, u32[]{:S(2)}) %collective-permute-start.13) | collective-permute-done | bytes 393248 | tf_op jit(solution)/shard_map/ppermute | solution.py:539
  135.3 1.7 %shard_map.102 = (bf16[256,768]{1,0:T(8,128)(2,1)}, bf16[256,768]{1,0:T(8,128)(2,1)}) custom-call(s32[1,3]{1,0:T(1,128)S(1)} %copy-done.5, f32[256,768]{1,0:T(8,128)S(1)} %get-tuple-element.58.key_sum, f32[256,768]{1,0:T(8,128)S(1)} %get-tuple-element.59.value_sum, bf16[256,768]{1,0:T(8,128)(2,1)S(1)} %collective-permute-done.10.low_block, ...), custom_call_target="tpu_custom_call" | custom-call | tf_op jit(solution)/shard_map/pallas_call | solution.py:400
  (32 shorter events, 12.0 us)
Async XLA Ops:
  0.6 1.0 copy-start.2
  1.6 1.0 copy-start.3
  2.6 0.7 copy-start.4
  4.9 31.3 %collective-permute-start.2 = (bf16[512,768]{1,0:T(8,128)(2,1)S(1)}, bf16[512,768]{1,0:T(8,128)(2,1)S(1)}, u32[]{:S(2)}, u32[]{:S(2)}) collective-permute-start(bf16[512,768]{1,0:T(8,128)(2,1)S(1)} %get-tuple-element.35.whole), channel_id=1, source_target_pairs={{1,2},{2,1},{5,6},{6,5},{9,10},{10,9},{13,14},{14,13},{17,18},{18,... | collective-permute-start | bytes 2359304 | tf_op jit(solution)/shard_map/ppermute | solution.py:533
  6.8 29.4 %collective-permute-start.1 = (bf16[512,768]{1,0:T(8,128)(2,1)S(1)}, bf16[512,768]{1,0:T(8,128)(2,1)S(1)}, u32[]{:S(2)}, u32[]{:S(2)}) collective-permute-start(bf16[512,768]{1,0:T(8,128)(2,1)S(1)} %get-tuple-element.35.whole), channel_id=1, source_target_pairs={{0,1},{1,0},{2,3},{3,2},{4,5},{5,4},{6,7},{7,6},{8,9},{9,8},{10,11... | collective-permute-start | bytes 2359304 | tf_op jit(solution)/shard_map/ppermute | solution.py:532
  8.7 41.1 %collective-permute-start = (bf16[256,768]{1,0:T(8,128)(2,1)}, bf16[256,768]{1,0:T(8,128)(2,1)}, u32[]{:S(2)}, u32[]{:S(2)}) collective-permute-start(bf16[256,768]{1,0:T(8,128)(2,1)} %get-tuple-element.36), channel_id=1, source_target_pairs={{0,64},{4,68},{8,72},{12,76},{16,80},{20,84},{24,88},{28,92},{32,9... | collective-permute-start | bytes 1179656 | tf_op jit(solution)/shard_map/ppermute | solution.py:539
  24.5 44.0 %collective-permute-start.3 = (bf16[256,768]{1,0:T(8,128)(2,1)}, bf16[256,768]{1,0:T(8,128)(2,1)}, u32[]{:S(2)}, u32[]{:S(2)}) collective-permute-start(bf16[256,768]{1,0:T(8,128)(2,1)} %get-tuple-element.37), channel_id=1, source_target_pairs={{0,4},{4,8},{8,12},{12,16},{16,20},{20,24},{24,28},{28,32},{32,36}... | collective-permute-start | bytes 1179656 | tf_op jit(solution)/shard_map/ppermute | solution.py:545
  28.8 39.8 %collective-permute-start.4 = (bf16[256,768]{1,0:T(8,128)(2,1)}, bf16[256,768]{1,0:T(8,128)(2,1)}, u32[]{:S(2)}, u32[]{:S(2)}) collective-permute-start(bf16[256,768]{1,0:T(8,128)(2,1)} %get-tuple-element.38), channel_id=1, source_target_pairs={{4,0},{8,4},{12,8},{16,12},{20,16},{24,20},{28,24},{32,28},{36,32}... | collective-permute-start | bytes 1179656 | tf_op jit(solution)/shard_map/ppermute | solution.py:545
  34.8 0.7 copy-start.6
  36.2 0.7 copy-start.5
  36.2 11.1 %copy-start = (bf16[256,768]{1,0:T(8,128)(2,1)S(1)}, bf16[256,768]{1,0:T(8,128)(2,1)}, u32[]{:S(2)}) copy-start(bf16[256,768]{1,0:T(8,128)(2,1)} %query.11) | copy-start | bytes 1179652
  36.2 11.1 %copy-start.1 = (bf16[256,768]{1,0:T(8,128)(2,1)S(1)}, bf16[256,768]{1,0:T(8,128)(2,1)}, u32[]{:S(2)}) copy-start(bf16[256,768]{1,0:T(8,128)(2,1)} %upward.9) | copy-start | bytes 1179652
  38.3 30.2 %collective-permute-start.5 = (bf16[256,768]{1,0:T(8,128)(2,1)}, bf16[256,768]{1,0:T(8,128)(2,1)S(1)}, u32[]{:S(2)}, u32[]{:S(2)}) collective-permute-start(bf16[256,768]{1,0:T(8,128)(2,1)} %get-tuple-element.39), channel_id=1, source_target_pairs={{0,256},{4,260},{8,264},{12,268},{16,272},{20,276},{24,280},{28,28... | collective-permute-start | bytes 1179656 | tf_op jit(solution)/shard_map/ppermute | solution.py:539
  42.5 27.0 %collective-permute-start.6 = (bf16[256,768]{1,0:T(8,128)(2,1)}, bf16[256,768]{1,0:T(8,128)(2,1)}, u32[]{:S(2)}, u32[]{:S(2)}) collective-permute-start(bf16[256,768]{1,0:T(8,128)(2,1)} %get-tuple-element.40), channel_id=1, source_target_pairs={{0,128},{4,132},{8,136},{12,140},{16,144},{20,148},{24,152},{28,15... | collective-permute-start | bytes 1179656 | tf_op jit(solution)/shard_map/ppermute | solution.py:539
  74.0 29.4 %collective-permute-start.7 = (bf16[512,768]{1,0:T(8,128)(2,1)S(1)}, bf16[512,768]{1,0:T(8,128)(2,1)S(1)}, u32[]{:S(2)}, u32[]{:S(2)}) collective-permute-start(bf16[512,768]{1,0:T(8,128)(2,1)S(1)} %get-tuple-element.46), channel_id=1, source_target_pairs={{0,1},{1,0},{2,3},{3,2},{4,5},{5,4},{6,7},{7,6},{8,9},{9,8},{10,11... | collective-permute-start | bytes 2359304 | tf_op jit(solution)/shard_map/ppermute | solution.py:532
  75.9 27.5 %collective-permute-start.8 = (bf16[512,768]{1,0:T(8,128)(2,1)S(1)}, bf16[512,768]{1,0:T(8,128)(2,1)S(1)}, u32[]{:S(2)}, u32[]{:S(2)}) collective-permute-start(bf16[512,768]{1,0:T(8,128)(2,1)S(1)} %get-tuple-element.47), channel_id=1, source_target_pairs={{1,2},{2,1},{5,6},{6,5},{9,10},{10,9},{13,14},{14,13},{17,18},{18,... | collective-permute-start | bytes 2359304 | tf_op jit(solution)/shard_map/ppermute | solution.py:533
  80.4 43.5 %collective-permute-start.9 = (bf16[256,768]{1,0:T(8,128)(2,1)S(1)}, bf16[256,768]{1,0:T(8,128)(2,1)S(1)}, u32[]{:S(2)}, u32[]{:S(2)}) collective-permute-start(bf16[256,768]{1,0:T(8,128)(2,1)S(1)} %get-tuple-element.55), channel_id=1, source_target_pairs={{0,64},{4,68},{8,72},{12,76},{16,80},{20,84},{24,88},{28,92},{32,9... | collective-permute-start | bytes 1179656 | tf_op jit(solution)/shard_map/ppermute | solution.py:539
  93.0 36.8 %collective-permute-start.10 = (bf16[256,768]{1,0:T(8,128)(2,1)S(1)}, bf16[256,768]{1,0:T(8,128)(2,1)S(1)}, u32[]{:S(2)}, u32[]{:S(2)}) collective-permute-start(bf16[256,768]{1,0:T(8,128)(2,1)S(1)} %get-tuple-element.60), channel_id=1, source_target_pairs={{0,4},{4,8},{8,12},{12,16},{16,20},{20,24},{24,28},{28,32},{32,36}... | collective-permute-start | bytes 1179656 | tf_op jit(solution)/shard_map/ppermute | solution.py:545
  94.9 34.9 %collective-permute-start.11 = (bf16[256,768]{1,0:T(8,128)(2,1)S(1)}, bf16[256,768]{1,0:T(8,128)(2,1)S(1)}, u32[]{:S(2)}, u32[]{:S(2)}) collective-permute-start(bf16[256,768]{1,0:T(8,128)(2,1)S(1)} %get-tuple-element.61), channel_id=1, source_target_pairs={{4,0},{8,4},{12,8},{16,12},{20,16},{24,20},{28,24},{32,28},{36,32}... | collective-permute-start | bytes 1179656 | tf_op jit(solution)/shard_map/ppermute | solution.py:545
  105.8 24.0 %collective-permute-start.12 = (bf16[256,768]{1,0:T(8,128)(2,1)S(1)}, bf16[256,768]{1,0:T(8,128)(2,1)S(1)}, u32[]{:S(2)}, u32[]{:S(2)}) collective-permute-start(bf16[256,768]{1,0:T(8,128)(2,1)S(1)} %get-tuple-element.62), channel_id=1, source_target_pairs={{0,256},{4,260},{8,264},{12,268},{16,272},{20,276},{24,280},{28,28... | collective-permute-start | bytes 1179656 | tf_op jit(solution)/shard_map/ppermute | solution.py:539
  110.4 25.0 %collective-permute-start.13 = (bf16[256,768]{1,0:T(8,128)(2,1)S(1)}, bf16[256,768]{1,0:T(8,128)(2,1)S(1)}, u32[]{:S(2)}, u32[]{:S(2)}) collective-permute-start(bf16[256,768]{1,0:T(8,128)(2,1)S(1)} %get-tuple-element.63), channel_id=1, source_target_pairs={{0,128},{4,132},{8,136},{12,140},{16,144},{20,148},{24,152},{28,15... | collective-permute-start | bytes 1179656 | tf_op jit(solution)/shard_map/ppermute | solution.py:539

commit v6 on v4

--- a/solution.py
+++ b/solution.py
@@ -130,8 +130,8 @@
     return [range(first, first + GROUP) for first in range(0, PAIRS, GROUP)]
 
 
-def own_slots(key, value):
-    return [(b, key, b * BLK, value, b * BLK) for b in range(BW)]
+def own_slots(whole):
+    return [(b, whole, b * BLK, whole, ROWS + b * BLK) for b in range(BW)]
 
 
 def side_slots(chip, cross):
@@ -195,14 +195,14 @@
     lax.fori_loop(0, count, step, 0)
 
 
-def first_kernel(seen, query, upward, key, value, chip, cross, stat, acc, upward_t, held, place):
+def first_kernel(seen, query, upward, whole, chip, cross, stat, acc, upward_t, held, place):
     for pair in range(PAIRS):
         stat[pair, 0:2, :] = jnp.full((2, ROWS), HIDDEN, f32)
         stat[pair, 2:4, :] = jnp.zeros((2, ROWS), f32)
         acc[pair] = jnp.zeros((BLK, ROWS), f32)
         upward_t[pair] = upward[:, feature(pair)].astype(f32).T
     forward_over(
-        own_slots(key, value) + side_slots(chip, cross), seen, query, stat, acc, held, place
+        own_slots(whole) + side_slots(chip, cross), seen, query, stat, acc, held, place
     )
 
 
@@ -262,10 +262,10 @@
     upward,
     chip,
     cross,
+    far0,
+    far1,
     left,
     right,
-    far0,
-    far1,
     stat_in,
     acc_in,
     upward_t,
@@ -350,8 +350,7 @@
     seen,
     query,
     upward,
-    key,
-    value,
+    whole,
     chip_back,
     cross_back,
     stat,
@@ -384,7 +383,7 @@
                     )
 
     backward_over(
-        own_slots(key, value), seen, query, upward, stat, query_t, held, place, terms, store
+        own_slots(whole), seen, query, upward, stat, query_t, held, place, terms, store
     )
     for pair in range(PAIRS):
         query_grad[:, feature(pair)] = (query_t[pair] * SCALE).T.astype(bf16)
@@ -438,35 +437,32 @@
 SIDE = shape((2 * ROWS, D), bf16)
 
 
-def block_of(key, value, start, out):
-    rows = pl.ds(pl.multiple_of(start, BLK), BLK)
-    out[0:BLK] = key[rows]
-    out[BLK : 2 * BLK] = value[rows]
+def block_of(whole, start, out):
+    for half in range(2):
+        rows = pl.ds(pl.multiple_of(half * ROWS + start, BLK), BLK)
+        out[half * BLK : (half + 1) * BLK] = whole[rows]
 
 
 def pack_first_kernel(pick, key, value, far2, whole):
-    block_of(key, value, pick[0, 2] * BLK, far2)
     whole[0:ROWS] = key[...]
     whole[ROWS : 2 * ROWS] = value[...]
-
-
-def pack_rest_kernel(pick, chip, cross, key, value, right, left, far0, far1):
-    block_of(key, value, 0, right)
-    block_of(key, value, ROWS - BLK, left)
-    block_of(key, value, pick[0, 0] * BLK, far0)
-    block_of(key, value, pick[0, 1] * BLK, far1)
+    block_of(whole, pick[0, 2] * BLK, far2)
+
+
+def pack_rest_kernel(pick, chip, cross, whole, right, left, far0, far1):
+    block_of(whole, 0, right)
+    block_of(whole, ROWS - BLK, left)
+    block_of(whole, pick[0, 0] * BLK, far0)
+    block_of(whole, pick[0, 1] * BLK, far1)
 
 
 def pack_first(pick, key, value):
     return call(pack_first_kernel, [RIM, SIDE], [smem(), vmem(), vmem()], (pick, key, value))
 
 
-def pack_rest(pick, chip, cross, key, value):
+def pack_rest(pick, chip, cross, whole):
     return call(
-        pack_rest_kernel,
-        [RIM] * 4,
-        [smem(), hbm(), hbm(), vmem(), vmem()],
-        (pick, chip, cross, key, value),
+        pack_rest_kernel, [RIM] * 4, [smem(), hbm(), hbm(), vmem()], (pick, chip, cross, whole)
     )
 
 
@@ -474,12 +470,12 @@
     return [pltpu.VMEM((slots, 2 * BLK, D), bf16), pltpu.SMEM((16,), jnp.int32)]
 
 
-def run_first(plan, queries, upstream, *near):
+def run_first(plan, *rest):
     return call(
         first_kernel,
         STATE + [shape((PAIRS, BLK, ROWS), f32)],
-        [smem()] + [vmem()] * 6,
-        (plan, queries, upstream, *near),
+        [smem()] + [vmem()] * 5,
+        (plan, *rest),
         scratch=seen_scratch(6),
     )
 
@@ -521,7 +517,7 @@
     return call(
         own_kernel,
         [whole, whole, total, total],
-        [smem()] + [vmem()] * 9,
+        [smem()] + [vmem()] * 8,
         (plan, *rest),
         scratch=[pltpu.VMEM((PAIRS, BLK, ROWS), f32), pltpu.VMEM((2 * BLK, D), bf16)]
         + seen_scratch(2),
@@ -587,26 +583,24 @@
     chip, cross = sides(whole, whole)
     far2 = partner(far2_pair, top_bit - EXP)
     right_pair, left_pair, far0_pair, far1_pair = pack_rest(
-        expander_pick, chip, cross, key_rows, value_rows
-    )
-    rest = (
-        shift(left_pair, "wide", 1),
-        shift(right_pair, "wide", -1),
-        partner(far0_pair, top_bit - 1),
-        partner(far1_pair, top_bit - 2),
-    )
-    stat, acc, upward_t = run_first(plan, queries, upstream, key_rows, value_rows, chip, cross)
+        expander_pick, chip, cross, whole
+    )
+    far0 = partner(far0_pair, top_bit - 1)
+    far1 = partner(far1_pair, top_bit - 2)
+    left = shift(left_pair, "wide", 1)
+    right = shift(right_pair, "wide", -1)
+    stat, acc, upward_t = run_first(plan, queries, upstream, whole, chip, cross)
     stat, acc = run_far(far2, plan, queries, stat, acc)
     stat, out_t, query_t, far2_term, chip_term, cross_term = run_middle(
-        far2, plan, queries, upstream, chip, cross, *rest, stat, acc, upward_t
+        far2, plan, queries, upstream, chip, cross, far0, far1, left, right, stat, acc, upward_t
     )
     far2_back = partner(far2_term, top_bit - EXP)
     back = sides(chip_term, cross_term)
     left_term, right_term, far0_term, far1_term, query_t = run_rest(
-        plan, queries, upstream, *rest, *back, stat, query_t
+        plan, queries, upstream, left, right, far0, far1, *back, stat, query_t
     )
     attention, query_grad, key_near, value_near = run_own(
-        plan, queries, upstream, key_rows, value_rows, *back, stat, out_t, query_t
+        plan, queries, upstream, whole, *back, stat, out_t, query_t
     )
     key_sum, value_sum = run_first_sum(far2_back, expander_pick, key_near, value_near)
     key_grad, value_grad = run_second_sum(

time: 135 us -> 135 us (level); the launches traced: 134 us -> 133 us
  waiting for transfers between devices: 38.4 us -> 36.5 us
    ppermute x4, starting transfers between devices: 19.8 us -> 22.3 us  [shift(): return lax.ppermute(value, axis, pairs)]
    ppermute x6, starting transfers between devices: 37.5 us -> 35.4 us  [partner(): lax.ppermute(value, 'wide', [(s, s ^ mask) for s in range(lax.axis_size('...]
    ppermute x4, waiting for transfers between devices: 32.8 us -> 31.4 us  [shift(): return lax.ppermute(value, axis, pairs)]
    ppermute x6, waiting for transfers between devices: 4.65 us -> 3.27 us  [partner(): lax.ppermute(value, 'wide', [(s, s ^ mask) for s in range(lax.axis_size('...]
    unnamed x18 -> x14, local copies, waits for them, and re-layouts: 3.94 us -> 3.95 us
  transfers between devices with their start and end apart: 14 -> 14, of which waited for: 4 -> 5; matrix products, arithmetic and copies ran while one was open for 2% -> 2% of each run, Pallas kernels for 10% -> 11%
where the time goes in v6:
time: 135 us; the launch traced here: 133 us
  starting transfers between devices  68.4 us (51%)
  waiting for transfers between devices  36.5 us (27%)
  Pallas kernels  20.6 us (15%)
  local copies, waits for them, and re-layouts  5.37 us (4%)
    ppermute x6, starting transfers between devices, partner(): lax.ppermute(value, 'wide', [(s, s ^ mask) for s in range(lax.axis_size('...  35.4 us
    ppermute x4, waiting for transfers between devices, shift(): return lax.ppermute(value, axis, pairs)  31.4 us
    ppermute x4, starting transfers between devices, shift(): return lax.ppermute(value, axis, pairs)  22.3 us
    pallas_call x9, Pallas kernels, call(): pl.pallas_call(kernel, out_shape=shapes, in_specs=specs, out_specs=outs i...  20.6 us
    ppermute x2, starting transfers between devices, sides(): lax.ppermute(cross, 'narrow', across + [(b, a) for a, b in across])  5.59 us
    ppermute x2, starting transfers between devices, sides(): lax.ppermute(chip, 'narrow', [(i, i ^ 1) for i in range(count)])  5.17 us
    unnamed x14, local copies, waits for them, and re-layouts  3.95 us
    ppermute x6, waiting for transfers between devices, partner(): lax.ppermute(value, 'wide', [(s, s ^ mask) for s in range(lax.axis_size('...  3.27 us
  transfers between devices with their start and end apart: 14, of which 5 were waited for; matrix products, arithmetic and copies ran while one was open for 2% of the time, Pallas kernels for 11%

profile of v6, /device:TPU:25, one launch (start us, length us, event | category | flops | bytes accessed | tf_op | source)
XLA Modules:
  0.0 132.5 jit_solution(11983311489593310748)
XLA Ops:
  4.6 3.7 %collective-permute-start.2 = (bf16[512,768]{1,0:T(8,128)(2,1)S(1)}, bf16[512,768]{1,0:T(8,128)(2,1)S(1)}, u32[]{:S(2)}, u32[]{:S(2)}) collective-permute-start(bf16[512,768]{1,0:T(8,128)(2,1)S(1)} %get-tuple-element.34.whole), channel_id=1, source_target_pairs={{1,2},{2,1},{5,6},{6,5},{9,10},{10,9},{13,14},{14,13},{17,18},{18,... | collective-permute-start | bytes 2359304 | tf_op jit(solution)/shard_map/ppermute | solution.py:544
  8.3 1.9 %collective-permute-start.1 = (bf16[512,768]{1,0:T(8,128)(2,1)S(1)}, bf16[512,768]{1,0:T(8,128)(2,1)S(1)}, u32[]{:S(2)}, u32[]{:S(2)}) collective-permute-start(bf16[512,768]{1,0:T(8,128)(2,1)S(1)} %get-tuple-element.34.whole), channel_id=1, source_target_pairs={{0,1},{1,0},{2,3},{3,2},{4,5},{5,4},{6,7},{7,6},{8,9},{9,8},{10,11... | collective-permute-start | bytes 2359304 | tf_op jit(solution)/shard_map/ppermute | solution.py:543
  10.2 15.4 %collective-permute-start = (bf16[256,768]{1,0:T(8,128)(2,1)}, bf16[256,768]{1,0:T(8,128)(2,1)S(1)}, u32[]{:S(2)}, u32[]{:S(2)}) collective-permute-start(bf16[256,768]{1,0:T(8,128)(2,1)} %get-tuple-element.35), channel_id=1, source_target_pairs={{0,64},{4,68},{8,72},{12,76},{16,80},{20,84},{24,88},{28,92},{32,9... | collective-permute-start | bytes 1179656 | tf_op jit(solution)/shard_map/ppermute | solution.py:550
  27.7 1.8 %shard_map.94 = (bf16[256,768]{1,0:T(8,128)(2,1)}, bf16[256,768]{1,0:T(8,128)(2,1)}, bf16[256,768]{1,0:T(8,128)(2,1)}, bf16[256,768]{1,0:T(8,128)(2,1)}) custom-call(s32[1,3]{1,0:T(1,128)S(1)} %copy-done.5, bf16[512,768]{1,0:T(8,128)(2,1)S(1)} %collective-permute-done.1.chip, bf16[512,768]{1,0:T(8,128)(2,1)S(1)} %collective-permute-done.2.cross, ...), custom_call_target="tpu_custom_call" | custom-call | tf_op jit(solution)/shard_map/pallas_call | solution.py:416
  29.5 2.9 %collective-permute-start.3 = (bf16[256,768]{1,0:T(8,128)(2,1)}, bf16[256,768]{1,0:T(8,128)(2,1)}, u32[]{:S(2)}, u32[]{:S(2)}) collective-permute-start(bf16[256,768]{1,0:T(8,128)(2,1)} %get-tuple-element.36), channel_id=1, source_target_pairs={{0,256},{4,260},{8,264},{12,268},{16,272},{20,276},{24,280},{28,28... | collective-permute-start | bytes 1179656 | tf_op jit(solution)/shard_map/ppermute | solution.py:550
  32.3 1.9 %collective-permute-start.4 = (bf16[256,768]{1,0:T(8,128)(2,1)}, bf16[256,768]{1,0:T(8,128)(2,1)}, u32[]{:S(2)}, u32[]{:S(2)}) collective-permute-start(bf16[256,768]{1,0:T(8,128)(2,1)} %get-tuple-element.37), channel_id=1, source_target_pairs={{0,128},{4,132},{8,136},{12,140},{16,144},{20,148},{24,152},{28,15... | collective-permute-start | bytes 1179656 | tf_op jit(solution)/shard_map/ppermute | solution.py:550
  34.3 4.4 %collective-permute-start.5 = (bf16[256,768]{1,0:T(8,128)(2,1)}, bf16[256,768]{1,0:T(8,128)(2,1)}, u32[]{:S(2)}, u32[]{:S(2)}) collective-permute-start(bf16[256,768]{1,0:T(8,128)(2,1)} %get-tuple-element.38), channel_id=1, source_target_pairs={{0,4},{4,8},{8,12},{12,16},{16,20},{20,24},{24,28},{28,32},{32,36}... | collective-permute-start | bytes 1179656 | tf_op jit(solution)/shard_map/ppermute | solution.py:556
  38.6 5.4 %collective-permute-start.6 = (bf16[256,768]{1,0:T(8,128)(2,1)}, bf16[256,768]{1,0:T(8,128)(2,1)}, u32[]{:S(2)}, u32[]{:S(2)}) collective-permute-start(bf16[256,768]{1,0:T(8,128)(2,1)} %get-tuple-element.39), channel_id=1, source_target_pairs={{4,0},{8,4},{12,8},{16,12},{20,16},{24,20},{28,24},{32,28},{36,32}... | collective-permute-start | bytes 1179656 | tf_op jit(solution)/shard_map/ppermute | solution.py:556
  45.6 2.5 %shard_map.95 = (f32[6,8,256]{2,1,0:T(8,128)S(1)}, f32[6,128,256]{2,1,0:T(8,128)S(1)}, f32[6,128,256]{2,1,0:T(8,128)S(1)}) custom-call(s32[2,11]{1,0:T(2,128)S(1)} %concatenate.3.seen, bf16[256,768]{1,0:T(8,128)(2,1)S(1)} %copy-done, bf16[256,768]{1,0:T(8,128)(2,1)S(1)} %copy-done.1, bf16[512,768]{1,0:T(8,128)(2,1)S(1)} %get-tuple-element.34.whole, ...), custom_call_target="tpu_custom_call" | custom-call | tf_op jit(solution)/shard_map/pallas_call | solution.py:416
  49.1 21.0 %collective-permute-done.5.left = bf16[256,768]{1,0:T(8,128)(2,1)} collective-permute-done((bf16[256,768]{1,0:T(8,128)(2,1)}, bf16[256,768]{1,0:T(8,128)(2,1)}, u32[]{:S(2)}, u32[]{:S(2)}) %collective-permute-start.5) | collective-permute-done | bytes 393248 | tf_op jit(solution)/shard_map/ppermute | solution.py:556
  70.1 3.6 %shard_map.97 = (f32[6,8,256]{2,1,0:T(8,128)S(1)}, bf16[6,128,256]{2,1,0:T(8,128)(2,1)S(1)}, f32[6,128,256]{2,1,0:T(8,128)S(1)}, bf16[256,768]{1,0:T(8,128)(2,1)...) custom-call(bf16[256,768]{1,0:T(8,128)(2,1)S(1)} %collective-permute-done.far2, ...), custom_call_target="tpu_custom_call" | custom-call | tf_op jit(solution)/shard_map/pallas_call | solution.py:416
  73.7 3.2 %collective-permute-start.7 = (bf16[512,768]{1,0:T(8,128)(2,1)S(1)}, bf16[512,768]{1,0:T(8,128)(2,1)S(1)}, u32[]{:S(2)}, u32[]{:S(2)}) collective-permute-start(bf16[512,768]{1,0:T(8,128)(2,1)S(1)} %get-tuple-element.45), channel_id=1, source_target_pairs={{0,1},{1,0},{2,3},{3,2},{4,5},{5,4},{6,7},{7,6},{8,9},{9,8},{10,11... | collective-permute-start | bytes 2359304 | tf_op jit(solution)/shard_map/ppermute | solution.py:543
  76.9 1.9 %collective-permute-start.8 = (bf16[512,768]{1,0:T(8,128)(2,1)S(1)}, bf16[512,768]{1,0:T(8,128)(2,1)S(1)}, u32[]{:S(2)}, u32[]{:S(2)}) collective-permute-start(bf16[512,768]{1,0:T(8,128)(2,1)S(1)} %get-tuple-element.46), channel_id=1, source_target_pairs={{1,2},{2,1},{5,6},{6,5},{9,10},{10,9},{13,14},{14,13},{17,18},{18,... | collective-permute-start | bytes 2359304 | tf_op jit(solution)/shard_map/ppermute | solution.py:544
  78.9 9.6 %collective-permute-start.9 = (bf16[256,768]{1,0:T(8,128)(2,1)S(1)}, bf16[256,768]{1,0:T(8,128)(2,1)S(1)}, u32[]{:S(2)}, u32[]{:S(2)}) collective-permute-start(bf16[256,768]{1,0:T(8,128)(2,1)S(1)} %get-tuple-element.53), channel_id=1, source_target_pairs={{0,64},{4,68},{8,72},{12,76},{16,80},{20,84},{24,88},{28,92},{32,9... | collective-permute-start | bytes 1179656 | tf_op jit(solution)/shard_map/ppermute | solution.py:550
  88.5 1.7 %collective-permute-done.8.cross_back = bf16[512,768]{1,0:T(8,128)(2,1)S(1)} collective-permute-done((bf16[512,768]{1,0:T(8,128)(2,1)S(1)}, bf16[512,768]{1,0:T(8,128)(2,1)S(1)}, u32[]{:S(2)}, u32[]{:S(2)}) %collective-permute-start.8) | collective-permute-done | bytes 786464 | tf_op jit(solution)/shard_map/ppermute | solution.py:544
  90.2 4.0 %shard_map.98 = (bf16[256,768]{1,0:T(8,128)(2,1)S(1)}, bf16[256,768]{1,0:T(8,128)(2,1)S(1)}, bf16[256,768]{1,0:T(8,128)(2,1)S(1)}, bf16[256,768]{1,0:T(8,128)(2,1)S(1)}, f32[6,128,256]{2,1,0:T(8,128)S(1)}) custom-call(s32[2,11]{1,0:T(2,128)S(1)} %concatenate.3.seen, bf16[256,768]{1,0:T(8,128)(2,1)S(1)} %copy-done, bf16[256,768]{1,0:T(8,128)(2,1)S(1)} %copy-done.1, ...), custom_call_target="tpu_custom_call" | custom-call | tf_op jit(solution)/shard_map/pallas_call | solution.py:416
  94.3 3.6 %collective-permute-start.10 = (bf16[256,768]{1,0:T(8,128)(2,1)S(1)}, bf16[256,768]{1,0:T(8,128)(2,1)S(1)}, u32[]{:S(2)}, u32[]{:S(2)}) collective-permute-start(bf16[256,768]{1,0:T(8,128)(2,1)S(1)} %get-tuple-element.58), channel_id=1, source_target_pairs={{0,256},{4,260},{8,264},{12,268},{16,272},{20,276},{24,280},{28,28... | collective-permute-start | bytes 1179656 | tf_op jit(solution)/shard_map/ppermute | solution.py:550
  97.9 1.9 %collective-permute-start.11 = (bf16[256,768]{1,0:T(8,128)(2,1)S(1)}, bf16[256,768]{1,0:T(8,128)(2,1)S(1)}, u32[]{:S(2)}, u32[]{:S(2)}) collective-permute-start(bf16[256,768]{1,0:T(8,128)(2,1)S(1)} %get-tuple-element.59), channel_id=1, source_target_pairs={{0,128},{4,132},{8,136},{12,140},{16,144},{20,148},{24,152},{28,15... | collective-permute-start | bytes 1179656 | tf_op jit(solution)/shard_map/ppermute | solution.py:550
  99.8 6.6 %collective-permute-start.12 = (bf16[256,768]{1,0:T(8,128)(2,1)S(1)}, bf16[256,768]{1,0:T(8,128)(2,1)S(1)}, u32[]{:S(2)}, u32[]{:S(2)}) collective-permute-start(bf16[256,768]{1,0:T(8,128)(2,1)S(1)} %get-tuple-element.60), channel_id=1, source_target_pairs={{0,4},{4,8},{8,12},{12,16},{16,20},{20,24},{24,28},{28,32},{32,36}... | collective-permute-start | bytes 1179656 | tf_op jit(solution)/shard_map/ppermute | solution.py:556
  106.4 5.9 %collective-permute-start.13 = (bf16[256,768]{1,0:T(8,128)(2,1)S(1)}, bf16[256,768]{1,0:T(8,128)(2,1)S(1)}, u32[]{:S(2)}, u32[]{:S(2)}) collective-permute-start(bf16[256,768]{1,0:T(8,128)(2,1)S(1)} %get-tuple-element.61), channel_id=1, source_target_pairs={{4,0},{8,4},{12,8},{16,12},{20,16},{24,20},{28,24},{32,28},{36,32}... | collective-permute-start | bytes 1179656 | tf_op jit(solution)/shard_map/ppermute | solution.py:556
  112.3 4.4 %shard_map.99 = (bf16[256,768]{1,0:T(8,128)(2,1)}, bf16[256,768]{1,0:T(8,128)(2,1)}, f32[256,768]{1,0:T(8,128)S(1)}, f32[256,768]{1,0:T(8,128)S(1)}) custom-call(s32[2,11]{1,0:T(2,128)S(1)} %concatenate.3.seen, bf16[256,768]{1,0:T(8,128)(2,1)S(1)} %copy-done, bf16[256,768]{1,0:T(8,128)(2,1)S(1)} %copy-done.1, bf16[512,768]{1,0:T(8,128)(2,1)S(1)} %get-tuple-element.34.whole, ...), custom_call_target="tpu_custom_call" | custom-call | tf_op jit(solution)/shard_map/pallas_call | solution.py:416
  116.7 2.9 %collective-permute-done.9.far2 = bf16[256,768]{1,0:T(8,128)(2,1)S(1)} collective-permute-done((bf16[256,768]{1,0:T(8,128)(2,1)S(1)}, bf16[256,768]{1,0:T(8,128)(2,1)S(1)}, u32[]{:S(2)}, u32[]{:S(2)}) %collective-permute-start.9) | collective-permute-done | bytes 393248 | tf_op jit(solution)/shard_map/ppermute | solution.py:550
  120.3 10.4 %collective-permute-done.12.low_block = bf16[256,768]{1,0:T(8,128)(2,1)S(1)} collective-permute-done((bf16[256,768]{1,0:T(8,128)(2,1)S(1)}, bf16[256,768]{1,0:T(8,128)(2,1)S(1)}, u32[]{:S(2)}, u32[]{:S(2)}) %collective-permute-start.12) | collective-permute-done | bytes 393248 | tf_op jit(solution)/shard_map/ppermute | solution.py:556
  130.8 1.7 %shard_map.101 = (bf16[256,768]{1,0:T(8,128)(2,1)}, bf16[256,768]{1,0:T(8,128)(2,1)}) custom-call(s32[1,3]{1,0:T(1,128)S(1)} %copy-done.5, f32[256,768]{1,0:T(8,128)S(1)} %get-tuple-element.56.key_sum, f32[256,768]{1,0:T(8,128)S(1)} %get-tuple-element.57.value_sum, bf16[256,768]{1,0:T(8,128)(2,1)S(1)} %collective-permute-done.10.far0, ...), custom_call_target="tpu_custom_call" | custom-call | tf_op jit(solution)/shard_map/pallas_call | solution.py:416
  (31 shorter events, 9.2 us)
Async XLA Ops:
  0.6 1.0 copy-start.2
  1.6 1.0 copy-start.3
  2.6 0.7 copy-start.4
  4.6 22.4 %collective-permute-start.2 = (bf16[512,768]{1,0:T(8,128)(2,1)S(1)}, bf16[512,768]{1,0:T(8,128)(2,1)S(1)}, u32[]{:S(2)}, u32[]{:S(2)}) collective-permute-start(bf16[512,768]{1,0:T(8,128)(2,1)S(1)} %get-tuple-element.34.whole), channel_id=1, source_target_pairs={{1,2},{2,1},{5,6},{6,5},{9,10},{10,9},{13,14},{14,13},{17,18},{18,... | collective-permute-start | bytes 2359304 | tf_op jit(solution)/shard_map/ppermute | solution.py:544
  8.3 18.7 %collective-permute-start.1 = (bf16[512,768]{1,0:T(8,128)(2,1)S(1)}, bf16[512,768]{1,0:T(8,128)(2,1)S(1)}, u32[]{:S(2)}, u32[]{:S(2)}) collective-permute-start(bf16[512,768]{1,0:T(8,128)(2,1)S(1)} %get-tuple-element.34.whole), channel_id=1, source_target_pairs={{0,1},{1,0},{2,3},{3,2},{4,5},{5,4},{6,7},{7,6},{8,9},{9,8},{10,11... | collective-permute-start | bytes 2359304 | tf_op jit(solution)/shard_map/ppermute | solution.py:543
  10.2 37.9 %collective-permute-start = (bf16[256,768]{1,0:T(8,128)(2,1)}, bf16[256,768]{1,0:T(8,128)(2,1)S(1)}, u32[]{:S(2)}, u32[]{:S(2)}) collective-permute-start(bf16[256,768]{1,0:T(8,128)(2,1)} %get-tuple-element.35), channel_id=1, source_target_pairs={{0,64},{4,68},{8,72},{12,76},{16,80},{20,84},{24,88},{28,92},{32,9... | collective-permute-start | bytes 1179656 | tf_op jit(solution)/shard_map/ppermute | solution.py:550
  25.7 0.7 copy-start.6
  27.0 0.7 copy-start.5
  27.0 18.6 %copy-start = (bf16[256,768]{1,0:T(8,128)(2,1)S(1)}, bf16[256,768]{1,0:T(8,128)(2,1)}, u32[]{:S(2)}) copy-start(bf16[256,768]{1,0:T(8,128)(2,1)} %query.9) | copy-start | bytes 1179652
  27.0 18.6 %copy-start.1 = (bf16[256,768]{1,0:T(8,128)(2,1)S(1)}, bf16[256,768]{1,0:T(8,128)(2,1)}, u32[]{:S(2)}) copy-start(bf16[256,768]{1,0:T(8,128)(2,1)} %upward.7) | copy-start | bytes 1179652
  29.5 19.3 %collective-permute-start.3 = (bf16[256,768]{1,0:T(8,128)(2,1)}, bf16[256,768]{1,0:T(8,128)(2,1)}, u32[]{:S(2)}, u32[]{:S(2)}) collective-permute-start(bf16[256,768]{1,0:T(8,128)(2,1)} %get-tuple-element.36), channel_id=1, source_target_pairs={{0,256},{4,260},{8,264},{12,268},{16,272},{20,276},{24,280},{28,28... | collective-permute-start | bytes 1179656 | tf_op jit(solution)/shard_map/ppermute | solution.py:550
  32.3 16.8 %collective-permute-start.4 = (bf16[256,768]{1,0:T(8,128)(2,1)}, bf16[256,768]{1,0:T(8,128)(2,1)}, u32[]{:S(2)}, u32[]{:S(2)}) collective-permute-start(bf16[256,768]{1,0:T(8,128)(2,1)} %get-tuple-element.37), channel_id=1, source_target_pairs={{0,128},{4,132},{8,136},{12,140},{16,144},{20,148},{24,152},{28,15... | collective-permute-start | bytes 1179656 | tf_op jit(solution)/shard_map/ppermute | solution.py:550
  34.3 35.8 %collective-permute-start.5 = (bf16[256,768]{1,0:T(8,128)(2,1)}, bf16[256,768]{1,0:T(8,128)(2,1)}, u32[]{:S(2)}, u32[]{:S(2)}) collective-permute-start(bf16[256,768]{1,0:T(8,128)(2,1)} %get-tuple-element.38), channel_id=1, source_target_pairs={{0,4},{4,8},{8,12},{12,16},{16,20},{20,24},{24,28},{28,32},{32,36}... | collective-permute-start | bytes 1179656 | tf_op jit(solution)/shard_map/ppermute | solution.py:556
  38.6 31.5 %collective-permute-start.6 = (bf16[256,768]{1,0:T(8,128)(2,1)}, bf16[256,768]{1,0:T(8,128)(2,1)}, u32[]{:S(2)}, u32[]{:S(2)}) collective-permute-start(bf16[256,768]{1,0:T(8,128)(2,1)} %get-tuple-element.39), channel_id=1, source_target_pairs={{4,0},{8,4},{12,8},{16,12},{20,16},{24,20},{28,24},{32,28},{36,32}... | collective-permute-start | bytes 1179656 | tf_op jit(solution)/shard_map/ppermute | solution.py:556
  73.7 14.8 %collective-permute-start.7 = (bf16[512,768]{1,0:T(8,128)(2,1)S(1)}, bf16[512,768]{1,0:T(8,128)(2,1)S(1)}, u32[]{:S(2)}, u32[]{:S(2)}) collective-permute-start(bf16[512,768]{1,0:T(8,128)(2,1)S(1)} %get-tuple-element.45), channel_id=1, source_target_pairs={{0,1},{1,0},{2,3},{3,2},{4,5},{5,4},{6,7},{7,6},{8,9},{9,8},{10,11... | collective-permute-start | bytes 2359304 | tf_op jit(solution)/shard_map/ppermute | solution.py:543
  76.9 13.3 %collective-permute-start.8 = (bf16[512,768]{1,0:T(8,128)(2,1)S(1)}, bf16[512,768]{1,0:T(8,128)(2,1)S(1)}, u32[]{:S(2)}, u32[]{:S(2)}) collective-permute-start(bf16[512,768]{1,0:T(8,128)(2,1)S(1)} %get-tuple-element.46), channel_id=1, source_target_pairs={{1,2},{2,1},{5,6},{6,5},{9,10},{10,9},{13,14},{14,13},{17,18},{18,... | collective-permute-start | bytes 2359304 | tf_op jit(solution)/shard_map/ppermute | solution.py:544
  78.9 40.7 %collective-permute-start.9 = (bf16[256,768]{1,0:T(8,128)(2,1)S(1)}, bf16[256,768]{1,0:T(8,128)(2,1)S(1)}, u32[]{:S(2)}, u32[]{:S(2)}) collective-permute-start(bf16[256,768]{1,0:T(8,128)(2,1)S(1)} %get-tuple-element.53), channel_id=1, source_target_pairs={{0,64},{4,68},{8,72},{12,76},{16,80},{20,84},{24,88},{28,92},{32,9... | collective-permute-start | bytes 1179656 | tf_op jit(solution)/shard_map/ppermute | solution.py:550
  94.3 26.1 %collective-permute-start.10 = (bf16[256,768]{1,0:T(8,128)(2,1)S(1)}, bf16[256,768]{1,0:T(8,128)(2,1)S(1)}, u32[]{:S(2)}, u32[]{:S(2)}) collective-permute-start(bf16[256,768]{1,0:T(8,128)(2,1)S(1)} %get-tuple-element.58), channel_id=1, source_target_pairs={{0,256},{4,260},{8,264},{12,268},{16,272},{20,276},{24,280},{28,28... | collective-permute-start | bytes 1179656 | tf_op jit(solution)/shard_map/ppermute | solution.py:550
  97.9 22.4 %collective-permute-start.11 = (bf16[256,768]{1,0:T(8,128)(2,1)S(1)}, bf16[256,768]{1,0:T(8,128)(2,1)S(1)}, u32[]{:S(2)}, u32[]{:S(2)}) collective-permute-start(bf16[256,768]{1,0:T(8,128)(2,1)S(1)} %get-tuple-element.59), channel_id=1, source_target_pairs={{0,128},{4,132},{8,136},{12,140},{16,144},{20,148},{24,152},{28,15... | collective-permute-start | bytes 1179656 | tf_op jit(solution)/shard_map/ppermute | solution.py:550
  99.8 31.0 %collective-permute-start.12 = (bf16[256,768]{1,0:T(8,128)(2,1)S(1)}, bf16[256,768]{1,0:T(8,128)(2,1)S(1)}, u32[]{:S(2)}, u32[]{:S(2)}) collective-permute-start(bf16[256,768]{1,0:T(8,128)(2,1)S(1)} %get-tuple-element.60), channel_id=1, source_target_pairs={{0,4},{4,8},{8,12},{12,16},{16,20},{20,24},{24,28},{28,32},{32,36}... | collective-permute-start | bytes 1179656 | tf_op jit(solution)/shard_map/ppermute | solution.py:556
  106.4 24.4 %collective-permute-start.13 = (bf16[256,768]{1,0:T(8,128)(2,1)S(1)}, bf16[256,768]{1,0:T(8,128)(2,1)S(1)}, u32[]{:S(2)}, u32[]{:S(2)}) collective-permute-start(bf16[256,768]{1,0:T(8,128)(2,1)S(1)} %get-tuple-element.61), channel_id=1, source_target_pairs={{4,0},{8,4},{12,8},{16,12},{20,16},{24,20},{28,24},{32,28},{36,32}... | collective-permute-start | bytes 1179656 | tf_op jit(solution)/shard_map/ppermute | solution.py:556

commit v7 on v6

--- a/solution.py
+++ b/solution.py
@@ -11,6 +11,7 @@
 BW = 2
 EXP = 3
 ROWS = BW * BLK
+MARK = 16
 PAIRS = D // BLK
 GROUP = 6
 SCALE = HD ** (-0.5)
@@ -206,7 +207,9 @@
     )
 
 
-def far_kernel(far2, seen, query, stat_in, acc_in, stat, acc, held, place):
+def far_kernel(far2, seen, query, stat_in, acc_in, stat, acc, wanted, held, place):
+    partner_sees = jnp.max(far2[2 * BLK :].astype(f32)) > 0
+    wanted[0, 0] = ((seen[0, 10] + seen[1, 10] > 0) | partner_sees).astype(jnp.int32)
     stat[...] = stat_in[...]
     acc[...] = acc_in[...]
     forward_over(pair_slots((10,), far2), seen, query, stat, acc, held, place)
@@ -443,10 +446,12 @@
         out[half * BLK : (half + 1) * BLK] = whole[rows]
 
 
-def pack_first_kernel(pick, key, value, far2, whole):
+def pack_first_kernel(pick, pattern, key, value, far2, whole):
     whole[0:ROWS] = key[...]
     whole[ROWS : 2 * ROWS] = value[...]
     block_of(whole, pick[0, 2] * BLK, far2)
+    sees = (pattern[0, 10] + pattern[1, 10] > 0).astype(f32)
+    far2[2 * BLK :] = jnp.full((MARK, D), sees, f32).astype(bf16)
 
 
 def pack_rest_kernel(pick, chip, cross, whole, right, left, far0, far1):
@@ -456,8 +461,13 @@
     block_of(whole, pick[0, 1] * BLK, far1)
 
 
-def pack_first(pick, key, value):
-    return call(pack_first_kernel, [RIM, SIDE], [smem(), vmem(), vmem()], (pick, key, value))
+def pack_first(pick, pattern, key, value):
+    return call(
+        pack_first_kernel,
+        [shape((2 * BLK + MARK, D), bf16), SIDE],
+        [smem(), smem(), vmem(), vmem()],
+        (pick, pattern, key, value),
+    )
 
 
 def pack_rest(pick, chip, cross, whole):
@@ -483,9 +493,10 @@
 def run_far(far2, plan, queries, stat, acc):
     return call(
         far_kernel,
-        STATE,
+        STATE + [shape((1, 1), jnp.int32)],
         [vmem(), smem()] + [vmem()] * 3,
         (far2, plan, queries, stat, acc),
+        outs=[vmem(), vmem(), smem()],
         scratch=seen_scratch(1),
     )
 
@@ -579,7 +590,7 @@
         axis=1,
     )
 
-    far2_pair, whole = pack_first(expander_pick, key_rows, value_rows)
+    far2_pair, whole = pack_first(expander_pick, pattern, key_rows, value_rows)
     chip, cross = sides(whole, whole)
     far2 = partner(far2_pair, top_bit - EXP)
     right_pair, left_pair, far0_pair, far1_pair = pack_rest(
@@ -590,17 +601,34 @@
     left = shift(left_pair, "wide", 1)
     right = shift(right_pair, "wide", -1)
     stat, acc, upward_t = run_first(plan, queries, upstream, whole, chip, cross)
-    stat, acc = run_far(far2, plan, queries, stat, acc)
+    stat, acc, wanted = run_far(far2, plan, queries, stat, acc)
     stat, out_t, query_t, far2_term, chip_term, cross_term = run_middle(
         far2, plan, queries, upstream, chip, cross, far0, far1, left, right, stat, acc, upward_t
     )
-    far2_back = partner(far2_term, top_bit - EXP)
     back = sides(chip_term, cross_term)
     left_term, right_term, far0_term, far1_term, query_t = run_rest(
         plan, queries, upstream, left, right, far0, far1, *back, stat, query_t
     )
-    attention, query_grad, key_near, value_near = run_own(
-        plan, queries, upstream, whole, *back, stat, out_t, query_t
+
+    def own_and_exchange(term, *args):
+        return partner(term, top_bit - EXP), run_own(*args)
+
+    def own_alone(term, *args):
+        return term, run_own(*args)
+
+    far2_back, (attention, query_grad, key_near, value_near) = lax.cond(
+        wanted[0, 0] > 0,
+        own_and_exchange,
+        own_alone,
+        far2_term,
+        plan,
+        queries,
+        upstream,
+        whole,
+        *back,
+        stat,
+        out_t,
+        query_t,
     )
     key_sum, value_sum = run_first_sum(far2_back, expander_pick, key_near, value_near)
     key_grad, value_grad = run_second_sum(

time: 135 us -> 143 us (1.059)
  the two profiles are of different devices: /device:TPU:25 before, /device:TPU:17 now
where the time goes in v7:
time: 143 us; the launch traced here: 142 us
  starting transfers between devices  65.4 us (46%)
  waiting for transfers between devices  42.2 us (30%)
  Pallas kernels  28.7 us (20%)
  local copies, waits for them, and re-layouts  4.19 us (3%)
  between operations  1.46 us (1%)
    ppermute x6, starting transfers between devices, partner(): lax.ppermute(value, 'wide', [(s, s ^ mask) for s in range(lax.axis_size('...  30 us
    pallas_call x9, Pallas kernels, call(): pl.pallas_call(kernel, out_shape=shapes, in_specs=specs, out_specs=outs i...  28.7 us
    ppermute x4, starting transfers between devices, shift(): return lax.ppermute(value, axis, pairs)  25.9 us
    ppermute x4, waiting for transfers between devices, shift(): return lax.ppermute(value, axis, pairs)  21.4 us
    ppermute x2, waiting for transfers between devices, sides(): lax.ppermute(cross, 'narrow', across + [(b, a) for a, b in across])  11.1 us
    ppermute x6, waiting for transfers between devices, partner(): lax.ppermute(value, 'wide', [(s, s ^ mask) for s in range(lax.axis_size('...  9.33 us
    ppermute x2, starting transfers between devices, sides(): lax.ppermute(cross, 'narrow', across + [(b, a) for a, b in across])  5.59 us
    unnamed x20, local copies, waits for them, and re-layouts  3.99 us
  transfers between devices with their start and end apart: 14, of which 4 were waited for; matrix products, arithmetic and copies ran while one was open for 0% of the time, Pallas kernels for 9%

profile of v7, /device:TPU:17, one launch (start us, length us, event | category | flops | bytes accessed | tf_op | source)
XLA Modules:
  0.0 142.1 jit_solution(14440747297168939447)
XLA Ops:
  5.4 3.7 %collective-permute-start.3 = (bf16[512,768]{1,0:T(8,128)(2,1)S(1)}, bf16[512,768]{1,0:T(8,128)(2,1)S(1)}, u32[]{:S(2)}, u32[]{:S(2)}) collective-permute-start(bf16[512,768]{1,0:T(8,128)(2,1)S(1)} %get-tuple-element.105.whole), channel_id=1, source_target_pairs={{1,2},{2,1},{5,6},{6,5},{9,10},{10,9},{13,14},{14,13},{17,18},{18,... | collective-permute-start | bytes 2359304 | tf_op jit(solution)/shard_map/ppermute | solution.py:555
  9.0 1.9 %collective-permute-start.2 = (bf16[512,768]{1,0:T(8,128)(2,1)S(1)}, bf16[512,768]{1,0:T(8,128)(2,1)S(1)}, u32[]{:S(2)}, u32[]{:S(2)}) collective-permute-start(bf16[512,768]{1,0:T(8,128)(2,1)S(1)} %get-tuple-element.105.whole), channel_id=1, source_target_pairs={{0,1},{1,0},{2,3},{3,2},{4,5},{5,4},{6,7},{7,6},{8,9},{9,8},{10,11... | collective-permute-start | bytes 2359304 | tf_op jit(solution)/shard_map/ppermute | solution.py:554
  11.0 15.4 %collective-permute-start.1 = (bf16[272,768]{1,0:T(8,128)(2,1)}, bf16[272,768]{1,0:T(8,128)(2,1)S(1)}, u32[]{:S(2)}, u32[]{:S(2)}) collective-permute-start(bf16[272,768]{1,0:T(8,128)(2,1)} %get-tuple-element.104), channel_id=1, source_target_pairs={{0,64},{4,68},{8,72},{12,76},{16,80},{20,84},{24,88},{28,92},{32,9... | collective-permute-start | bytes 1253384 | tf_op jit(solution)/shard_map/ppermute | solution.py:561
  27.1 1.8 %shard_map.96 = (bf16[256,768]{1,0:T(8,128)(2,1)}, bf16[256,768]{1,0:T(8,128)(2,1)}, bf16[256,768]{1,0:T(8,128)(2,1)}, bf16[256,768]{1,0:T(8,128)(2,1)}) custom-call(s32[1,3]{1,0:T(1,128)S(1)} %copy-done.5, bf16[512,768]{1,0:T(8,128)(2,1)S(1)} %collective-permute-done.2.chip, bf16[512,768]{1,0:T(8,128)(2,1)S(1)} %collective-permute-done.3.cross, ...), custom_call_target="tpu_custom_call" | custom-call | tf_op jit(solution)/shard_map/pallas_call | solution.py:419
  28.9 2.0 %collective-permute-start.4 = (bf16[256,768]{1,0:T(8,128)(2,1)}, bf16[256,768]{1,0:T(8,128)(2,1)S(1)}, u32[]{:S(2)}, u32[]{:S(2)}) collective-permute-start(bf16[256,768]{1,0:T(8,128)(2,1)} %get-tuple-element.109), channel_id=1, source_target_pairs={{0,256},{4,260},{8,264},{12,268},{16,272},{20,276},{24,280},{28,28... | collective-permute-start | bytes 1179656 | tf_op jit(solution)/shard_map/ppermute | solution.py:561
  30.9 3.8 %collective-permute-start.5 = (bf16[256,768]{1,0:T(8,128)(2,1)}, bf16[256,768]{1,0:T(8,128)(2,1)S(1)}, u32[]{:S(2)}, u32[]{:S(2)}) collective-permute-start(bf16[256,768]{1,0:T(8,128)(2,1)} %get-tuple-element.110), channel_id=1, source_target_pairs={{0,128},{4,132},{8,136},{12,140},{16,144},{20,148},{24,152},{28,15... | collective-permute-start | bytes 1179656 | tf_op jit(solution)/shard_map/ppermute | solution.py:561
  34.7 4.4 %collective-permute-start.6 = (bf16[256,768]{1,0:T(8,128)(2,1)}, bf16[256,768]{1,0:T(8,128)(2,1)S(1)}, u32[]{:S(2)}, u32[]{:S(2)}) collective-permute-start(bf16[256,768]{1,0:T(8,128)(2,1)} %get-tuple-element.111), channel_id=1, source_target_pairs={{0,4},{4,8},{8,12},{12,16},{16,20},{20,24},{24,28},{28,32},{32,36}... | collective-permute-start | bytes 1179656 | tf_op jit(solution)/shard_map/ppermute | solution.py:567
  39.1 5.4 %collective-permute-start.7 = (bf16[256,768]{1,0:T(8,128)(2,1)}, bf16[256,768]{1,0:T(8,128)(2,1)}, u32[]{:S(2)}, u32[]{:S(2)}) collective-permute-start(bf16[256,768]{1,0:T(8,128)(2,1)} %get-tuple-element.112), channel_id=1, source_target_pairs={{4,0},{8,4},{12,8},{16,12},{20,16},{24,20},{28,24},{32,28},{36,32}... | collective-permute-start | bytes 1179656 | tf_op jit(solution)/shard_map/ppermute | solution.py:567
  44.8 4.2 %shard_map.94 = (f32[6,8,256]{2,1,0:T(8,128)S(1)}, f32[6,128,256]{2,1,0:T(8,128)S(1)}, f32[6,128,256]{2,1,0:T(8,128)S(1)}) custom-call(s32[2,11]{1,0:T(2,128)S(1)} %concatenate.3.seen, bf16[256,768]{1,0:T(8,128)(2,1)} %query.7, bf16[256,768]{1,0:T(8,128)(2,1)} %upward.5, bf16[512,768]{1,0:T(8,128)(2,1)} %copy-done.7, ...), custom_call_target="tpu_custom_call" | custom-call | tf_op jit(solution)/shard_map/pallas_call | solution.py:419
  49.0 2.0 %shard_map.95 = (f32[6,8,256]{2,1,0:T(8,128)S(1)}, f32[6,128,256]{2,1,0:T(8,128)S(1)}, s32[1,1]{1,0:T(1,128)}) custom-call(bf16[272,768]{1,0:T(8,128)(2,1)S(1)} %collective-permute-done.1.far2, s32[2,11]{1,0:T(2,128)S(1)} %concatenate.3.seen, bf16[256,768]{1,0:T(8,128)(2,1)S(1)} %copy-done.6, f32[6,8,256]{2,1,0:T(8,128)S(1)} %get-tuple-element.106.stat_in, ...), custom_call_target="tpu_custom_call" | custom-call | tf_op jit(solution)/shard_map/pallas_call | solution.py:419
  51.1 21.4 %collective-permute-done.6.left = bf16[256,768]{1,0:T(8,128)(2,1)S(1)} collective-permute-done((bf16[256,768]{1,0:T(8,128)(2,1)}, bf16[256,768]{1,0:T(8,128)(2,1)S(1)}, u32[]{:S(2)}, u32[]{:S(2)}) %collective-permute-start.6) | collective-permute-done | bytes 393248 | tf_op jit(solution)/shard_map/ppermute | solution.py:567
  72.5 6.5 %shard_map.97 = (f32[6,8,256]{2,1,0:T(8,128)S(1)}, bf16[6,128,256]{2,1,0:T(8,128)(2,1)S(1)}, f32[6,128,256]{2,1,0:T(8,128)S(1)}, bf16[256,768]{1,0:T(8,128)(2,1)...) custom-call(bf16[272,768]{1,0:T(8,128)(2,1)S(1)} %collective-permute-done.1.far2, ...), custom_call_target="tpu_custom_call" | custom-call | tf_op jit(solution)/shard_map/pallas_call | solution.py:419
  79.1 1.9 %collective-permute-start.8 = (bf16[512,768]{1,0:T(8,128)(2,1)S(1)}, bf16[512,768]{1,0:T(8,128)(2,1)S(1)}, u32[]{:S(2)}, u32[]{:S(2)}) collective-permute-start(bf16[512,768]{1,0:T(8,128)(2,1)S(1)} %get-tuple-element.116), channel_id=1, source_target_pairs={{0,1},{1,0},{2,3},{3,2},{4,5},{5,4},{6,7},{7,6},{8,9},{9,8},{10,11... | collective-permute-start | bytes 2359304 | tf_op jit(solution)/shard_map/ppermute | solution.py:554
  81.0 1.9 %collective-permute-start.9 = (bf16[512,768]{1,0:T(8,128)(2,1)S(1)}, bf16[512,768]{1,0:T(8,128)(2,1)S(1)}, u32[]{:S(2)}, u32[]{:S(2)}) collective-permute-start(bf16[512,768]{1,0:T(8,128)(2,1)S(1)} %get-tuple-element.117), channel_id=1, source_target_pairs={{1,2},{2,1},{5,6},{6,5},{9,10},{10,9},{13,14},{14,13},{17,18},{18,... | collective-permute-start | bytes 2359304 | tf_op jit(solution)/shard_map/ppermute | solution.py:555
  83.2 11.1 %collective-permute-done.9.cross_back = bf16[512,768]{1,0:T(8,128)(2,1)S(1)} collective-permute-done((bf16[512,768]{1,0:T(8,128)(2,1)S(1)}, bf16[512,768]{1,0:T(8,128)(2,1)S(1)}, u32[]{:S(2)}, u32[]{:S(2)}) %collective-permute-start.9) | collective-permute-done | bytes 786464 | tf_op jit(solution)/shard_map/ppermute | solution.py:555
  94.3 6.0 %shard_map.98 = (bf16[256,768]{1,0:T(8,128)(2,1)S(1)}, bf16[256,768]{1,0:T(8,128)(2,1)}, bf16[256,768]{1,0:T(8,128)(2,1)}, bf16[256,768]{1,0:T(8,128)(2,1)}, f32[6,128,256]{2,1,0:T(8,128)S(1)}) custom-call(s32[2,11]{1,0:T(2,128)S(1)} %concatenate.3.seen, bf16[256,768]{1,0:T(8,128)(2,1)S(1)} %copy-done.6, bf16[256,768]{1,0:T(8,128)(2,1)S(1)} %copy-done.9, ...), custom_call_target="tpu_custom_call" | custom-call | tf_op jit(solution)/shard_map/pallas_call | solution.py:419
  100.3 1.9 %collective-permute-start.10 = (bf16[256,768]{1,0:T(8,128)(2,1)}, bf16[256,768]{1,0:T(8,128)(2,1)S(1)}, u32[]{:S(2)}, u32[]{:S(2)}) collective-permute-start(bf16[256,768]{1,0:T(8,128)(2,1)} %get-tuple-element.130), channel_id=1, source_target_pairs={{0,256},{4,260},{8,264},{12,268},{16,272},{20,276},{24,280},{28,28... | collective-permute-start | bytes 1179656 | tf_op jit(solution)/shard_map/ppermute | solution.py:561
  102.2 3.1 %collective-permute-start.11 = (bf16[256,768]{1,0:T(8,128)(2,1)}, bf16[256,768]{1,0:T(8,128)(2,1)S(1)}, u32[]{:S(2)}, u32[]{:S(2)}) collective-permute-start(bf16[256,768]{1,0:T(8,128)(2,1)} %get-tuple-element.131), channel_id=1, source_target_pairs={{0,128},{4,132},{8,136},{12,140},{16,144},{20,148},{24,152},{28,15... | collective-permute-start | bytes 1179656 | tf_op jit(solution)/shard_map/ppermute | solution.py:561
  105.3 6.2 %collective-permute-start.12 = (bf16[256,768]{1,0:T(8,128)(2,1)}, bf16[256,768]{1,0:T(8,128)(2,1)S(1)}, u32[]{:S(2)}, u32[]{:S(2)}) collective-permute-start(bf16[256,768]{1,0:T(8,128)(2,1)} %get-tuple-element.132), channel_id=1, source_target_pairs={{0,4},{4,8},{8,12},{12,16},{16,20},{20,24},{24,28},{28,32},{32,36}... | collective-permute-start | bytes 1179656 | tf_op jit(solution)/shard_map/ppermute | solution.py:567
  111.6 9.9 %collective-permute-start.13 = (bf16[256,768]{1,0:T(8,128)(2,1)S(1)}, bf16[256,768]{1,0:T(8,128)(2,1)S(1)}, u32[]{:S(2)}, u32[]{:S(2)}) collective-permute-start(bf16[256,768]{1,0:T(8,128)(2,1)S(1)} %get-tuple-element.133), channel_id=1, source_target_pairs={{4,0},{8,4},{12,8},{16,12},{20,16},{24,20},{28,24},{32,28},{36,32}... | collective-permute-start | bytes 1179656 | tf_op jit(solution)/shard_map/ppermute | solution.py:567
  122.0 17.6 %conditional.1 = (bf16[256,768]{1,0:T(8,128)(2,1)S(1)}, bf16[256,768]{1,0:T(8,128)(2,1)}, bf16[256,768]{1,0:T(8,128)(2,1)}, f32[256,768]{1,0:T(8,128)S(1)}, f32[256,768]{1,0:T(8,128)S(1)}) conditional(s32[]{:T(128)} %bitcast, (s32[2,11]{1,0:T(2,128)S(1)}, bf16[256,768]{1,0:T(8,128)(2,1)S(1)}, bf16[256,768]{1,0:T(8,128)(2,1)S(1)}, ...), branch_computations={%region_0.1_spmd, %region_1.2_spmd} | conditional | bytes 2359376 | solution.py:619
  122.1 3.8 %collective-permute-start = (bf16[256,768]{1,0:T(8,128)(2,1)S(1)}, bf16[256,768]{1,0:T(8,128)(2,1)S(1)}, u32[]{:S(2)}, u32[]{:S(2)}) collective-permute-start(bf16[256,768]{1,0:T(8,128)(2,1)S(1)} %get-tuple-element.54), channel_id=1, source_target_pairs={{0,64},{4,68},{8,72},{12,76},{16,80},{20,84},{24,88},{28,92},{32,9... | collective-permute-start | bytes 1179656 | tf_op jit(solution)/shard_map/cond/branch_1_fun/ppermute | solution.py:561
  125.9 4.4 %branch_1_fun.1 = (bf16[256,768]{1,0:T(8,128)(2,1)}, bf16[256,768]{1,0:T(8,128)(2,1)}, f32[256,768]{1,0:T(8,128)S(1)}, f32[256,768]{1,0:T(8,128)S(1)}) custom-call(s32[2,11]{1,0:T(2,128)S(1)} %get-tuple-element.55.seen, bf16[256,768]{1,0:T(8,128)(2,1)S(1)} %get-tuple-element.56.query, bf16[256,768]{1,0:T(8,128)(2,1)S(1)} %get-tuple-element.57.upward, ...), custom_call_target="tpu_custom_call" | custom-call | tf_op jit(solution)/shard_map/cond/branch_1_fun/pallas_call | solution.py:419
  130.2 9.3 %collective-permute-done = bf16[256,768]{1,0:T(8,128)(2,1)S(1)} collective-permute-done((bf16[256,768]{1,0:T(8,128)(2,1)S(1)}, bf16[256,768]{1,0:T(8,128)(2,1)S(1)}, u32[]{:S(2)}, u32[]{:S(2)}) %collective-permute-start) | collective-permute-done | bytes 393248 | tf_op jit(solution)/shard_map/cond/branch_1_fun/ppermute | solution.py:561
  (39 shorter events, 8.5 us)
Async XLA Ops:
  0.6 1.0 copy-start
  1.6 1.0 copy-start.1
  2.6 0.7 copy-start.2
  3.3 0.7 copy-start.4
  5.4 23.6 %copy-start.7 = (bf16[512,768]{1,0:T(8,128)(2,1)}, bf16[512,768]{1,0:T(8,128)(2,1)S(1)}, u32[]{:S(2)}) copy-start(bf16[512,768]{1,0:T(8,128)(2,1)S(1)} %get-tuple-element.105.whole) | copy-start | bytes 2359300
  5.4 21.1 %collective-permute-start.3 = (bf16[512,768]{1,0:T(8,128)(2,1)S(1)}, bf16[512,768]{1,0:T(8,128)(2,1)S(1)}, u32[]{:S(2)}, u32[]{:S(2)}) collective-permute-start(bf16[512,768]{1,0:T(8,128)(2,1)S(1)} %get-tuple-element.105.whole), channel_id=1, source_target_pairs={{1,2},{2,1},{5,6},{6,5},{9,10},{10,9},{13,14},{14,13},{17,18},{18,... | collective-permute-start | bytes 2359304 | tf_op jit(solution)/shard_map/ppermute | solution.py:555
  9.0 17.5 %collective-permute-start.2 = (bf16[512,768]{1,0:T(8,128)(2,1)S(1)}, bf16[512,768]{1,0:T(8,128)(2,1)S(1)}, u32[]{:S(2)}, u32[]{:S(2)}) collective-permute-start(bf16[512,768]{1,0:T(8,128)(2,1)S(1)} %get-tuple-element.105.whole), channel_id=1, source_target_pairs={{0,1},{1,0},{2,3},{3,2},{4,5},{5,4},{6,7},{7,6},{8,9},{9,8},{10,11... | collective-permute-start | bytes 2359304 | tf_op jit(solution)/shard_map/ppermute | solution.py:554
  11.0 38.0 %collective-permute-start.1 = (bf16[272,768]{1,0:T(8,128)(2,1)}, bf16[272,768]{1,0:T(8,128)(2,1)S(1)}, u32[]{:S(2)}, u32[]{:S(2)}) collective-permute-start(bf16[272,768]{1,0:T(8,128)(2,1)} %get-tuple-element.104), channel_id=1, source_target_pairs={{0,64},{4,68},{8,72},{12,76},{16,80},{20,84},{24,88},{28,92},{32,9... | collective-permute-start | bytes 1253384 | tf_op jit(solution)/shard_map/ppermute | solution.py:561
  26.5 0.7 copy-start.5
  28.9 22.2 %collective-permute-start.4 = (bf16[256,768]{1,0:T(8,128)(2,1)}, bf16[256,768]{1,0:T(8,128)(2,1)S(1)}, u32[]{:S(2)}, u32[]{:S(2)}) collective-permute-start(bf16[256,768]{1,0:T(8,128)(2,1)} %get-tuple-element.109), channel_id=1, source_target_pairs={{0,256},{4,260},{8,264},{12,268},{16,272},{20,276},{24,280},{28,28... | collective-permute-start | bytes 1179656 | tf_op jit(solution)/shard_map/ppermute | solution.py:561
  30.9 20.2 %collective-permute-start.5 = (bf16[256,768]{1,0:T(8,128)(2,1)}, bf16[256,768]{1,0:T(8,128)(2,1)S(1)}, u32[]{:S(2)}, u32[]{:S(2)}) collective-permute-start(bf16[256,768]{1,0:T(8,128)(2,1)} %get-tuple-element.110), channel_id=1, source_target_pairs={{0,128},{4,132},{8,136},{12,140},{16,144},{20,148},{24,152},{28,15... | collective-permute-start | bytes 1179656 | tf_op jit(solution)/shard_map/ppermute | solution.py:561
  34.7 9.8 %copy-start.3 = (s32[2,11]{1,0:T(2,128)S(1)}, s32[2,11]{1,0:T(2,128)}, u32[]{:S(2)}) copy-start(s32[2,11]{1,0:T(2,128)} %pattern.1) | copy-start | bytes 268
  34.7 37.8 %collective-permute-start.6 = (bf16[256,768]{1,0:T(8,128)(2,1)}, bf16[256,768]{1,0:T(8,128)(2,1)S(1)}, u32[]{:S(2)}, u32[]{:S(2)}) collective-permute-start(bf16[256,768]{1,0:T(8,128)(2,1)} %get-tuple-element.111), channel_id=1, source_target_pairs={{0,4},{4,8},{8,12},{12,16},{16,20},{20,24},{24,28},{28,32},{32,36}... | collective-permute-start | bytes 1179656 | tf_op jit(solution)/shard_map/ppermute | solution.py:567
  39.1 33.5 %collective-permute-start.7 = (bf16[256,768]{1,0:T(8,128)(2,1)}, bf16[256,768]{1,0:T(8,128)(2,1)}, u32[]{:S(2)}, u32[]{:S(2)}) collective-permute-start(bf16[256,768]{1,0:T(8,128)(2,1)} %get-tuple-element.112), channel_id=1, source_target_pairs={{4,0},{8,4},{12,8},{16,12},{20,16},{24,20},{28,24},{32,28},{36,32}... | collective-permute-start | bytes 1179656 | tf_op jit(solution)/shard_map/ppermute | solution.py:567
  44.8 4.2 %copy-start.6 = (bf16[256,768]{1,0:T(8,128)(2,1)S(1)}, bf16[256,768]{1,0:T(8,128)(2,1)}, u32[]{:S(2)}) copy-start(bf16[256,768]{1,0:T(8,128)(2,1)} %query.7) | copy-start | bytes 1179652
  49.0 23.5 %copy-start.9 = (bf16[256,768]{1,0:T(8,128)(2,1)S(1)}, bf16[256,768]{1,0:T(8,128)(2,1)}, u32[]{:S(2)}) copy-start(bf16[256,768]{1,0:T(8,128)(2,1)} %upward.5) | copy-start | bytes 1179652
  79.1 4.2 %collective-permute-start.8 = (bf16[512,768]{1,0:T(8,128)(2,1)S(1)}, bf16[512,768]{1,0:T(8,128)(2,1)S(1)}, u32[]{:S(2)}, u32[]{:S(2)}) collective-permute-start(bf16[512,768]{1,0:T(8,128)(2,1)S(1)} %get-tuple-element.116), channel_id=1, source_target_pairs={{0,1},{1,0},{2,3},{3,2},{4,5},{5,4},{6,7},{7,6},{8,9},{9,8},{10,11... | collective-permute-start | bytes 2359304 | tf_op jit(solution)/shard_map/ppermute | solution.py:554
  81.0 13.3 %collective-permute-start.9 = (bf16[512,768]{1,0:T(8,128)(2,1)S(1)}, bf16[512,768]{1,0:T(8,128)(2,1)S(1)}, u32[]{:S(2)}, u32[]{:S(2)}) collective-permute-start(bf16[512,768]{1,0:T(8,128)(2,1)S(1)} %get-tuple-element.117), channel_id=1, source_target_pairs={{1,2},{2,1},{5,6},{6,5},{9,10},{10,9},{13,14},{14,13},{17,18},{18,... | collective-permute-start | bytes 2359304 | tf_op jit(solution)/shard_map/ppermute | solution.py:555
  94.3 27.7 %copy-start.8 = (bf16[512,768]{1,0:T(8,128)(2,1)S(1)}, bf16[512,768]{1,0:T(8,128)(2,1)}, u32[]{:S(2)}) copy-start(bf16[512,768]{1,0:T(8,128)(2,1)} %copy-done.7) | copy-start | bytes 2359300
  100.3 40.0 %collective-permute-start.10 = (bf16[256,768]{1,0:T(8,128)(2,1)}, bf16[256,768]{1,0:T(8,128)(2,1)S(1)}, u32[]{:S(2)}, u32[]{:S(2)}) collective-permute-start(bf16[256,768]{1,0:T(8,128)(2,1)} %get-tuple-element.130), channel_id=1, source_target_pairs={{0,256},{4,260},{8,264},{12,268},{16,272},{20,276},{24,280},{28,28... | collective-permute-start | bytes 1179656 | tf_op jit(solution)/shard_map/ppermute | solution.py:561
  102.2 38.1 %collective-permute-start.11 = (bf16[256,768]{1,0:T(8,128)(2,1)}, bf16[256,768]{1,0:T(8,128)(2,1)S(1)}, u32[]{:S(2)}, u32[]{:S(2)}) collective-permute-start(bf16[256,768]{1,0:T(8,128)(2,1)} %get-tuple-element.131), channel_id=1, source_target_pairs={{0,128},{4,132},{8,136},{12,140},{16,144},{20,148},{24,152},{28,15... | collective-permute-start | bytes 1179656 | tf_op jit(solution)/shard_map/ppermute | solution.py:561
  105.3 35.0 %collective-permute-start.12 = (bf16[256,768]{1,0:T(8,128)(2,1)}, bf16[256,768]{1,0:T(8,128)(2,1)S(1)}, u32[]{:S(2)}, u32[]{:S(2)}) collective-permute-start(bf16[256,768]{1,0:T(8,128)(2,1)} %get-tuple-element.132), channel_id=1, source_target_pairs={{0,4},{4,8},{8,12},{12,16},{16,20},{20,24},{24,28},{28,32},{32,36}... | collective-permute-start | bytes 1179656 | tf_op jit(solution)/shard_map/ppermute | solution.py:567
  111.6 28.8 %collective-permute-start.13 = (bf16[256,768]{1,0:T(8,128)(2,1)S(1)}, bf16[256,768]{1,0:T(8,128)(2,1)S(1)}, u32[]{:S(2)}, u32[]{:S(2)}) collective-permute-start(bf16[256,768]{1,0:T(8,128)(2,1)S(1)} %get-tuple-element.133), channel_id=1, source_target_pairs={{4,0},{8,4},{12,8},{16,12},{20,16},{24,20},{28,24},{32,28},{36,32}... | collective-permute-start | bytes 1179656 | tf_op jit(solution)/shard_map/ppermute | solution.py:567
  122.1 17.5 %collective-permute-start = (bf16[256,768]{1,0:T(8,128)(2,1)S(1)}, bf16[256,768]{1,0:T(8,128)(2,1)S(1)}, u32[]{:S(2)}, u32[]{:S(2)}) collective-permute-start(bf16[256,768]{1,0:T(8,128)(2,1)S(1)} %get-tuple-element.54), channel_id=1, source_target_pairs={{0,64},{4,68},{8,72},{12,76},{16,80},{20,84},{24,88},{28,92},{32,9... | collective-permute-start | bytes 1179656 | tf_op jit(solution)/shard_map/cond/branch_1_fun/ppermute | solution.py:561

commit v8 on v7

--- a/solution.py
+++ b/solution.py
@@ -319,8 +319,6 @@
     right,
     far0,
     far1,
-    chip_back,
-    cross_back,
     stat,
     query_t_in,
     left_term,
@@ -516,7 +514,7 @@
     return call(
         rest_kernel,
         [RIM] * 4 + [STATE[1]],
-        [smem()] + [vmem()] * 6 + [hbm()] * 2 + [vmem()] * 2,
+        [smem()] + [vmem()] * 8,
         (plan, *rest),
         scratch=[pltpu.VMEM((2 * BLK, D), bf16)] + seen_scratch(4),
     )
@@ -607,7 +605,7 @@
     )
     back = sides(chip_term, cross_term)
     left_term, right_term, far0_term, far1_term, query_t = run_rest(
-        plan, queries, upstream, left, right, far0, far1, *back, stat, query_t
+        plan, queries, upstream, left, right, far0, far1, stat, query_t
     )
 
     def own_and_exchange(term, *args):

time: 143 us -> 138 us (0.965)
  the two profiles are of different devices: /device:TPU:17 before, /device:TPU:2 now
where the time goes in v8:
time: 138 us; the launch traced here: 136 us
  starting transfers between devices  82.9 us (60%)
  Pallas kernels  26.7 us (19%)
  waiting for transfers between devices  20.8 us (15%)
  local copies, waits for them, and re-layouts  4.19 us (3%)
  between operations  1.47 us (1%)
    ppermute x6, starting transfers between devices, partner(): lax.ppermute(value, 'wide', [(s, s ^ mask) for s in range(lax.axis_size('...  62.5 us
    pallas_call x9, Pallas kernels, call(): pl.pallas_call(kernel, out_shape=shapes, in_specs=specs, out_specs=outs i...  26.7 us
    ppermute x6, waiting for transfers between devices, partner(): lax.ppermute(value, 'wide', [(s, s ^ mask) for s in range(lax.axis_size('...  18.3 us
    ppermute x4, starting transfers between devices, shift(): return lax.ppermute(value, axis, pairs)  12.7 us
    unnamed x20, local copies, waits for them, and re-layouts  3.99 us
    ppermute x2, starting transfers between devices, sides(): lax.ppermute(chip, 'narrow', [(i, i ^ 1) for i in range(count)])  3.84 us
    ppermute x2, starting transfers between devices, sides(): lax.ppermute(cross, 'narrow', across + [(b, a) for a, b in across])  3.83 us
  transfers between devices with their start and end apart: 14, of which 3 were waited for; matrix products, arithmetic and copies ran while one was open for 0% of the time, Pallas kernels for 13%

profile of v8, /device:TPU:2, one launch (start us, length us, event | category | flops | bytes accessed | tf_op | source)
XLA Modules:
  0.0 136.2 jit_solution(9974037405235751972)
XLA Ops:
  4.0 1.4 %shard_map.93 = (bf16[272,768]{1,0:T(8,128)(2,1)}, bf16[512,768]{1,0:T(8,128)(2,1)S(1)}) custom-call(s32[1,3]{1,0:T(1,128)S(1)} %copy-done.4, s32[2,11]{1,0:T(2,128)S(1)} %copy-done.2, bf16[256,768]{1,0:T(8,128)(2,1)S(1)} %copy-done, bf16[256,768]{1,0:T(8,128)(2,1)S(1)} %copy-done.1), custom_call_target="tpu_custom_call" | custom-call | tf_op jit(solution)/shard_map/pallas_call | solution.py:417
  5.4 1.9 %collective-permute-start.3 = (bf16[512,768]{1,0:T(8,128)(2,1)S(1)}, bf16[512,768]{1,0:T(8,128)(2,1)S(1)}, u32[]{:S(2)}, u32[]{:S(2)}) collective-permute-start(bf16[512,768]{1,0:T(8,128)(2,1)S(1)} %get-tuple-element.105.whole), channel_id=1, source_target_pairs={{1,2},{2,1},{5,6},{6,5},{9,10},{10,9},{13,14},{14,13},{17,18},{18,... | collective-permute-start | bytes 2359304 | tf_op jit(solution)/shard_map/ppermute | solution.py:553
  7.3 1.9 %collective-permute-start.2 = (bf16[512,768]{1,0:T(8,128)(2,1)S(1)}, bf16[512,768]{1,0:T(8,128)(2,1)S(1)}, u32[]{:S(2)}, u32[]{:S(2)}) collective-permute-start(bf16[512,768]{1,0:T(8,128)(2,1)S(1)} %get-tuple-element.105.whole), channel_id=1, source_target_pairs={{0,1},{1,0},{2,3},{3,2},{4,5},{5,4},{6,7},{7,6},{8,9},{9,8},{10,11... | collective-permute-start | bytes 2359304 | tf_op jit(solution)/shard_map/ppermute | solution.py:552
  9.2 15.7 %collective-permute-start.1 = (bf16[272,768]{1,0:T(8,128)(2,1)}, bf16[272,768]{1,0:T(8,128)(2,1)S(1)}, u32[]{:S(2)}, u32[]{:S(2)}) collective-permute-start(bf16[272,768]{1,0:T(8,128)(2,1)} %get-tuple-element.104), channel_id=1, source_target_pairs={{0,64},{4,68},{8,72},{12,76},{16,80},{20,84},{24,88},{28,92},{32,9... | collective-permute-start | bytes 1253384 | tf_op jit(solution)/shard_map/ppermute | solution.py:559
  25.7 1.8 %shard_map.96 = (bf16[256,768]{1,0:T(8,128)(2,1)}, bf16[256,768]{1,0:T(8,128)(2,1)}, bf16[256,768]{1,0:T(8,128)(2,1)}, bf16[256,768]{1,0:T(8,128)(2,1)}) custom-call(s32[1,3]{1,0:T(1,128)S(1)} %copy-done.5, bf16[512,768]{1,0:T(8,128)(2,1)S(1)} %collective-permute-done.2.chip, bf16[512,768]{1,0:T(8,128)(2,1)S(1)} %collective-permute-done.3.cross, ...), custom_call_target="tpu_custom_call" | custom-call | tf_op jit(solution)/shard_map/pallas_call | solution.py:417
  27.4 5.1 %collective-permute-start.4 = (bf16[256,768]{1,0:T(8,128)(2,1)}, bf16[256,768]{1,0:T(8,128)(2,1)S(1)}, u32[]{:S(2)}, u32[]{:S(2)}) collective-permute-start(bf16[256,768]{1,0:T(8,128)(2,1)} %get-tuple-element.109), channel_id=1, source_target_pairs={{0,256},{4,260},{8,264},{12,268},{16,272},{20,276},{24,280},{28,28... | collective-permute-start | bytes 1179656 | tf_op jit(solution)/shard_map/ppermute | solution.py:559
  32.5 2.6 %collective-permute-start.5 = (bf16[256,768]{1,0:T(8,128)(2,1)}, bf16[256,768]{1,0:T(8,128)(2,1)S(1)}, u32[]{:S(2)}, u32[]{:S(2)}) collective-permute-start(bf16[256,768]{1,0:T(8,128)(2,1)} %get-tuple-element.110), channel_id=1, source_target_pairs={{0,128},{4,132},{8,136},{12,140},{16,144},{20,148},{24,152},{28,15... | collective-permute-start | bytes 1179656 | tf_op jit(solution)/shard_map/ppermute | solution.py:559
  35.1 4.3 %collective-permute-start.6 = (bf16[256,768]{1,0:T(8,128)(2,1)}, bf16[256,768]{1,0:T(8,128)(2,1)S(1)}, u32[]{:S(2)}, u32[]{:S(2)}) collective-permute-start(bf16[256,768]{1,0:T(8,128)(2,1)} %get-tuple-element.111), channel_id=1, source_target_pairs={{0,4},{4,8},{8,12},{12,16},{16,20},{20,24},{24,28},{28,32},{32,36}... | collective-permute-start | bytes 1179656 | tf_op jit(solution)/shard_map/ppermute | solution.py:565
  41.0 4.2 %shard_map.94 = (f32[6,8,256]{2,1,0:T(8,128)S(1)}, f32[6,128,256]{2,1,0:T(8,128)S(1)}, f32[6,128,256]{2,1,0:T(8,128)S(1)}) custom-call(s32[2,11]{1,0:T(2,128)S(1)} %concatenate.3.seen, bf16[256,768]{1,0:T(8,128)(2,1)} %query.7, bf16[256,768]{1,0:T(8,128)(2,1)} %upward.5, bf16[512,768]{1,0:T(8,128)(2,1)} %copy-done.7, ...), custom_call_target="tpu_custom_call" | custom-call | tf_op jit(solution)/shard_map/pallas_call | solution.py:417
  45.3 2.0 %shard_map.95 = (f32[6,8,256]{2,1,0:T(8,128)S(1)}, f32[6,128,256]{2,1,0:T(8,128)S(1)}, s32[1,1]{1,0:T(1,128)}) custom-call(bf16[272,768]{1,0:T(8,128)(2,1)S(1)} %collective-permute-done.1.far2, s32[2,11]{1,0:T(2,128)S(1)} %concatenate.3.seen, bf16[256,768]{1,0:T(8,128)(2,1)S(1)} %copy-done.6, f32[6,8,256]{2,1,0:T(8,128)S(1)} %get-tuple-element.106.stat_in, ...), custom_call_target="tpu_custom_call" | custom-call | tf_op jit(solution)/shard_map/pallas_call | solution.py:417
  47.3 3.7 %collective-permute-done.5.far1 = bf16[256,768]{1,0:T(8,128)(2,1)S(1)} collective-permute-done((bf16[256,768]{1,0:T(8,128)(2,1)}, bf16[256,768]{1,0:T(8,128)(2,1)S(1)}, u32[]{:S(2)}, u32[]{:S(2)}) %collective-permute-start.5) | collective-permute-done | bytes 393248 | tf_op jit(solution)/shard_map/ppermute | solution.py:559
  51.0 2.5 %collective-permute-done.7.right = bf16[256,768]{1,0:T(8,128)(2,1)} collective-permute-done((bf16[256,768]{1,0:T(8,128)(2,1)}, bf16[256,768]{1,0:T(8,128)(2,1)}, u32[]{:S(2)}, u32[]{:S(2)}) %collective-permute-start.7) | collective-permute-done | bytes 393248 | tf_op jit(solution)/shard_map/ppermute | solution.py:565
  53.6 5.7 %shard_map.97 = (f32[6,8,256]{2,1,0:T(8,128)S(1)}, bf16[6,128,256]{2,1,0:T(8,128)(2,1)S(1)}, f32[6,128,256]{2,1,0:T(8,128)S(1)}, bf16[256,768]{1,0:T(8,128)(2,1)...) custom-call(bf16[272,768]{1,0:T(8,128)(2,1)S(1)} %collective-permute-done.1.far2, ...), custom_call_target="tpu_custom_call" | custom-call | tf_op jit(solution)/shard_map/pallas_call | solution.py:417
  59.3 1.9 %collective-permute-start.8 = (bf16[512,768]{1,0:T(8,128)(2,1)S(1)}, bf16[512,768]{1,0:T(8,128)(2,1)S(1)}, u32[]{:S(2)}, u32[]{:S(2)}) collective-permute-start(bf16[512,768]{1,0:T(8,128)(2,1)S(1)} %get-tuple-element.116), channel_id=1, source_target_pairs={{0,1},{1,0},{2,3},{3,2},{4,5},{5,4},{6,7},{7,6},{8,9},{9,8},{10,11... | collective-permute-start | bytes 2359304 | tf_op jit(solution)/shard_map/ppermute | solution.py:552
  61.2 1.9 %collective-permute-start.9 = (bf16[512,768]{1,0:T(8,128)(2,1)S(1)}, bf16[512,768]{1,0:T(8,128)(2,1)S(1)}, u32[]{:S(2)}, u32[]{:S(2)}) collective-permute-start(bf16[512,768]{1,0:T(8,128)(2,1)S(1)} %get-tuple-element.117), channel_id=1, source_target_pairs={{1,2},{2,1},{5,6},{6,5},{9,10},{10,9},{13,14},{14,13},{17,18},{18,... | collective-permute-start | bytes 2359304 | tf_op jit(solution)/shard_map/ppermute | solution.py:553
  63.1 4.8 %shard_map.98 = (bf16[256,768]{1,0:T(8,128)(2,1)S(1)}, bf16[256,768]{1,0:T(8,128)(2,1)}, bf16[256,768]{1,0:T(8,128)(2,1)}, bf16[256,768]{1,0:T(8,128)(2,1)}, f32[6,128,256]{2,1,0:T(8,128)S(1)}) custom-call(s32[2,11]{1,0:T(2,128)S(1)} %concatenate.3.seen, bf16[256,768]{1,0:T(8,128)(2,1)S(1)} %copy-done.6, bf16[256,768]{1,0:T(8,128)(2,1)S(1)} %copy-done.9, ...), custom_call_target="tpu_custom_call" | custom-call | tf_op jit(solution)/shard_map/pallas_call | solution.py:417
  67.9 22.8 %collective-permute-start.10 = (bf16[256,768]{1,0:T(8,128)(2,1)}, bf16[256,768]{1,0:T(8,128)(2,1)S(1)}, u32[]{:S(2)}, u32[]{:S(2)}) collective-permute-start(bf16[256,768]{1,0:T(8,128)(2,1)} %get-tuple-element.130), channel_id=1, source_target_pairs={{0,256},{4,260},{8,264},{12,268},{16,272},{20,276},{24,280},{28,28... | collective-permute-start | bytes 1179656 | tf_op jit(solution)/shard_map/ppermute | solution.py:559
  90.7 4.2 %collective-permute-start.11 = (bf16[256,768]{1,0:T(8,128)(2,1)}, bf16[256,768]{1,0:T(8,128)(2,1)S(1)}, u32[]{:S(2)}, u32[]{:S(2)}) collective-permute-start(bf16[256,768]{1,0:T(8,128)(2,1)} %get-tuple-element.131), channel_id=1, source_target_pairs={{0,128},{4,132},{8,136},{12,140},{16,144},{20,148},{24,152},{28,15... | collective-permute-start | bytes 1179656 | tf_op jit(solution)/shard_map/ppermute | solution.py:559
  94.9 5.8 %collective-permute-start.12 = (bf16[256,768]{1,0:T(8,128)(2,1)}, bf16[256,768]{1,0:T(8,128)(2,1)S(1)}, u32[]{:S(2)}, u32[]{:S(2)}) collective-permute-start(bf16[256,768]{1,0:T(8,128)(2,1)} %get-tuple-element.132), channel_id=1, source_target_pairs={{0,4},{4,8},{8,12},{12,16},{16,20},{20,24},{24,28},{28,32},{32,36}... | collective-permute-start | bytes 1179656 | tf_op jit(solution)/shard_map/ppermute | solution.py:565
  102.6 31.1 %conditional.1 = (bf16[256,768]{1,0:T(8,128)(2,1)S(1)}, bf16[256,768]{1,0:T(8,128)(2,1)}, bf16[256,768]{1,0:T(8,128)(2,1)}, f32[256,768]{1,0:T(8,128)S(1)}, f32[256,768]{1,0:T(8,128)S(1)}) conditional(s32[]{:T(128)} %bitcast, (s32[2,11]{1,0:T(2,128)S(1)}, bf16[256,768]{1,0:T(8,128)(2,1)S(1)}, bf16[256,768]{1,0:T(8,128)(2,1)S(1)}, ...), branch_computations={%region_0.1_spmd, %region_1.2_spmd} | conditional | bytes 2359376 | solution.py:617
  102.6 12.1 %collective-permute-start = (bf16[256,768]{1,0:T(8,128)(2,1)S(1)}, bf16[256,768]{1,0:T(8,128)(2,1)S(1)}, u32[]{:S(2)}, u32[]{:S(2)}) collective-permute-start(bf16[256,768]{1,0:T(8,128)(2,1)S(1)} %get-tuple-element.54), channel_id=1, source_target_pairs={{0,64},{4,68},{8,72},{12,76},{16,80},{20,84},{24,88},{28,92},{32,9... | collective-permute-start | bytes 1179656 | tf_op jit(solution)/shard_map/cond/branch_1_fun/ppermute | solution.py:559
  114.8 4.4 %branch_1_fun.1 = (bf16[256,768]{1,0:T(8,128)(2,1)}, bf16[256,768]{1,0:T(8,128)(2,1)}, f32[256,768]{1,0:T(8,128)S(1)}, f32[256,768]{1,0:T(8,128)S(1)}) custom-call(s32[2,11]{1,0:T(2,128)S(1)} %get-tuple-element.55.seen, bf16[256,768]{1,0:T(8,128)(2,1)S(1)} %get-tuple-element.56.query, bf16[256,768]{1,0:T(8,128)(2,1)S(1)} %get-tuple-element.57.upward, ...), custom_call_target="tpu_custom_call" | custom-call | tf_op jit(solution)/shard_map/cond/branch_1_fun/pallas_call | solution.py:417
  119.1 14.5 %collective-permute-done = bf16[256,768]{1,0:T(8,128)(2,1)S(1)} collective-permute-done((bf16[256,768]{1,0:T(8,128)(2,1)S(1)}, bf16[256,768]{1,0:T(8,128)(2,1)S(1)}, u32[]{:S(2)}, u32[]{:S(2)}) %collective-permute-start) | collective-permute-done | bytes 393248 | tf_op jit(solution)/shard_map/cond/branch_1_fun/ppermute | solution.py:559
  134.4 1.7 %shard_map.100 = (bf16[256,768]{1,0:T(8,128)(2,1)}, bf16[256,768]{1,0:T(8,128)(2,1)}) custom-call(s32[1,3]{1,0:T(1,128)S(1)} %copy-done.5, f32[256,768]{1,0:T(8,128)S(1)} %get-tuple-element.128.key_sum, f32[256,768]{1,0:T(8,128)S(1)} %get-tuple-element.129.value_sum, bf16[256,768]{1,0:T(8,128)(2,1)S(1)} %collective-permute-done.10.far0, ...), custom_call_target="tpu_custom_call" | custom-call | tf_op jit(solution)/shard_map/pallas_call | solution.py:417
  (39 shorter events, 7.6 us)
Async XLA Ops:
  0.6 1.0 copy-start
  1.6 1.0 copy-start.1
  2.6 0.7 copy-start.2
  3.3 0.7 copy-start.4
  5.4 22.1 %copy-start.7 = (bf16[512,768]{1,0:T(8,128)(2,1)}, bf16[512,768]{1,0:T(8,128)(2,1)S(1)}, u32[]{:S(2)}) copy-start(bf16[512,768]{1,0:T(8,128)(2,1)S(1)} %get-tuple-element.105.whole) | copy-start | bytes 2359300
  5.4 19.7 %collective-permute-start.3 = (bf16[512,768]{1,0:T(8,128)(2,1)S(1)}, bf16[512,768]{1,0:T(8,128)(2,1)S(1)}, u32[]{:S(2)}, u32[]{:S(2)}) collective-permute-start(bf16[512,768]{1,0:T(8,128)(2,1)S(1)} %get-tuple-element.105.whole), channel_id=1, source_target_pairs={{1,2},{2,1},{5,6},{6,5},{9,10},{10,9},{13,14},{14,13},{17,18},{18,... | collective-permute-start | bytes 2359304 | tf_op jit(solution)/shard_map/ppermute | solution.py:553
  7.3 17.7 %collective-permute-start.2 = (bf16[512,768]{1,0:T(8,128)(2,1)S(1)}, bf16[512,768]{1,0:T(8,128)(2,1)S(1)}, u32[]{:S(2)}, u32[]{:S(2)}) collective-permute-start(bf16[512,768]{1,0:T(8,128)(2,1)S(1)} %get-tuple-element.105.whole), channel_id=1, source_target_pairs={{0,1},{1,0},{2,3},{3,2},{4,5},{5,4},{6,7},{7,6},{8,9},{9,8},{10,11... | collective-permute-start | bytes 2359304 | tf_op jit(solution)/shard_map/ppermute | solution.py:552
  9.2 36.0 %collective-permute-start.1 = (bf16[272,768]{1,0:T(8,128)(2,1)}, bf16[272,768]{1,0:T(8,128)(2,1)S(1)}, u32[]{:S(2)}, u32[]{:S(2)}) collective-permute-start(bf16[272,768]{1,0:T(8,128)(2,1)} %get-tuple-element.104), channel_id=1, source_target_pairs={{0,64},{4,68},{8,72},{12,76},{16,80},{20,84},{24,88},{28,92},{32,9... | collective-permute-start | bytes 1253384 | tf_op jit(solution)/shard_map/ppermute | solution.py:559
  25.0 0.7 copy-start.5
  27.4 19.9 %collective-permute-start.4 = (bf16[256,768]{1,0:T(8,128)(2,1)}, bf16[256,768]{1,0:T(8,128)(2,1)S(1)}, u32[]{:S(2)}, u32[]{:S(2)}) collective-permute-start(bf16[256,768]{1,0:T(8,128)(2,1)} %get-tuple-element.109), channel_id=1, source_target_pairs={{0,256},{4,260},{8,264},{12,268},{16,272},{20,276},{24,280},{28,28... | collective-permute-start | bytes 1179656 | tf_op jit(solution)/shard_map/ppermute | solution.py:559
  32.5 18.5 %collective-permute-start.5 = (bf16[256,768]{1,0:T(8,128)(2,1)}, bf16[256,768]{1,0:T(8,128)(2,1)S(1)}, u32[]{:S(2)}, u32[]{:S(2)}) collective-permute-start(bf16[256,768]{1,0:T(8,128)(2,1)} %get-tuple-element.110), channel_id=1, source_target_pairs={{0,128},{4,132},{8,136},{12,140},{16,144},{20,148},{24,152},{28,15... | collective-permute-start | bytes 1179656 | tf_op jit(solution)/shard_map/ppermute | solution.py:559
  35.1 5.6 %copy-start.3 = (s32[2,11]{1,0:T(2,128)S(1)}, s32[2,11]{1,0:T(2,128)}, u32[]{:S(2)}) copy-start(s32[2,11]{1,0:T(2,128)} %pattern.1) | copy-start | bytes 268
  35.1 15.9 %collective-permute-start.6 = (bf16[256,768]{1,0:T(8,128)(2,1)}, bf16[256,768]{1,0:T(8,128)(2,1)S(1)}, u32[]{:S(2)}, u32[]{:S(2)}) collective-permute-start(bf16[256,768]{1,0:T(8,128)(2,1)} %get-tuple-element.111), channel_id=1, source_target_pairs={{0,4},{4,8},{8,12},{12,16},{16,20},{20,24},{24,28},{28,32},{32,36}... | collective-permute-start | bytes 1179656 | tf_op jit(solution)/shard_map/ppermute | solution.py:565
  39.5 14.1 %collective-permute-start.7 = (bf16[256,768]{1,0:T(8,128)(2,1)}, bf16[256,768]{1,0:T(8,128)(2,1)}, u32[]{:S(2)}, u32[]{:S(2)}) collective-permute-start(bf16[256,768]{1,0:T(8,128)(2,1)} %get-tuple-element.112), channel_id=1, source_target_pairs={{4,0},{8,4},{12,8},{16,12},{20,16},{24,20},{28,24},{32,28},{36,32}... | collective-permute-start | bytes 1179656 | tf_op jit(solution)/shard_map/ppermute | solution.py:565
  41.0 4.2 %copy-start.6 = (bf16[256,768]{1,0:T(8,128)(2,1)S(1)}, bf16[256,768]{1,0:T(8,128)(2,1)}, u32[]{:S(2)}) copy-start(bf16[256,768]{1,0:T(8,128)(2,1)} %query.7) | copy-start | bytes 1179652
  45.3 8.3 %copy-start.9 = (bf16[256,768]{1,0:T(8,128)(2,1)S(1)}, bf16[256,768]{1,0:T(8,128)(2,1)}, u32[]{:S(2)}) copy-start(bf16[256,768]{1,0:T(8,128)(2,1)} %upward.5) | copy-start | bytes 1179652
  59.3 41.5 %collective-permute-start.8 = (bf16[512,768]{1,0:T(8,128)(2,1)S(1)}, bf16[512,768]{1,0:T(8,128)(2,1)S(1)}, u32[]{:S(2)}, u32[]{:S(2)}) collective-permute-start(bf16[512,768]{1,0:T(8,128)(2,1)S(1)} %get-tuple-element.116), channel_id=1, source_target_pairs={{0,1},{1,0},{2,3},{3,2},{4,5},{5,4},{6,7},{7,6},{8,9},{9,8},{10,11... | collective-permute-start | bytes 2359304 | tf_op jit(solution)/shard_map/ppermute | solution.py:552
  61.2 41.4 %collective-permute-start.9 = (bf16[512,768]{1,0:T(8,128)(2,1)S(1)}, bf16[512,768]{1,0:T(8,128)(2,1)S(1)}, u32[]{:S(2)}, u32[]{:S(2)}) collective-permute-start(bf16[512,768]{1,0:T(8,128)(2,1)S(1)} %get-tuple-element.117), channel_id=1, source_target_pairs={{1,2},{2,1},{5,6},{6,5},{9,10},{10,9},{13,14},{14,13},{17,18},{18,... | collective-permute-start | bytes 2359304 | tf_op jit(solution)/shard_map/ppermute | solution.py:553
  63.1 39.5 %copy-start.8 = (bf16[512,768]{1,0:T(8,128)(2,1)S(1)}, bf16[512,768]{1,0:T(8,128)(2,1)}, u32[]{:S(2)}) copy-start(bf16[512,768]{1,0:T(8,128)(2,1)} %copy-done.7) | copy-start | bytes 2359300
  67.9 66.5 %collective-permute-start.10 = (bf16[256,768]{1,0:T(8,128)(2,1)}, bf16[256,768]{1,0:T(8,128)(2,1)S(1)}, u32[]{:S(2)}, u32[]{:S(2)}) collective-permute-start(bf16[256,768]{1,0:T(8,128)(2,1)} %get-tuple-element.130), channel_id=1, source_target_pairs={{0,256},{4,260},{8,264},{12,268},{16,272},{20,276},{24,280},{28,28... | collective-permute-start | bytes 1179656 | tf_op jit(solution)/shard_map/ppermute | solution.py:559
  90.7 43.7 %collective-permute-start.11 = (bf16[256,768]{1,0:T(8,128)(2,1)}, bf16[256,768]{1,0:T(8,128)(2,1)S(1)}, u32[]{:S(2)}, u32[]{:S(2)}) collective-permute-start(bf16[256,768]{1,0:T(8,128)(2,1)} %get-tuple-element.131), channel_id=1, source_target_pairs={{0,128},{4,132},{8,136},{12,140},{16,144},{20,148},{24,152},{28,15... | collective-permute-start | bytes 1179656 | tf_op jit(solution)/shard_map/ppermute | solution.py:559
  94.9 39.6 %collective-permute-start.12 = (bf16[256,768]{1,0:T(8,128)(2,1)}, bf16[256,768]{1,0:T(8,128)(2,1)S(1)}, u32[]{:S(2)}, u32[]{:S(2)}) collective-permute-start(bf16[256,768]{1,0:T(8,128)(2,1)} %get-tuple-element.132), channel_id=1, source_target_pairs={{0,4},{4,8},{8,12},{12,16},{16,20},{20,24},{24,28},{28,32},{32,36}... | collective-permute-start | bytes 1179656 | tf_op jit(solution)/shard_map/ppermute | solution.py:565
  100.7 33.7 %collective-permute-start.13 = (bf16[256,768]{1,0:T(8,128)(2,1)S(1)}, bf16[256,768]{1,0:T(8,128)(2,1)S(1)}, u32[]{:S(2)}, u32[]{:S(2)}) collective-permute-start(bf16[256,768]{1,0:T(8,128)(2,1)S(1)} %get-tuple-element.133), channel_id=1, source_target_pairs={{4,0},{8,4},{12,8},{16,12},{20,16},{24,20},{28,24},{32,28},{36,32}... | collective-permute-start | bytes 1179656 | tf_op jit(solution)/shard_map/ppermute | solution.py:565
  102.6 31.0 %collective-permute-start = (bf16[256,768]{1,0:T(8,128)(2,1)S(1)}, bf16[256,768]{1,0:T(8,128)(2,1)S(1)}, u32[]{:S(2)}, u32[]{:S(2)}) collective-permute-start(bf16[256,768]{1,0:T(8,128)(2,1)S(1)} %get-tuple-element.54), channel_id=1, source_target_pairs={{0,64},{4,68},{8,72},{12,76},{16,80},{20,84},{24,88},{28,92},{32,9... | collective-permute-start | bytes 1179656 | tf_op jit(solution)/shard_map/cond/branch_1_fun/ppermute | solution.py:559
